TPU v7x, 32 devices: a whole 2x2x4 slice. The times are simulated.
32 devices in a mesh: seq: 4 (over x, core), exp: 8 (over z, y).
Axes of the slice: x: 2, y: 2, z: 4, core: 2. Of those that a mesh axis runs over, the one named last changes fastest.
Arguments:
- queries: bfloat16 [8, 256, 4096], P('exp', 'seq'), may hold values from -130 to 130
- new_keys: bfloat16 [8, 256, 512], P('exp', 'seq'), may hold values from -6 to 6
- new_values: bfloat16 [8, 256, 512], P('exp', 'seq'), may hold values from -6 to 6
- cache_keys: bfloat16 [8, 2048, 512], P('exp', 'seq'), may hold values from -7 to 7
- cache_values: bfloat16 [8, 2048, 512], P('exp', 'seq'), may hold values from -6 to 6
- cache_len: int32 [8], P('exp'), may hold values from 512 to 2048, as said below
- residual_in: bfloat16 [8, 256, 2048], P('exp', 'seq'), may hold values from -6 to 6
- out_weight: bfloat16 [4096, 2048], P('seq'), may hold values from -0.09375 to 0.09375
- norm_gain: float32 [2048], replicated, may hold values from 0.25 to 1.75
- router_weight: bfloat16 [2048, 32], replicated, may hold values from -0.125 to 0.125
- expert_ids: int32 [8, 256, 8], P('exp', 'seq'), may hold values from 0 to 31, all different within a row; in each aligned block of 64 rows (0 to 63, 64 to 127, ..., all dimensions but the last counted through in order) at most 24 rows name the same one
- gate_proj: bfloat16 [32, 2048, 768], P(('seq', 'exp')), may hold values from -0.125 to 0.125
- up_proj: bfloat16 [32, 2048, 768], P(('seq', 'exp')), may hold values from -0.125 to 0.125
- down_proj: bfloat16 [32, 768, 2048], P(('seq', 'exp')), may hold values from -0.21875 to 0.21875
Outputs:
- layer_out: bfloat16 [8, 256, 2048], P('exp', 'seq')
Inputs may be any that keep to these rules, and one draw needn't show every extreme that they name: `expert_ids`: among the rows of one device (aligned blocks of 64 tokens of one document) no expert is chosen more than 24 times; every token chooses 8 different experts. `cache_len`: some document fills its whole cache.
All inputs are finite; a program needn't handle non-finite values.
Results may differ from a plain program's by a relative error of at most 0.0042.
Values may be sent and summed in bfloat16 or wider, within the bound.
No kernel may reach another device: no remote copies, remote signals or barrier semaphores. Data moves between devices by JAX's collectives and lax.ppermute only.
A program may use at most 128 MiB of HBM per device.

v0:
```python
import jax
import jax.numpy as jnp
from jax import lax
from jax.sharding import PartitionSpec as P

QH = 32
KVH = 4
HD = 128
TOPK = 8


def spread_heads(kv_rows, nseq):
    count = kv_rows.shape[0]
    slots = max(KVH, nseq)
    repeat = slots // KVH
    per_dev = slots // nseq
    heads = kv_rows.reshape(count, KVH, 1, HD)
    heads = jnp.broadcast_to(heads, (count, KVH, repeat, HD))
    return heads.reshape(count, nseq, per_dev * HD)


def expert_token_rows(piece, gate_proj, up_proj, down_proj):
    width = piece.shape[-1]
    rows = piece.reshape(-1, width)
    gate = jnp.dot(rows, gate_proj[0], preferred_element_type=jnp.float32)
    upv = jnp.dot(rows, up_proj[0], preferred_element_type=jnp.float32)
    act = (jax.nn.silu(gate) * upv).astype(jnp.bfloat16)
    result = jnp.dot(act, down_proj[0], preferred_element_type=jnp.float32).astype(jnp.bfloat16)
    return result.reshape(piece.shape)


def attention_per_head(queries, new_keys, new_values, cache_keys, cache_values, length, nseq):
    tokens = queries.shape[1]
    local_q = QH // nseq
    per_dev = max(KVH, nseq) // nseq
    group = local_q // per_dev
    q_split = queries[0].reshape(tokens, nseq, local_q * HD)
    q_all, k_new, v_new, k_old, v_old = (
        lax.all_to_all(q_split, "seq", split_axis=1, concat_axis=0, tiled=True),
        lax.all_to_all(
            spread_heads(new_keys[0], nseq), "seq", split_axis=1, concat_axis=0, tiled=True
        ),
        lax.all_to_all(
            spread_heads(new_values[0], nseq), "seq", split_axis=1, concat_axis=0, tiled=True
        ),
        lax.all_to_all(
            spread_heads(cache_keys[0], nseq), "seq", split_axis=1, concat_axis=0, tiled=True
        ),
        lax.all_to_all(
            spread_heads(cache_values[0], nseq), "seq", split_axis=1, concat_axis=0, tiled=True
        ),
    )
    qtok = q_all.shape[0]
    ncache = k_old.shape[0]
    total = ncache + qtok
    qheads = q_all.reshape(qtok, per_dev, group, HD)
    keys = jnp.concatenate([k_old, k_new], 0)
    value_entries = jnp.concatenate([v_old, v_new], 0)
    block = min(512, qtok)
    scale = 1.0 / jnp.sqrt(jnp.float32(HD))
    kpos = jnp.arange(total, dtype=jnp.int32)[None, :]

    def attend(start):
        scores = (
            jnp.einsum("bpgd,kpd->pgbk", qheads, keys, preferred_element_type=jnp.float32) * scale
        )
        qpos = start + jnp.arange(block, dtype=jnp.int32)[:, None]
        visible = jnp.where(kpos < ncache, kpos < length, kpos - ncache <= qpos)
        scores = jnp.where(visible[None, None], scores, jnp.float32(-1e30))
        peak = jnp.max(scores, axis=-1, keepdims=True)
        expo = jnp.exp(scores - peak)
        weight_matrices = (expo / jnp.sum(expo, axis=-1, keepdims=True)).astype(jnp.bfloat16)
        outs = jnp.einsum(
            "pgbk,kpd->bpgd", weight_matrices, value_entries, preferred_element_type=jnp.float32
        )
        return outs.astype(jnp.bfloat16).reshape(block, local_q * HD)

    starts = jnp.arange(qtok // block, dtype=jnp.int32) * block
    return lax.map(attend, starts).reshape(qtok, local_q * HD)


def body(
    queries,
    new_keys,
    new_values,
    cache_keys,
    cache_values,
    cache_len,
    residual_in,
    out_weight,
    norm_gain,
    router_weight,
    expert_ids,
    gate_proj,
    up_proj,
    down_proj,
):
    nseq = lax.axis_size("seq")
    tokens = queries.shape[1]
    width = residual_in.shape[2]
    length = cache_len[0]
    attn = attention_per_head(queries, new_keys, new_values, cache_keys, cache_values, length, nseq)
    projected = lax.psum_scatter(
        jnp.dot(attn, out_weight, preferred_element_type=jnp.float32),
        "seq",
        scatter_dimension=0,
        tiled=True,
    )
    mixed = residual_in[0].astype(jnp.float32) + projected
    meansq = jnp.mean(mixed * mixed, axis=-1, keepdims=True)
    normed = (mixed / jnp.sqrt(meansq + 1e-06) * norm_gain).astype(jnp.bfloat16)
    logits = jnp.dot(normed, router_weight, preferred_element_type=jnp.float32)
    nexp = router_weight.shape[1]
    chosen = expert_ids[0]
    onehot = chosen[:, :, None] == jnp.arange(nexp, dtype=jnp.int32)[None, None, :]
    picked = jnp.sum(jnp.where(onehot, logits[:, None, :], jnp.float32(0.0)), axis=2)
    expo = jnp.exp(picked)
    gates = expo / jnp.sum(expo, axis=1, keepdims=True)
    capacity = 3 * tokens * TOPK // (2 * nexp)
    flat = chosen.reshape(-1)
    member = (flat[:, None] == jnp.arange(nexp, dtype=jnp.int32)[None, :]).astype(jnp.int32)
    rank = jnp.sum((jnp.cumsum(member, axis=0) - 1) * member, axis=1)
    slot = flat * capacity + rank
    place = slot[:, None] == jnp.arange(nexp * capacity, dtype=jnp.int32)[None, :]
    route = jnp.any(place.reshape(tokens, TOPK, nexp * capacity), axis=1).astype(jnp.bfloat16)
    packed = jnp.einsum("ts,td->sd", route, normed, preferred_element_type=jnp.float32).astype(
        jnp.bfloat16
    )
    outgoing = packed.reshape(nexp, capacity, width)
    result = expert_token_rows(
        lax.all_to_all(outgoing, ("seq", "exp"), split_axis=0, concat_axis=0, tiled=True),
        gate_proj,
        up_proj,
        down_proj,
    )
    back = lax.all_to_all(result, ("seq", "exp"), split_axis=0, concat_axis=0, tiled=True)
    back = back.reshape(nexp * capacity, width)
    gathered = back[slot].reshape(tokens, TOPK, width)
    moe = jnp.sum(gates[:, :, None] * gathered.astype(jnp.float32), axis=1)
    return (mixed + moe).astype(jnp.bfloat16).reshape(1, tokens, width)


def solution(mesh):
    in_specs = (
        P("exp", "seq", None),
        P("exp", "seq", None),
        P("exp", "seq", None),
        P("exp", "seq", None),
        P("exp", "seq", None),
        P("exp"),
        P("exp", "seq", None),
        P("seq", None),
        P(),
        P(),
        P("exp", "seq", None),
        P(("seq", "exp"), None, None),
        P(("seq", "exp"), None, None),
        P(("seq", "exp"), None, None),
    )
    out_specs = P("exp", "seq", None)
    return jax.shard_map(body, mesh=mesh, in_specs=in_specs, out_specs=out_specs, check_vma=False)
```

profile of v0, /device:TPU:0, one launch (start us, length us, event | category | flops | bytes accessed | tf_op | source)
XLA Modules:
  0.0 322.3 jit_solution(15527099677942321906)
XLA Ops:
  8.2 4.2 %all-to-all-start.3 = ((bf16[64,4,128]{2,0,1:T(8,128)(2,1)}), bf16[64,4,128]{2,0,1:T(8,128)(2,1)S(1)}, u32[]{:S(2)}, u32[]{:S(2)}) async-start(bf16[64,4,128]{2,0,1:T(8,128)(2,1)} %copy.70), calls=%async_computation.3 | async-start | bytes 131072 | tf_op jit(solution)/shard_map/all_to_all | solution.py:40
  13.9 2.6 all-to-all-done.3
  16.5 3.3 %all-to-all-start.1 = ((bf16[64,4,128]{2,0,1:T(8,128)(2,1)}), bf16[64,4,128]{2,0,1:T(8,128)(2,1)S(1)}, u32[]{:S(2)}, u32[]{:S(2)}) async-start(bf16[64,4,128]{2,0,1:T(8,128)(2,1)} %copy.67), calls=%async_computation.1 | async-start | bytes 131072 | tf_op jit(solution)/shard_map/all_to_all | solution.py:43
  19.8 2.2 reshape_squeeze.4
  24.0 4.1 %all-to-all-start.4 = ((bf16[64,4,1024]{2,0,1:T(8,128)(2,1)}), bf16[64,4,1024]{2,0,1:T(8,128)(2,1)}, u32[]{:S(2)}, u32[]{:S(2)}) async-start(bf16[64,4,1024]{2,0,1:T(8,128)(2,1)} %copy.71), calls=%async_computation.4 | async-start | bytes 1048576 | tf_op jit(solution)/shard_map/all_to_all | solution.py:39
  30.2 6.8 %all-to-all-done.4 = bf16[64,4,1024]{2,0,1:T(8,128)(2,1)} async-done(((bf16[64,4,1024]{2,0,1:T(8,128)(2,1)}), bf16[64,4,1024]{2,0,1:T(8,128)(2,1)}, u32[]{:S(2)}, u32[]{:S(2)}) %all-to-all-start.4) | async-done | bytes 524320 | tf_op jit(solution)/shard_map/all_to_all | solution.py:39
  37.1 4.1 %all-to-all-start = ((bf16[512,4,128]{0,2,1:T(8,128)(2,1)}), bf16[512,4,128]{0,2,1:T(8,128)(2,1)}, u32[]{:S(2)}, u32[]{:S(2)}) async-start(bf16[512,4,128]{0,2,1:T(8,128)(2,1)} %bitcast.131), calls=%async_computation | async-start | bytes 1048576 | tf_op jit(solution)/shard_map/all_to_all | solution.py:49
  45.8 4.4 %all-to-all-done = bf16[512,4,128]{0,2,1:T(8,128)(2,1)} async-done(((bf16[512,4,128]{0,2,1:T(8,128)(2,1)}), bf16[512,4,128]{0,2,1:T(8,128)(2,1)}, u32[]{:S(2)}, u32[]{:S(2)}) %all-to-all-start) | async-done | bytes 524320 | tf_op jit(solution)/shard_map/all_to_all | solution.py:49
  50.1 4.1 %all-to-all-start.2 = ((bf16[512,4,128]{2,0,1:T(8,128)(2,1)}), bf16[512,4,128]{2,0,1:T(8,128)(2,1)}, u32[]{:S(2)}, u32[]{:S(2)}) async-start(bf16[512,4,128]{2,0,1:T(8,128)(2,1)} %copy.69), calls=%async_computation.2 | async-start | bytes 1048576 | tf_op jit(solution)/shard_map/all_to_all | solution.py:46
  54.3 2.7 fusion.10
  61.0 2.2 all-to-all-done.2
  63.2 10.8 %fusion.1 = (f32[8,256]{1,0:T(8,128)S(1)}, f32[2304,256,8]{1,0,2:T(8,128)}) fusion(pred[256,2304]{0,1:T(8,128)(4,1)} %fusion.10, bf16[256,8,128]{2,1,0:T(8,128)(2,1)} %bitcast.133, bf16[256,1,128]{2,0,1:T(8,128)(2,1)S(1)} %bitcast.135, bf16[2048,1,128]{2,0,1:T(8,128)(2,1)} %bitcast.12), kind=kOutput, calls=%fused_computation.5 | convolution fusion | flops 1223292928 | bytes 20586496 | tf_op jit(solution)/shard_map/while/body/eval_jaxpr/bpgd,kpd->pgbk/dot_general | solution.py:65
  73.9 10.2 %fusion = f32[8,256]{1,0:T(8,128)S(1)} fusion(f32[2304,256,8]{1,0,2:T(8,128)} %get-tuple-element.18, f32[8,256]{1,0:T(8,128)S(1)} %get-tuple-element.17, pred[256,2304]{0,1:T(8,128)(4,1)} %fusion.10), kind=kLoop, calls=%fused_computation.4 | loop fusion | flops 18872320 | bytes 19480576 | tf_op jit(solution)/shard_map/while/body/eval_jaxpr/reduce_sum | solution.py:72
  84.2 9.4 %fusion.14 = bf16[128,8,256]{2,0,1:T(8,128)(2,1)S(1)} fusion(f32[8,256]{1,0:T(8,128)S(1)} %fusion, f32[8,256]{1,0:T(8,128)S(1)} %get-tuple-element.17, f32[2304,256,8]{1,0,2:T(8,128)} %get-tuple-element.18, pred[256,2304]{0,1:T(8,128)(4,1)} %fusion.10, bf16[256,1,128]{0,2,1:T(8,128)(2,1)S(1)} %copy.68, bf16[2048,1,128]{0,2,1:T(8,128)(2,1)} %bitcast.132), kind=kOutput, calls=%fused_computation.22 | convolution fusion | flops 1232994304 | bytes 20594688 | tf_op jit(solution)/shard_map/while/body/eval_jaxpr/pgbk,kpd->bpgd/dot_general | solution.py:73
  93.7 2.6 fusion.35
  97.2 2.4 reduce-window.6
  100.7 28.0 %reduce-scatter.2.cloned.1.call-done = f32[64,2048]{1,0:T(8,128)} async-done(((f32[256,2048]{1,0:T(8,128)}), f32[64,2048]{1,0:T(8,128)}) %reduce-scatter.2.cloned.1.call-update) | async-done | bytes 524304 | tf_op jit(solution)/shard_map/reduce_scatter | solution.py:103
  132.2 76.9 %all_to_all.97 = bf16[32,24,2048]{2,1,0:T(8,128)(2,1)S(1)} all-to-all(bf16[32,24,2048]{2,1,0:T(8,128)(2,1)S(1)} %bitcast.127), channel_id=1, replica_groups=mesh['seq'=4,'exp'=8] {'seq','exp'}, dimensions={0} | all-to-all | bytes 6291456 | tf_op jit(solution)/shard_map/all_to_all | solution.py:131
  210.8 4.0 %fusion.6 = f32[768,768]{1,0:T(8,128)} fusion(bf16[768,2048]{1,0:T(8,128)(2,1)S(1)} %bitcast.129, bf16[1,2048,768]{2,1,0:T(8,128)(2,1)S(1)} %copy-done.8), kind=kOutput, calls=%fused_computation.13 | convolution fusion | flops 2415919104 | bytes 8650752 | tf_op jit(solution)/shard_map/dot_general | solution.py:26
  214.9 11.0 %convolution_convert_fusion = bf16[768,2048]{1,0:T(8,128)(2,1)} fusion(bf16[1,768,2048]{2,1,0:T(8,128)(2,1)S(1)} %copy-done, f32[768,768]{1,0:T(8,128)} %fusion.6, bf16[768,2048]{1,0:T(8,128)(2,1)} %bitcast.130, bf16[1,2048,768]{2,1,0:T(8,128)(2,1)} %param.25), kind=kOutput, calls=%fused_computation.10 | convolution fusion | flops 4836950016 | bytes 14942208 | tf_op jit(solution)/shard_map/dot_general | solution.py:28
  225.9 3.9 %all-to-all-start.6 = ((bf16[32,24,2048]{2,1,0:T(8,128)(2,1)}), bf16[32,24,2048]{2,1,0:T(8,128)(2,1)}, u32[]{:S(2)}, u32[]{:S(2)}) async-start(bf16[32,24,2048]{2,1,0:T(8,128)(2,1)} %bitcast.128), calls=%async_computation.7 | async-start | bytes 6291456 | tf_op jit(solution)/shard_map/all_to_all | solution.py:136
  232.6 70.0 %all-to-all-done.6 = bf16[32,24,2048]{2,1,0:T(8,128)(2,1)} async-done(((bf16[32,24,2048]{2,1,0:T(8,128)(2,1)}), bf16[32,24,2048]{2,1,0:T(8,128)(2,1)}, u32[]{:S(2)}, u32[]{:S(2)}) %all-to-all-start.6) | async-done | bytes 3145760 | tf_op jit(solution)/shard_map/all_to_all | solution.py:136
  302.6 7.6 %gather_fusion = bf16[512,2048]{1,0:T(8,128)(2,1)} fusion(bf16[768,2048]{1,0:T(8,128)(2,1)} %bitcast.35, s32[1024]{0:T(1024)S(1)} %pad_clamp_fusion), kind=kCustom, calls=%fused_computation | custom fusion | bytes 4196352 | tf_op jit(solution)/shard_map/gather | solution.py:138
  310.2 3.4 %fusion.4 = f32[64,2048]{1,0:T(8,128)S(1)} fusion(bf16[512,2048]{1,0:T(8,128)(2,1)} %gather_fusion, f32[64,8]{1,0:T(8,128)S(1)} %copy.76), kind=kLoop, calls=%fused_computation.9 | loop fusion | flops 3014656 | bytes 2623488 | tf_op jit(solution)/shard_map/reduce_sum | solution.py:139
  (60 shorter events, 26.9 us)
Async XLA Ops:
  6.5 208.3 %copy-start = (bf16[1,768,2048]{2,1,0:T(8,128)(2,1)S(1)}, bf16[1,768,2048]{2,1,0:T(8,128)(2,1)}, u32[]{:S(2)}) copy-start(bf16[1,768,2048]{2,1,0:T(8,128)(2,1)} %param.27) | copy-start | bytes 9437188
  8.2 8.3 %all-to-all-start.3 = ((bf16[64,4,128]{2,0,1:T(8,128)(2,1)}), bf16[64,4,128]{2,0,1:T(8,128)(2,1)S(1)}, u32[]{:S(2)}, u32[]{:S(2)}) async-start(bf16[64,4,128]{2,0,1:T(8,128)(2,1)} %copy.70), calls=%async_computation.3 | async-start | bytes 131072 | tf_op jit(solution)/shard_map/all_to_all | solution.py:40
  16.5 7.5 %all-to-all-start.1 = ((bf16[64,4,128]{2,0,1:T(8,128)(2,1)}), bf16[64,4,128]{2,0,1:T(8,128)(2,1)S(1)}, u32[]{:S(2)}, u32[]{:S(2)}) async-start(bf16[64,4,128]{2,0,1:T(8,128)(2,1)} %copy.67), calls=%async_computation.1 | async-start | bytes 131072 | tf_op jit(solution)/shard_map/all_to_all | solution.py:43
  24.0 13.0 %all-to-all-start.4 = ((bf16[64,4,1024]{2,0,1:T(8,128)(2,1)}), bf16[64,4,1024]{2,0,1:T(8,128)(2,1)}, u32[]{:S(2)}, u32[]{:S(2)}) async-start(bf16[64,4,1024]{2,0,1:T(8,128)(2,1)} %copy.71), calls=%async_computation.4 | async-start | bytes 1048576 | tf_op jit(solution)/shard_map/all_to_all | solution.py:39
  37.1 13.1 %all-to-all-start = ((bf16[512,4,128]{0,2,1:T(8,128)(2,1)}), bf16[512,4,128]{0,2,1:T(8,128)(2,1)}, u32[]{:S(2)}, u32[]{:S(2)}) async-start(bf16[512,4,128]{0,2,1:T(8,128)(2,1)} %bitcast.131), calls=%async_computation | async-start | bytes 1048576 | tf_op jit(solution)/shard_map/all_to_all | solution.py:49
  50.1 13.0 %all-to-all-start.2 = ((bf16[512,4,128]{2,0,1:T(8,128)(2,1)}), bf16[512,4,128]{2,0,1:T(8,128)(2,1)}, u32[]{:S(2)}, u32[]{:S(2)}) async-start(bf16[512,4,128]{2,0,1:T(8,128)(2,1)} %copy.69), calls=%async_computation.2 | async-start | bytes 1048576 | tf_op jit(solution)/shard_map/all_to_all | solution.py:46
  54.3 74.4 %reduce-scatter.2.cloned.1.call-start = ((), (), s32[]{:S(2)}) async-start(), calls=%async_computation.8 | async-start | bytes 2621440 | tf_op jit(solution)/shard_map/reduce_scatter | solution.py:103
  84.2 9.4 %copy-start.7 = (bf16[1024,2048]{1,0:T(8,128)(2,1)S(1)}, bf16[1024,2048]{1,0:T(8,128)(2,1)}, u32[]{:S(2)}) copy-start(bf16[1024,2048]{1,0:T(8,128)(2,1)} %param.21) | copy-start | bytes 12582916
  93.6 2.7 copy-start.5
  93.6 35.1 %copy-start.2 = (bf16[1,64,2048]{2,1,0:T(8,128)(2,1)S(1)}, bf16[1,64,2048]{2,1,0:T(8,128)(2,1)}, u32[]{:S(2)}) copy-start(bf16[1,64,2048]{2,1,0:T(8,128)(2,1)} %param.20) | copy-start | bytes 786436
  96.3 33.7 %copy-start.6 = (f32[2048]{0:T(1024)S(1)}, f32[2048]{0:T(1024)}, u32[]{:S(2)}) copy-start(f32[2048]{0:T(1024)} %param.22) | copy-start | bytes 24580
  131.1 1.1 copy-start.3
  132.2 78.6 %copy-start.8 = (bf16[1,2048,768]{2,1,0:T(8,128)(2,1)S(1)}, bf16[1,2048,768]{2,1,0:T(8,128)(2,1)}, u32[]{:S(2)}) copy-start(bf16[1,2048,768]{2,1,0:T(8,128)(2,1)} %param.26) | copy-start | bytes 9437188
  209.1 1.7 copy-start.1
  225.9 5.5 %copy-start.4 = (bf16[2048,32]{0,1:T(8,128)(2,1)S(1)}, bf16[2048,32]{0,1:T(8,128)(2,1)}, u32[]{:S(2)}) copy-start(bf16[2048,32]{0,1:T(8,128)(2,1)} %param.23) | copy-start | bytes 393220
  225.9 76.7 %all-to-all-start.6 = ((bf16[32,24,2048]{2,1,0:T(8,128)(2,1)}), bf16[32,24,2048]{2,1,0:T(8,128)(2,1)}, u32[]{:S(2)}, u32[]{:S(2)}) async-start(bf16[32,24,2048]{2,1,0:T(8,128)(2,1)} %bitcast.128), calls=%async_computation.7 | async-start | bytes 6291456 | tf_op jit(solution)/shard_map/all_to_all | solution.py:136
Sparse Core Ops, SparseCore 0:
  96.4 32.2 reduce-scatter.1
where the time goes:
time: 324 us; the launch traced here: 322 us
  waiting for transfers between devices  114 us (35%)
  blocking collectives  76.9 us (24%)
  matrix products  40 us (12%)
  local copies, waits for them, and re-layouts  28.8 us (9%)
  other arithmetic  24.5 us (8%)
  starting transfers between devices  23.8 us (7%)
  between operations  14.3 us (4%)
    all_to_all x1, blocking collectives, body(): lax.all_to_all(outgoing, ('seq', 'exp'), split_axis=0, concat_axis=0, til...  76.9 us
    all_to_all x1, waiting for transfers between devices, body(): lax.all_to_all(result, ('seq', 'exp'), split_axis=0, concat_axis=0, tiled...  70 us
    reduce_scatter x1, waiting for transfers between devices, body(): lax.psum_scatter(jnp.dot(attn, out_weight, preferred_element_type=jnp.flo...  28 us
    dot_general x1, matrix products, expert_token_rows(): jnp.dot(act, down_proj[0], preferred_element_type=jnp.float32)  11 us
    dot_general x1, matrix products, attend(): jnp.einsum('bpgd,kpd->pgbk', qheads, keys, preferred_element_type=jnp.flo...  10.8 us
    reduce_sum x1, other arithmetic, attend(): jnp.sum(expo, axis=-1, keepdims=True)  10.2 us
    dot_general x1, matrix products, attend(): jnp.einsum('pgbk,kpd->bpgd', weight_matrices, value_entries, preferred_el...  9.41 us
    gather x1, local copies, waits for them, and re-layouts, body(): gathered = back[slot].reshape(tokens, TOPK, width)  7.58 us
  transfers between devices with their start and end apart: 7, of which 6 were waited for; matrix products, arithmetic and copies ran while one was open for 8% of the time, Pallas kernels for 0%

commit v1 on v0

v1 whole, which is shorter than its diff:
```python
import functools
import math

import jax
import jax.numpy as jnp
from jax import lax
from jax.experimental import pallas as pl
from jax.experimental.pallas import tpu as pltpu
from jax.sharding import PartitionSpec as P

QH = 32
KVH = 4
HD = 128
TOPK = 8
MASKED = -1e30
EXP2_SCALE = math.log2(math.e) / math.sqrt(HD)
NT = (((1,), (1,)), ((), ()))
TN = (((0,), (0,)), ((), ()))
VMEM = pl.BlockSpec(memory_space=pltpu.VMEM)
SMEM = pl.BlockSpec(memory_space=pltpu.SMEM)
f32 = jnp.float32
bf16 = jnp.bfloat16


def swap(rows, axis, bits):
    return lax.ppermute(rows, axis, [(i, i ^ bits) for i in range(lax.axis_size(axis))])


def params(mib):
    return pltpu.CompilerParams(vmem_limit_bytes=mib << 20)


def pack_kernel(nseq, me_ref, q_ref, nk_ref, nv_ref, ck_ref, cv_ref, *outs):
    qcols = QH // nseq * HD
    for k in range(nseq):
        dest = me_ref[0] ^ k
        qat = pl.ds(pl.multiple_of(dest * qcols, HD), qcols)
        kvat = pl.ds(pl.multiple_of(dest * KVH // nseq * HD, HD), HD)
        head, cache = outs[k], outs[nseq + k]
        head[:, :qcols] = q_ref[:, qat]
        head[:, qcols : qcols + HD] = nk_ref[:, kvat]
        head[:, qcols + HD :] = nv_ref[:, kvat]
        cache[:, :HD] = ck_ref[:, kvat]
        cache[:, HD:] = cv_ref[:, kvat]


def pack(me, queries, new_keys, new_values, cache_keys, cache_values, nseq):
    tokens, slots = queries.shape[0], cache_keys.shape[0]
    qcols = QH // nseq * HD
    shapes = [jax.ShapeDtypeStruct((tokens, qcols + 2 * HD), bf16)] * nseq
    shapes += [jax.ShapeDtypeStruct((slots, 2 * HD), bf16)] * nseq
    outs = pl.pallas_call(
        functools.partial(pack_kernel, nseq),
        out_shape=shapes,
        in_specs=[SMEM] + [VMEM] * 5,
        out_specs=[VMEM] * (2 * nseq),
        compiler_params=params(24),
        name="pack_heads",
    )(me, queries, new_keys, new_values, cache_keys, cache_values)
    return outs[:nseq], outs[nseq:]


def head_rows(heads, start):
    return jnp.concatenate([ref[:, start : start + HD] for ref in heads], 0)


def slot_bias(me, length, ks, slots):
    parts = []
    for k in ks:
        pos = (me ^ k) * slots + lax.broadcasted_iota(jnp.int32, (1, slots), 1)
        parts.append(jnp.where(pos < length, f32(0.0), f32(MASKED)))
    return jnp.concatenate(parts, 1)


def near_kernel(nseq, me_ref, len_ref, *refs):
    heads, caches = refs[:nseq], refs[nseq : nseq + 2]
    peak_ref, sum_ref, acc_ref = refs[nseq + 2 :]
    group = QH // nseq
    slots = caches[0].shape[0]
    bias = slot_bias(me_ref[0], len_ref[0], (0, 1), slots)
    keys = jnp.concatenate([ref[:, :HD] for ref in caches], 0)
    vals = jnp.concatenate([ref[:, HD:] for ref in caches], 0)
    for g in range(group):
        q = head_rows(heads, g * HD)
        s = lax.dot_general(q, keys, NT, preferred_element_type=f32) + bias
        peak = jnp.max(s, axis=1, keepdims=True)
        p = jnp.exp2((s - peak) * f32(EXP2_SCALE))
        peak_ref[:, g : g + 1] = peak
        sum_ref[:, g : g + 1] = jnp.sum(p, axis=1, keepdims=True)
        acc_ref[:, g * HD : (g + 1) * HD] = jnp.dot(
            p.astype(bf16), vals, preferred_element_type=f32
        )


def far_kernel(nseq, me_ref, len_ref, *refs):
    heads, caches = refs[:nseq], refs[nseq : 2 * nseq - 2]
    peak_ref, sum_ref, acc_ref, w_ref, keep_ref, send_ref, attn_ref = refs[2 * nseq - 2 :]
    group = QH // nseq
    qcols = group * HD
    me = me_ref[0]
    slots, tokens = caches[0].shape[0], heads[0].shape[0]
    qtok = nseq * tokens
    bias = slot_bias(me, len_ref[0], range(2, nseq), slots)
    keys = jnp.concatenate([ref[:, :HD] for ref in caches], 0)
    vals = jnp.concatenate([ref[:, HD:] for ref in caches], 0)
    new_keys, new_vals = head_rows(heads, qcols), head_rows(heads, qcols + HD)
    row = lax.broadcasted_iota(jnp.int32, (qtok, qtok), 0)
    col = lax.broadcasted_iota(jnp.int32, (qtok, qtok), 1)
    qpos = (me ^ (row // tokens)) * tokens + row % tokens
    kpos = (me ^ (col // tokens)) * tokens + col % tokens
    new_bias = jnp.where(kpos <= qpos, f32(0.0), f32(MASKED))
    for g in range(group):
        at = slice(g * HD, (g + 1) * HD)
        q = head_rows(heads, g * HD)
        s = lax.dot_general(q, keys, NT, preferred_element_type=f32) + bias
        t = lax.dot_general(q, new_keys, NT, preferred_element_type=f32) + new_bias
        old = peak_ref[:, g : g + 1]
        peak = jnp.maximum(jnp.max(s, axis=1, keepdims=True), jnp.max(t, axis=1, keepdims=True))
        peak = jnp.maximum(peak, old)
        fade = jnp.exp2((old - peak) * f32(EXP2_SCALE))
        p = jnp.exp2((s - peak) * f32(EXP2_SCALE))
        r = jnp.exp2((t - peak) * f32(EXP2_SCALE))
        total = sum_ref[:, g : g + 1] * fade
        total += jnp.sum(p, axis=1, keepdims=True) + jnp.sum(r, axis=1, keepdims=True)
        acc = acc_ref[:, at] * fade
        acc += jnp.dot(p.astype(bf16), vals, preferred_element_type=f32)
        acc += jnp.dot(r.astype(bf16), new_vals, preferred_element_type=f32)
        attn_ref[:, at] = (acc / total).astype(bf16)
    for k in range(nseq):
        rows = attn_ref[k * tokens : (k + 1) * tokens, :]
        out = keep_ref if k % 2 == 0 else send_ref
        out[k // 2 * tokens : (k // 2 + 1) * tokens, :] = jnp.dot(
            rows, w_ref[...], preferred_element_type=f32
        )


def project_attention(me, length, queries, new_keys, new_values, cache_keys, cache_values, out_weight):
    nseq = lax.axis_size("seq")
    tokens, slots = queries.shape[0], cache_keys.shape[0]
    width = out_weight.shape[1]
    group = QH // nseq
    qtok = nseq * tokens
    heads, caches = pack(me, queries, new_keys, new_values, cache_keys, cache_values, nseq)
    order = sorted(range(1, nseq), reverse=True)
    heads = {0: heads[0]} | {k: swap(heads[k], "seq", k) for k in order}
    caches = {0: caches[0]} | {k: swap(caches[k], "seq", k) for k in order}
    heads = [heads[k] for k in range(nseq)]
    caches = [caches[k] for k in range(nseq)]
    state = pl.pallas_call(
        functools.partial(near_kernel, nseq),
        out_shape=[
            jax.ShapeDtypeStruct((qtok, HD), f32),
            jax.ShapeDtypeStruct((qtok, HD), f32),
            jax.ShapeDtypeStruct((qtok, group * HD), f32),
        ],
        in_specs=[SMEM] * 2 + [VMEM] * (nseq + 2),
        out_specs=[VMEM] * 3,
        compiler_params=params(32),
        name="attend_near",
    )(me, length, *heads, *caches[:2])
    half = nseq // 2 * tokens
    keep, send = pl.pallas_call(
        functools.partial(far_kernel, nseq),
        out_shape=[jax.ShapeDtypeStruct((half, width), f32)] * 2,
        in_specs=[SMEM] * 2 + [VMEM] * (2 * nseq + 2),
        out_specs=[VMEM] * 2,
        scratch_shapes=[pltpu.VMEM((qtok, group * HD), bf16)],
        compiler_params=params(48),
        name="attend_far",
    )(me, length, *heads, *caches[2:], *state, out_weight)
    got = swap(send, "seq", 1)
    others = []
    for k in range(2, nseq, 2):
        at = slice(k // 2 * tokens, (k // 2 + 1) * tokens)
        others.append(swap((keep[at] + got[at]).astype(bf16), "seq", k))
    return keep, got, others


def norm_kernel(others, res_ref, keep_ref, got_ref, *refs):
    gain_ref, router_ref, ids_ref, mixed_ref, rows_ref = refs[others:]
    tokens, width = res_ref.shape
    mixed = res_ref[...].astype(f32) + keep_ref[:tokens, :] + got_ref[:tokens, :]
    for ref in refs[:others]:
        mixed += ref[...].astype(f32)
    mixed_ref[...] = mixed
    meansq = jnp.mean(mixed * mixed, axis=1, keepdims=True)
    normed = (mixed / jnp.sqrt(meansq + 1e-06) * gain_ref[...]).astype(bf16)
    rows_ref[:, :width] = normed
    logits = jnp.dot(normed, router_ref[...], preferred_element_type=f32)
    nexp = logits.shape[1]
    expert = lax.broadcasted_iota(jnp.int32, (tokens, nexp), 1)
    chosen = expert == ids_ref[:, 0:1]
    for k in range(1, ids_ref.shape[1]):
        chosen = jnp.logical_or(chosen, expert == ids_ref[:, k : k + 1])
    expo = jnp.where(chosen, jnp.exp(logits), f32(0.0))
    gates = expo / jnp.sum(expo, axis=1, keepdims=True)
    high = gates.astype(bf16)
    low = (gates - high.astype(f32)).astype(bf16)
    extra = rows_ref.shape[1] - width
    row = lax.broadcasted_iota(jnp.int32, (nexp, extra), 0)
    col = lax.broadcasted_iota(jnp.int32, (nexp, extra), 1)
    spread = jnp.dot(high, (col == row).astype(bf16), preferred_element_type=f32)
    spread += jnp.dot(low, (col == row + nexp).astype(bf16), preferred_element_type=f32)
    rows_ref[:, width:] = spread.astype(bf16)


def norm_rows(residual, keep, got, others, gain, router, ids):
    tokens, width = residual.shape
    extra = -(-2 * router.shape[1] // 128) * 128
    return pl.pallas_call(
        functools.partial(norm_kernel, len(others)),
        out_shape=[
            jax.ShapeDtypeStruct((tokens, width), f32),
            jax.ShapeDtypeStruct((tokens, width + extra), bf16),
        ],
        in_specs=[VMEM] * (6 + len(others)),
        out_specs=[VMEM] * 2,
        compiler_params=params(24),
        name="norm_and_route",
    )(residual, keep, got, *others, gain.reshape(1, width), router, ids)


def gather_rows(rows, planes, sides):
    half = rows.shape[0] // 2
    columns = [rows] + [swap(rows, "exp", 2 * kz) for kz in range(1, planes)]
    blocks = []
    for col in columns:
        right = [swap(col, "seq", 2 * kx) for kx in range(1, sides)]
        up = swap(col, "exp", 1)
        over = [
            (swap(up[:half], "seq", 2 * kx), swap(right[kx - 1][half:], "exp", 1))
            for kx in range(1, sides)
        ]
        blocks.append([[(col,)] + [(r,) for r in right], [(up,)] + over])
    return blocks


def expert_kernel(planes, sides, cap, gtiles, dtiles, pieces, places, *refs):
    mine_ref = refs[0]
    blocks = refs[1 : 1 + pieces]
    (g0, u0, d0, g1, u1, d1) = refs[1 + pieces : 7 + pieces]
    nout = planes * 4
    outs = refs[7 + pieces : 7 + pieces + nout]
    x_ref, act_ref, y_ref, hot_ref, gate_ref = refs[7 + pieces + nout :]
    e, j = pl.program_id(0), pl.program_id(1)
    width = x_ref.shape[2]
    ext = blocks[0].shape[1] - width
    tokens = places["tokens"]
    per_group = 2 * sides
    gtok = per_group * tokens
    grows = per_group * cap
    step = 256

    @pl.when(jnp.logical_and(e == 0, j == 0))
    def gather():
        ecol = lax.broadcasted_iota(jnp.int32, (8, ext), 1)
        erow = lax.broadcasted_iota(jnp.int32, (8, ext), 0)
        want = jnp.where(erow == 0, mine_ref[0], jnp.where(erow == 1, mine_ref[1], -ext))
        nexp = places["nexp"]
        pick = jnp.logical_or(ecol == want, ecol == want + nexp).astype(bf16)
        trow = lax.broadcasted_iota(jnp.int32, (gtok, gtok), 0)
        tcol = lax.broadcasted_iota(jnp.int32, (gtok, gtok), 1)
        before = jnp.logical_and(trow < tcol, trow // tokens == tcol // tokens).astype(bf16)
        block = lax.broadcasted_iota(jnp.int32, (8, gtok), 1) // tokens
        slot = lax.broadcasted_iota(jnp.int32, (grows, gtok), 0).astype(f32)
        for g in range(planes):
            mine = [blocks[i] for i in places["blocks"][g]]
            tail = jnp.concatenate([ref[:, width:] for ref in mine], 0)
            gates = lax.dot_general(pick, tail, NT, preferred_element_type=f32)
            chosen = gates > 0.0
            rank = jnp.dot(chosen.astype(bf16), before, preferred_element_type=f32)
            target = jnp.where(chosen, (block * cap).astype(f32) + rank, f32(-1.0))
            hot = jnp.concatenate(
                [(slot == target[i : i + 1, :]).astype(f32) for i in range(2)], 0
            ).astype(bf16)
            hot_ref[g] = hot
            for at in range(0, width, step):
                part = jnp.concatenate([ref[:, at : at + step] for ref in mine], 0)
                got = jnp.dot(hot, part, preferred_element_type=f32).astype(bf16)
                for i in range(2):
                    x_ref[i, g * grows : (g + 1) * grows, at : at + step] = got[
                        i * grows : (i + 1) * grows
                    ]
            got = jnp.dot(hot, tail, preferred_element_type=f32)
            for i in range(2):
                sel = pick[i : i + 1, :].astype(f32)
                gate = jnp.sum(got[i * grows : (i + 1) * grows] * sel, axis=1, keepdims=True)
                gate_ref[i, g * grows : (g + 1) * grows, :] = jnp.broadcast_to(gate, (grows, 128))

    def expert(i, gate_w, up_w, down_w):
        @pl.when(jnp.logical_and(e == i, j < gtiles))
        def _():
            x = x_ref[i]
            tile = gate_w.shape[2]
            gate = jnp.dot(x, gate_w[0], preferred_element_type=f32)
            upv = jnp.dot(x, up_w[0], preferred_element_type=f32)
            act_ref[:, pl.ds(pl.multiple_of(j * tile, 128), tile)] = (
                gate / (1.0 + jnp.exp(-gate)) * upv
            ).astype(bf16)

        @pl.when(jnp.logical_and(e == i, j >= gtiles))
        def _():
            tile = down_w.shape[2]
            y = jnp.dot(act_ref[...], down_w[0], preferred_element_type=f32)
            y = y * gate_ref[i][:, 0:1]
            y_ref[i, :, pl.ds(pl.multiple_of((j - gtiles) * tile, 128), tile)] = y.astype(bf16)

    expert(0, g0, u0, d0)
    expert(1, g1, u1, d1)

    @pl.when(jnp.logical_and(e == 1, j == gtiles + dtiles - 1))
    def scatter():
        half = tokens // 2
        for g in range(planes):
            hot = hot_ref[g]
            keep_a, keep_b, send_a, send_b = outs[4 * g : 4 * g + 4]
            for at in range(0, width, step):
                y = jnp.concatenate(
                    [y_ref[i, g * grows : (g + 1) * grows, at : at + step] for i in range(2)], 0
                )
                total = lax.dot_general(hot, y, TN, preferred_element_type=f32).astype(bf16)
                cols = slice(at, at + step)
                for ky in range(2):
                    for kx in range(sides):
                        row = (ky * sides + kx) * tokens
                        low, high = total[row : row + half], total[row + half : row + tokens]
                        if kx == 0:
                            keep_a[ky * half : (ky + 1) * half, cols] = low
                        else:
                            a = ((kx - 1) * 2 + ky) * half
                            send_a[a : a + half, cols] = low
                        b = keep_b if ky == 0 else send_b
                        b[kx * half : (kx + 1) * half, cols] = high


def expert_terms(blocks, mine, weights, cap, nexp):
    planes, sides = len(blocks), len(blocks[0][0])
    tokens = blocks[0][0][0][0].shape[0]
    flat, index = [], []
    for plane in blocks:
        at = []
        for line in plane:
            for pieces in line:
                at += range(len(flat), len(flat) + len(pieces))
                flat += pieces
        index.append(at)
    gate0, up0, down0, gate1, up1, down1 = weights
    _, width, hidden = gate0.shape
    gtiles, dtiles = hidden // 256, width // 1024
    grows = 2 * sides * cap
    rows = planes * grows
    half = tokens // 2

    def first(e, j, tiles, base):
        t = jnp.clip(j - base, 0, tiles - 1)
        return jnp.where(e == 0, t, tiles - 1)

    def second(e, j, tiles, base):
        t = jnp.clip(j - base, 0, tiles - 1)
        return jnp.where(e == 1, t, 0)

    def specs(which):
        wide = pl.BlockSpec((1, width, 256), lambda e, j: (0, 0, which(e, j, gtiles, 0)))
        down = pl.BlockSpec((1, hidden, 1024), lambda e, j: (0, 0, which(e, j, dtiles, gtiles)))
        return [wide, wide, down]

    out_shape = []
    for _ in range(planes):
        out_shape += [
            jax.ShapeDtypeStruct((2 * half, width), bf16),
            jax.ShapeDtypeStruct((sides * half, width), bf16),
            jax.ShapeDtypeStruct(((sides - 1) * 2 * half, width), bf16),
            jax.ShapeDtypeStruct((sides * half, width), bf16),
        ]
    places = {"tokens": tokens, "blocks": index, "nexp": nexp}
    kernel = functools.partial(
        expert_kernel, planes, sides, cap, gtiles, dtiles, len(flat), places
    )
    outs = pl.pallas_call(
        kernel,
        grid=(2, gtiles + dtiles),
        out_shape=out_shape,
        in_specs=[SMEM] + [VMEM] * len(flat) + specs(first) + specs(second),
        out_specs=[VMEM] * len(out_shape),
        scratch_shapes=[
            pltpu.VMEM((2, rows, width), bf16),
            pltpu.VMEM((rows, hidden), bf16),
            pltpu.VMEM((2, rows, width), bf16),
            pltpu.VMEM((planes, 2 * grows, 2 * sides * tokens), bf16),
            pltpu.VMEM((2, rows, 128), f32),
        ],
        compiler_params=params(52),
        name="experts",
    )(mine, *flat, *weights)
    return [outs[4 * g : 4 * g + 4] for g in range(planes)]


def add(*terms):
    total = terms[0].astype(f32)
    for term in terms[1:]:
        total = total + term.astype(f32)
    return total


def return_terms(terms, sides):
    own = []
    for kz in reversed(range(len(terms))):
        keep_a, keep_b, send_a, send_b = terms[kz]
        half = keep_a.shape[0] // 2
        got_a = [
            swap(send_a[(kx - 1) * 2 * half : kx * 2 * half], "seq", 2 * kx)
            for kx in range(1, sides)
        ]
        got_b = swap(send_b, "exp", 1)
        next_a = swap(
            add(keep_a[half:], *[a[half:] for a in got_a]).astype(bf16), "exp", 1
        )
        next_b = [
            swap(
                add(keep_b[kx * half : (kx + 1) * half], got_b[kx * half : (kx + 1) * half]).astype(bf16),
                "seq",
                2 * kx,
            )
            for kx in range(1, sides)
        ]
        top = add(keep_a[:half], *[a[:half] for a in got_a], next_a)
        low = add(keep_b[:half], got_b[:half], *next_b)
        if kz == 0:
            own.append(jnp.concatenate([top, low], 0))
        else:
            both = jnp.concatenate([top.astype(bf16), low.astype(bf16)], 0)
            own.append(swap(both, "exp", 2 * kz).astype(f32))
    return own


def experts_by_chip(rows, width, weights, nexp):
    nseq, nplace = lax.axis_size("seq"), lax.axis_size("exp")
    cap = 3 * rows.shape[0] * TOPK // (2 * nexp)
    planes, sides = nplace // 2, nseq // 2
    me = lax.axis_index("seq") * nplace + lax.axis_index("exp")
    other = (lax.axis_index("seq") ^ 1) * nplace + lax.axis_index("exp")
    mine = jnp.stack([me, other]).astype(jnp.int32)
    blocks = gather_rows(rows, planes, sides)
    return return_terms(expert_terms(blocks, mine, weights, cap, nexp), sides)


def experts_by_device(rows, width, ids, gate_proj, up_proj, down_proj, nexp):
    tokens = rows.shape[0]
    normed = rows[:, :width]
    gates = rows[:, width : width + nexp].astype(f32) + rows[
        :, width + nexp : width + 2 * nexp
    ].astype(f32)
    gates = jnp.take_along_axis(gates, ids, axis=1)
    capacity = 3 * tokens * TOPK // (2 * nexp)
    flat = ids.reshape(-1)
    member = (flat[:, None] == jnp.arange(nexp, dtype=jnp.int32)[None, :]).astype(jnp.int32)
    rank = jnp.sum((jnp.cumsum(member, axis=0) - 1) * member, axis=1)
    slot = flat * capacity + rank
    place = slot[:, None] == jnp.arange(nexp * capacity, dtype=jnp.int32)[None, :]
    route = jnp.any(place.reshape(tokens, TOPK, nexp * capacity), axis=1).astype(bf16)
    packed = jnp.einsum("ts,td->sd", route, normed, preferred_element_type=f32).astype(bf16)
    outgoing = packed.reshape(nexp, capacity, width)
    taken = lax.all_to_all(outgoing, ("seq", "exp"), split_axis=0, concat_axis=0, tiled=True)
    taken = taken.reshape(-1, width)
    gate = jnp.dot(taken, gate_proj[0], preferred_element_type=f32)
    upv = jnp.dot(taken, up_proj[0], preferred_element_type=f32)
    act = (jax.nn.silu(gate) * upv).astype(bf16)
    result = jnp.dot(act, down_proj[0], preferred_element_type=f32).astype(bf16)
    result = result.reshape(nexp, capacity, width)
    back = lax.all_to_all(result, ("seq", "exp"), split_axis=0, concat_axis=0, tiled=True)
    gathered = back.reshape(nexp * capacity, width)[slot].reshape(tokens, TOPK, width)
    return [jnp.sum(gates[:, :, None] * gathered.astype(f32), axis=1)]


def body(
    queries,
    new_keys,
    new_values,
    cache_keys,
    cache_values,
    cache_len,
    residual_in,
    out_weight,
    norm_gain,
    router_weight,
    expert_ids,
    gate_proj,
    up_proj,
    down_proj,
):
    nseq, nplace = lax.axis_size("seq"), lax.axis_size("exp")
    tokens, width = residual_in.shape[1:]
    nexp = router_weight.shape[1]
    by_chip = nseq * nplace <= 32
    me = lax.axis_index("seq").astype(jnp.int32).reshape(1)
    keep, got, others = project_attention(
        me,
        cache_len,
        queries[0],
        new_keys[0],
        new_values[0],
        cache_keys[0],
        cache_values[0],
        out_weight,
    )
    mixed, rows = norm_rows(
        residual_in[0], keep, got, others, norm_gain, router_weight, expert_ids[0]
    )
    if by_chip:
        weights = [gate_proj, up_proj, down_proj]
        weights += [swap(w, "seq", 1) for w in weights]
        terms = experts_by_chip(rows, width, weights, nexp)
    else:
        terms = experts_by_device(
            rows, width, expert_ids[0], gate_proj, up_proj, down_proj, nexp
        )
    return add(mixed, *terms).astype(bf16).reshape(1, tokens, width)


def solution(mesh):
    in_specs = (
        P("exp", "seq", None),
        P("exp", "seq", None),
        P("exp", "seq", None),
        P("exp", "seq", None),
        P("exp", "seq", None),
        P("exp"),
        P("exp", "seq", None),
        P("seq", None),
        P(),
        P(),
        P("exp", "seq", None),
        P(("seq", "exp"), None, None),
        P(("seq", "exp"), None, None),
        P(("seq", "exp"), None, None),
    )
    out_specs = P("exp", "seq", None)
    return jax.shard_map(body, mesh=mesh, in_specs=in_specs, out_specs=out_specs, check_vma=False)
```

time: 324 us -> 205 us (0.63)
  blocking collectives: 76.9 us -> 0 us
  starting transfers between devices: 23.8 us -> 68.1 us
  matrix products: 40 us -> 0 us
  Pallas kernels: 0 us -> 38.2 us
  waiting for transfers between devices: 114 us -> 80.7 us
  local copies, waits for them, and re-layouts: 28.8 us -> 9.24 us
  other arithmetic: 24.5 us -> 7.24 us
  between operations: 14.3 us -> 1.15 us
    all_to_all x6 -> x0, waiting for transfers between devices: 86 us -> none  [the longest x1 70 us: body(): lax.all_to_all(result, ('seq', 'exp'), split_axis=0, concat_axis=0, tiled...]
    ppermute x0 -> x49, waiting for transfers between devices: none -> 80.7 us  [swap(): lax.ppermute(rows, axis, [(i, i ^ bits) for i in range(lax.axis_size(axis...]
    all_to_all x1 -> x0, blocking collectives: 76.9 us -> none  [body(): lax.all_to_all(outgoing, ('seq', 'exp'), split_axis=0, concat_axis=0, til...]
    ppermute x0 -> x49, starting transfers between devices: none -> 68.1 us  [swap(): lax.ppermute(rows, axis, [(i, i ^ bits) for i in range(lax.axis_size(axis...]
    dot_general x7 -> x0, matrix products: 40 us -> none  [the longest x1 11 us: expert_token_rows(): jnp.dot(act, down_proj[0], preferred_element_type=jnp.float32)]
    pallas_call x0 -> x5, Pallas kernels: none -> 38.2 us  [the longest x1 22 us: expert_terms(): pl.pallas_call(kernel, grid=(2, gtiles + dtiles), out_shape=out_shape, in...]
    reduce_scatter x1 -> x0, waiting for transfers between devices: 28 us -> none  [body(): lax.psum_scatter(jnp.dot(attn, out_weight, preferred_element_type=jnp.flo...]
    all_to_all x6 -> x0, starting transfers between devices: 23.8 us -> none  [the longest x1 4.21 us: attention_per_head(): lax.all_to_all(spread_heads(new_keys[0], nseq), 'seq', split_axis=1, conc...]
  transfers between devices with their start and end apart: 7 -> 49, of which waited for: 6 -> 25; matrix products, arithmetic and copies ran while one was open for 8% -> 4% of each run, Pallas kernels for 0% -> 2%
where the time goes in v1:
time: 205 us
  waiting for transfers between devices  80.7 us (39%)
  starting transfers between devices  68.1 us (33%)
  Pallas kernels  38.2 us (19%)
  local copies, waits for them, and re-layouts  9.24 us (5%)
  other arithmetic  7.24 us (4%)
    ppermute x49, waiting for transfers between devices, swap(): lax.ppermute(rows, axis, [(i, i ^ bits) for i in range(lax.axis_size(axis...  80.7 us
    ppermute x49, starting transfers between devices, swap(): lax.ppermute(rows, axis, [(i, i ^ bits) for i in range(lax.axis_size(axis...  68.1 us
    pallas_call x1, Pallas kernels, expert_terms(): pl.pallas_call(kernel, grid=(2, gtiles + dtiles), out_shape=out_shape, in...  22 us
    pallas_call x1, Pallas kernels, project_attention(): pl.pallas_call(functools.partial(far_kernel, nseq), out_shape=[jax.ShapeD...  11.3 us
    unnamed x60, local copies, waits for them, and re-layouts  7.85 us
  transfers between devices with their start and end apart: 49, of which 25 were waited for; matrix products, arithmetic and copies ran while one was open for 4% of the time, Pallas kernels for 2%

profile of v1, /device:TPU:0, one launch (start us, length us, event | category | flops | bytes accessed | tf_op | source)
XLA Modules:
  0.0 204.6 jit_solution(9248065387346602287)
XLA Ops:
  5.6 2.9 %collective-permute-start.3 = (bf16[512,256]{1,0:T(8,128)(2,1)S(1)}, bf16[512,256]{1,0:T(8,128)(2,1)S(1)}, u32[]{:S(2)}, u32[]{:S(2)}) collective-permute-start(bf16[512,256]{1,0:T(8,128)(2,1)S(1)} %get-tuple-element.40), channel_id=1, source_target_pairs={{0,16},{8,24},{16,0},{24,8},{1,17},{9,25},{17,1},{25,9},{2,18},{10... | collective-permute-start | bytes 786440 | tf_op jit(solution)/shard_map/ppermute | solution.py:26
  11.0 13.8 %collective-permute-done.1.refs_2_ = bf16[64,1280]{1,0:T(8,128)(2,1)S(1)} collective-permute-done((bf16[64,1280]{1,0:T(8,128)(2,1)S(1)}, bf16[64,1280]{1,0:T(8,128)(2,1)S(1)}, u32[]{:S(2)}, u32[]{:S(2)}) %collective-permute-start.1) | collective-permute-done | bytes 163872 | tf_op jit(solution)/shard_map/ppermute | solution.py:26
  24.8 2.4 %collective-permute-done.2.refs_3_ = bf16[64,1280]{1,0:T(8,128)(2,1)S(1)} collective-permute-done((bf16[64,1280]{1,0:T(8,128)(2,1)S(1)}, bf16[64,1280]{1,0:T(8,128)(2,1)S(1)}, u32[]{:S(2)}, u32[]{:S(2)}) %collective-permute-start.2) | collective-permute-done | bytes 163872 | tf_op jit(solution)/shard_map/ppermute | solution.py:26
  27.2 4.0 %attend_near.1 = (f32[256,128]{1,0:T(8,128)S(1)}, f32[256,128]{1,0:T(8,128)S(1)}, f32[256,1024]{1,0:T(8,128)S(1)}) custom-call(s32[1]{0:T(128)} %bitcast.1.me_ref, s32[1]{0:T(128)S(6)} %copy.17.len_ref, bf16[64,1280]{1,0:T(8,128)(2,1)S(1)} %get-tuple-element.36.refs_0_, bf16[64,1280]{1,0:T(8,128)(2,1)S(1)} %collective-permute-done.refs_1_, ...), custom_call_target="tpu_custom_call" | custom-call | tf_op jit(solution)/shard_map/attend_near/pallas_call | solution.py:149
  31.3 11.3 %attend_far.1 = (f32[128,2048]{1,0:T(8,128)S(1)}, f32[128,2048]{1,0:T(8,128)S(1)}) custom-call(s32[1]{0:T(128)} %bitcast.1.me_ref, s32[1]{0:T(128)S(6)} %copy.17.len_ref, bf16[64,1280]{1,0:T(8,128)(2,1)S(1)} %get-tuple-element.36.refs_0_, bf16[64,1280]{1,0:T(8,128)(2,1)S(1)} %collective-permute-done.refs_1_, ...), custom_call_target="tpu_custom_call" | custom-call | tf_op jit(solution)/shard_map/attend_far/pallas_call | solution.py:162
  45.3 1.8 collective-permute-start.7
  47.5 6.5 %collective-permute-done.7.refs_0_ = bf16[64,2048]{1,0:T(8,128)(2,1)S(1)} collective-permute-done((bf16[64,2048]{1,0:T(8,128)(2,1)S(1)}, bf16[64,2048]{1,0:T(8,128)(2,1)S(1)}, u32[]{:S(2)}, u32[]{:S(2)}) %collective-permute-start.7) | collective-permute-done | bytes 262176 | tf_op jit(solution)/shard_map/ppermute | solution.py:26
  57.3 3.9 %collective-permute-start.22 = (bf16[64,2176]{1,0:T(8,128)(2,1)S(1)}, bf16[64,2176]{1,0:T(8,128)(2,1)S(1)}, u32[]{:S(2)}, u32[]{:S(2)}) collective-permute-start(bf16[64,2176]{1,0:T(8,128)(2,1)S(1)} %get-tuple-element.50.refs_1_), channel_id=1, source_target_pairs={{0,6},{1,7},{2,4},{3,5},{4,2},{5,3},{6,0},{7,1},{8,14},{9,15},{10,... | collective-permute-start | bytes 835592 | tf_op jit(solution)/shard_map/ppermute | solution.py:26
  62.7 4.9 %collective-permute-done.22.refs_16_ = bf16[64,2176]{1,0:T(8,128)(2,1)S(1)} collective-permute-done((bf16[64,2176]{1,0:T(8,128)(2,1)S(1)}, bf16[64,2176]{1,0:T(8,128)(2,1)S(1)}, u32[]{:S(2)}, u32[]{:S(2)}) %collective-permute-start.22) | collective-permute-done | bytes 278560 | tf_op jit(solution)/shard_map/ppermute | solution.py:26
  69.2 6.6 %collective-permute-start.17 = (bf16[64,2176]{1,0:T(8,128)(2,1)S(1)}, bf16[64,2176]{1,0:T(8,128)(2,1)S(1)}, u32[]{:S(2)}, u32[]{:S(2)}) collective-permute-start(bf16[64,2176]{1,0:T(8,128)(2,1)S(1)} %get-tuple-element.50.refs_1_), channel_id=1, source_target_pairs={{0,4},{1,5},{2,6},{3,7},{4,0},{5,1},{6,2},{7,3},{8,12},{9,13},{10,... | collective-permute-start | bytes 835592 | tf_op jit(solution)/shard_map/ppermute | solution.py:26
  75.8 5.2 %collective-permute-start.12 = (bf16[64,2176]{1,0:T(8,128)(2,1)S(1)}, bf16[64,2176]{1,0:T(8,128)(2,1)S(1)}, u32[]{:S(2)}, u32[]{:S(2)}) collective-permute-start(bf16[64,2176]{1,0:T(8,128)(2,1)S(1)} %get-tuple-element.50.refs_1_), channel_id=1, source_target_pairs={{0,2},{1,3},{2,0},{3,1},{4,6},{5,7},{6,4},{7,5},{8,10},{9,11},{10,... | collective-permute-start | bytes 835592 | tf_op jit(solution)/shard_map/ppermute | solution.py:26
  80.9 6.1 %collective-permute-done.17.refs_11_ = bf16[64,2176]{1,0:T(8,128)(2,1)S(1)} collective-permute-done((bf16[64,2176]{1,0:T(8,128)(2,1)S(1)}, bf16[64,2176]{1,0:T(8,128)(2,1)S(1)}, u32[]{:S(2)}, u32[]{:S(2)}) %collective-permute-start.17) | collective-permute-done | bytes 278560 | tf_op jit(solution)/shard_map/ppermute | solution.py:26
  87.6 2.7 %collective-permute-done.12.refs_6_ = bf16[64,2176]{1,0:T(8,128)(2,1)S(1)} collective-permute-done((bf16[64,2176]{1,0:T(8,128)(2,1)S(1)}, bf16[64,2176]{1,0:T(8,128)(2,1)S(1)}, u32[]{:S(2)}, u32[]{:S(2)}) %collective-permute-start.12) | collective-permute-done | bytes 278560 | tf_op jit(solution)/shard_map/ppermute | solution.py:26
  93.6 3.3 %collective-permute-done.11.refs_5_ = bf16[32,2176]{1,0:T(8,128)(2,1)S(1)} collective-permute-done((bf16[32,2176]{1,0:T(8,128)(2,1)S(1)}, bf16[32,2176]{1,0:T(8,128)(2,1)S(1)}, u32[]{:S(2)}, u32[]{:S(2)}) %collective-permute-start.11) | collective-permute-done | bytes 139296 | tf_op jit(solution)/shard_map/ppermute | solution.py:26
  101.5 4.1 %collective-permute-done.23.refs_17_ = bf16[64,2176]{1,0:T(8,128)(2,1)S(1)} collective-permute-done((bf16[64,2176]{1,0:T(8,128)(2,1)S(1)}, bf16[64,2176]{1,0:T(8,128)(2,1)S(1)}, u32[]{:S(2)}, u32[]{:S(2)}) %collective-permute-start.23) | collective-permute-done | bytes 278560 | tf_op jit(solution)/shard_map/ppermute | solution.py:26
  109.2 6.0 %collective-permute-done.18.refs_12_ = bf16[64,2176]{1,0:T(8,128)(2,1)S(1)} collective-permute-done((bf16[64,2176]{1,0:T(8,128)(2,1)S(1)}, bf16[64,2176]{1,0:T(8,128)(2,1)S(1)}, u32[]{:S(2)}, u32[]{:S(2)}) %collective-permute-start.18) | collective-permute-done | bytes 278560 | tf_op jit(solution)/shard_map/ppermute | solution.py:26
  117.3 5.9 %collective-permute-done.13.refs_7_ = bf16[64,2176]{1,0:T(8,128)(2,1)S(1)} collective-permute-done((bf16[64,2176]{1,0:T(8,128)(2,1)S(1)}, bf16[64,2176]{1,0:T(8,128)(2,1)S(1)}, u32[]{:S(2)}, u32[]{:S(2)}) %collective-permute-start.13) | collective-permute-done | bytes 278560 | tf_op jit(solution)/shard_map/ppermute | solution.py:26
  126.7 2.6 %collective-permute-done.26.refs_20_ = bf16[32,2176]{1,0:T(8,128)(2,1)S(1)} collective-permute-done((bf16[32,2176]{1,0:T(8,128)(2,1)S(1)}, bf16[32,2176]{1,0:T(8,128)(2,1)S(1)}, u32[]{:S(2)}, u32[]{:S(2)}) %collective-permute-start.26) | collective-permute-done | bytes 139296 | tf_op jit(solution)/shard_map/ppermute | solution.py:26
  137.1 2.5 %collective-permute-done.16.refs_10_ = bf16[32,2176]{1,0:T(8,128)(2,1)S(1)} collective-permute-done((bf16[32,2176]{1,0:T(8,128)(2,1)}, bf16[32,2176]{1,0:T(8,128)(2,1)S(1)}, u32[]{:S(2)}, u32[]{:S(2)}) %collective-permute-start.16) | collective-permute-done | bytes 139296 | tf_op jit(solution)/shard_map/ppermute | solution.py:26
  139.7 22.0 %experts.1 = (bf16[64,2048]{1,0:T(8,128)(2,1)S(1)}, bf16[64,2048]{1,0:T(8,128)(2,1)S(1)}, bf16[64,2048]{1,0:T(8,128)(2,1)S(1)}, bf16[64,2048]{1,0:T(8,128)(2,1)}...) custom-call(s32[2]{0:T(128)S(1)} %pad_add_fusion.refs_0_, ...), custom_call_target="tpu_custom_call" | custom-call | tf_op jit(solution)/shard_map/experts/pallas_call | solution.py:379
  167.2 2.6 %collective-permute-done.30 = bf16[64,2048]{1,0:T(8,128)(2,1)S(1)} collective-permute-done((bf16[64,2048]{1,0:T(8,128)(2,1)}, bf16[64,2048]{1,0:T(8,128)(2,1)S(1)}, u32[]{:S(2)}, u32[]{:S(2)}) %collective-permute-start.30) | collective-permute-done | bytes 262176 | tf_op jit(solution)/shard_map/ppermute | solution.py:26
  191.3 3.5 %collective-permute-start.44 = (bf16[64,2048]{1,0:T(8,128)(2,1)S(1)}, bf16[64,2048]{1,0:T(8,128)(2,1)S(1)}, u32[]{:S(2)}, u32[]{:S(2)}) collective-permute-start(bf16[64,2048]{1,0:T(8,128)(2,1)S(1)} %pad_maximum_fusion.2), channel_id=1, source_target_pairs={{0,2},{1,3},{2,0},{3,1},{4,6},{5,7},{6,4},{7,5},{8,10},{9,11},{10,... | collective-permute-start | bytes 786440 | tf_op jit(solution)/shard_map/ppermute | solution.py:26
  194.8 3.5 %collective-permute-done.34 = bf16[64,2048]{1,0:T(8,128)(2,1)S(1)} collective-permute-done((bf16[64,2048]{1,0:T(8,128)(2,1)S(1)}, bf16[64,2048]{1,0:T(8,128)(2,1)S(1)}, u32[]{:S(2)}, u32[]{:S(2)}) %collective-permute-start.34) | collective-permute-done | bytes 262176 | tf_op jit(solution)/shard_map/ppermute | solution.py:26
  198.3 5.4 %collective-permute-done.39 = bf16[64,2048]{1,0:T(8,128)(2,1)S(1)} collective-permute-done((bf16[64,2048]{1,0:T(8,128)(2,1)S(1)}, bf16[64,2048]{1,0:T(8,128)(2,1)S(1)}, u32[]{:S(2)}, u32[]{:S(2)}) %collective-permute-start.39) | collective-permute-done | bytes 262176 | tf_op jit(solution)/shard_map/ppermute | solution.py:26
  (169 shorter events, 70.0 us)
Async XLA Ops:
  5.6 21.6 %collective-permute-start.5 = (bf16[512,256]{1,0:T(8,128)(2,1)S(1)}, bf16[512,256]{1,0:T(8,128)(2,1)S(1)}, u32[]{:S(2)}, u32[]{:S(2)}) collective-permute-start(bf16[512,256]{1,0:T(8,128)(2,1)S(1)} %get-tuple-element.43), channel_id=1, source_target_pairs={{0,8},{8,0},{16,24},{24,16},{1,9},{9,1},{17,25},{25,17},{2,10},{10... | collective-permute-start | bytes 786440 | tf_op jit(solution)/shard_map/ppermute | solution.py:26
  5.6 25.6 %collective-permute-start.3 = (bf16[512,256]{1,0:T(8,128)(2,1)S(1)}, bf16[512,256]{1,0:T(8,128)(2,1)S(1)}, u32[]{:S(2)}, u32[]{:S(2)}) collective-permute-start(bf16[512,256]{1,0:T(8,128)(2,1)S(1)} %get-tuple-element.40), channel_id=1, source_target_pairs={{0,16},{8,24},{16,0},{24,8},{1,17},{9,25},{17,1},{25,9},{2,18},{10... | collective-permute-start | bytes 786440 | tf_op jit(solution)/shard_map/ppermute | solution.py:26
  8.6 22.6 %collective-permute-start.4 = (bf16[512,256]{1,0:T(8,128)(2,1)S(1)}, bf16[512,256]{1,0:T(8,128)(2,1)S(1)}, u32[]{:S(2)}, u32[]{:S(2)}) collective-permute-start(bf16[512,256]{1,0:T(8,128)(2,1)S(1)} %get-tuple-element.41), channel_id=1, source_target_pairs={{0,24},{8,16},{16,8},{24,0},{1,25},{9,17},{17,9},{25,1},{2,26},{10... | collective-permute-start | bytes 786440 | tf_op jit(solution)/shard_map/ppermute | solution.py:26
  8.6 16.2 %collective-permute-start.1 = (bf16[64,1280]{1,0:T(8,128)(2,1)S(1)}, bf16[64,1280]{1,0:T(8,128)(2,1)S(1)}, u32[]{:S(2)}, u32[]{:S(2)}) collective-permute-start(bf16[64,1280]{1,0:T(8,128)(2,1)S(1)} %get-tuple-element.38), channel_id=1, source_target_pairs={{0,16},{8,24},{16,0},{24,8},{1,17},{9,25},{17,1},{25,9},{2,18},{10... | collective-permute-start | bytes 491528 | tf_op jit(solution)/shard_map/ppermute | solution.py:26
  10.0 17.2 %collective-permute-start.2 = (bf16[64,1280]{1,0:T(8,128)(2,1)S(1)}, bf16[64,1280]{1,0:T(8,128)(2,1)S(1)}, u32[]{:S(2)}, u32[]{:S(2)}) collective-permute-start(bf16[64,1280]{1,0:T(8,128)(2,1)S(1)} %get-tuple-element.39), channel_id=1, source_target_pairs={{0,24},{8,16},{16,8},{24,0},{1,25},{9,17},{17,9},{25,1},{2,26},{10... | collective-permute-start | bytes 491528 | tf_op jit(solution)/shard_map/ppermute | solution.py:26
  43.0 96.6 %collective-permute-start.27 = (bf16[1,2048,768]{2,1,0:T(8,128)(2,1)}, bf16[1,2048,768]{2,1,0:T(8,128)(2,1)}, u32[]{:S(2)}, u32[]{:S(2)}) collective-permute-start(bf16[1,2048,768]{2,1,0:T(8,128)(2,1)} %refs_21_.1), channel_id=1, source_target_pairs={{0,8},{8,0},{16,24},{24,16},{1,9},{9,1},{17,25},{25,17},{2,10},{10... | collective-permute-start | bytes 9437192 | tf_op jit(solution)/shard_map/ppermute | solution.py:26
  43.2 96.4 %collective-permute-start.28 = (bf16[1,2048,768]{2,1,0:T(8,128)(2,1)}, bf16[1,2048,768]{2,1,0:T(8,128)(2,1)}, u32[]{:S(2)}, u32[]{:S(2)}) collective-permute-start(bf16[1,2048,768]{2,1,0:T(8,128)(2,1)} %refs_22_.1), channel_id=1, source_target_pairs={{0,8},{8,0},{16,24},{24,16},{1,9},{9,1},{17,25},{25,17},{2,10},{10... | collective-permute-start | bytes 9437192 | tf_op jit(solution)/shard_map/ppermute | solution.py:26
  43.5 96.1 %collective-permute-start.29 = (bf16[1,768,2048]{2,1,0:T(8,128)(2,1)}, bf16[1,768,2048]{2,1,0:T(8,128)(2,1)}, u32[]{:S(2)}, u32[]{:S(2)}) collective-permute-start(bf16[1,768,2048]{2,1,0:T(8,128)(2,1)} %refs_23_.1), channel_id=1, source_target_pairs={{0,8},{8,0},{16,24},{24,16},{1,9},{9,1},{17,25},{25,17},{2,10},{10... | collective-permute-start | bytes 9437192 | tf_op jit(solution)/shard_map/ppermute | solution.py:26
  45.3 8.7 %collective-permute-start.7 = (bf16[64,2048]{1,0:T(8,128)(2,1)S(1)}, bf16[64,2048]{1,0:T(8,128)(2,1)S(1)}, u32[]{:S(2)}, u32[]{:S(2)}) collective-permute-start(bf16[64,2048]{1,0:T(8,128)(2,1)S(1)} %fusion), channel_id=1, source_target_pairs={{0,16},{8,24},{16,0},{24,8},{1,17},{9,25},{17,1},{25,9},{2,18},{10... | collective-permute-start | bytes 786440 | tf_op jit(solution)/shard_map/ppermute | solution.py:26
  57.3 10.4 %collective-permute-start.22 = (bf16[64,2176]{1,0:T(8,128)(2,1)S(1)}, bf16[64,2176]{1,0:T(8,128)(2,1)S(1)}, u32[]{:S(2)}, u32[]{:S(2)}) collective-permute-start(bf16[64,2176]{1,0:T(8,128)(2,1)S(1)} %get-tuple-element.50.refs_1_), channel_id=1, source_target_pairs={{0,6},{1,7},{2,4},{3,5},{4,2},{5,3},{6,0},{7,1},{8,14},{9,15},{10,... | collective-permute-start | bytes 835592 | tf_op jit(solution)/shard_map/ppermute | solution.py:26
  69.2 17.9 %collective-permute-start.17 = (bf16[64,2176]{1,0:T(8,128)(2,1)S(1)}, bf16[64,2176]{1,0:T(8,128)(2,1)S(1)}, u32[]{:S(2)}, u32[]{:S(2)}) collective-permute-start(bf16[64,2176]{1,0:T(8,128)(2,1)S(1)} %get-tuple-element.50.refs_1_), channel_id=1, source_target_pairs={{0,4},{1,5},{2,6},{3,7},{4,0},{5,1},{6,2},{7,3},{8,12},{9,13},{10,... | collective-permute-start | bytes 835592 | tf_op jit(solution)/shard_map/ppermute | solution.py:26
  75.8 14.5 %collective-permute-start.12 = (bf16[64,2176]{1,0:T(8,128)(2,1)S(1)}, bf16[64,2176]{1,0:T(8,128)(2,1)S(1)}, u32[]{:S(2)}, u32[]{:S(2)}) collective-permute-start(bf16[64,2176]{1,0:T(8,128)(2,1)S(1)} %get-tuple-element.50.refs_1_), channel_id=1, source_target_pairs={{0,2},{1,3},{2,0},{3,1},{4,6},{5,7},{6,4},{7,5},{8,10},{9,11},{10,... | collective-permute-start | bytes 835592 | tf_op jit(solution)/shard_map/ppermute | solution.py:26
  96.9 8.8 %collective-permute-start.23 = (bf16[64,2176]{1,0:T(8,128)(2,1)S(1)}, bf16[64,2176]{1,0:T(8,128)(2,1)S(1)}, u32[]{:S(2)}, u32[]{:S(2)}) collective-permute-start(bf16[64,2176]{1,0:T(8,128)(2,1)S(1)} %collective-permute-done.22.refs_16_), channel_id=1, source_target_pairs={{0,16},{8,24},{16,0},{24,8},{1,17},{9,25},{17,1},{25,9},{2,18},{10... | collective-permute-start | bytes 835592 | tf_op jit(solution)/shard_map/ppermute | solution.py:26
  105.7 9.5 %collective-permute-start.18 = (bf16[64,2176]{1,0:T(8,128)(2,1)S(1)}, bf16[64,2176]{1,0:T(8,128)(2,1)S(1)}, u32[]{:S(2)}, u32[]{:S(2)}) collective-permute-start(bf16[64,2176]{1,0:T(8,128)(2,1)S(1)} %collective-permute-done.17.refs_11_), channel_id=1, source_target_pairs={{0,16},{8,24},{16,0},{24,8},{1,17},{9,25},{17,1},{25,9},{2,18},{10... | collective-permute-start | bytes 835592 | tf_op jit(solution)/shard_map/ppermute | solution.py:26
  107.6 8.7 %collective-permute-start.14 = (bf16[64,2176]{1,0:T(8,128)(2,1)S(1)}, bf16[64,2176]{1,0:T(8,128)(2,1)S(1)}, u32[]{:S(2)}, u32[]{:S(2)}) collective-permute-start(bf16[64,2176]{1,0:T(8,128)(2,1)S(1)} %collective-permute-done.12.refs_6_), channel_id=1, source_target_pairs={{0,1},{1,0},{2,3},{3,2},{4,5},{5,4},{6,7},{7,6},{8,9},{9,8},{10,11... | collective-permute-start | bytes 835592 | tf_op jit(solution)/shard_map/ppermute | solution.py:26
  163.1 9.5 %collective-permute-start.32 = (bf16[64,2048]{1,0:T(8,128)(2,1)}, bf16[64,2048]{1,0:T(8,128)(2,1)S(1)}, u32[]{:S(2)}, u32[]{:S(2)}) collective-permute-start(bf16[64,2048]{1,0:T(8,128)(2,1)} %get-tuple-element.54), channel_id=1, source_target_pairs={{0,1},{1,0},{2,3},{3,2},{4,5},{5,4},{6,7},{7,6},{8,9},{9,8},{10,11... | collective-permute-start | bytes 786440 | tf_op jit(solution)/shard_map/ppermute | solution.py:26
  164.2 11.2 %collective-permute-start.35 = (bf16[64,2048]{1,0:T(8,128)(2,1)}, bf16[64,2048]{1,0:T(8,128)(2,1)S(1)}, u32[]{:S(2)}, u32[]{:S(2)}) collective-permute-start(bf16[64,2048]{1,0:T(8,128)(2,1)} %get-tuple-element.56), channel_id=1, source_target_pairs={{0,16},{8,24},{16,0},{24,8},{1,17},{9,25},{17,1},{25,9},{2,18},{10... | collective-permute-start | bytes 786440 | tf_op jit(solution)/shard_map/ppermute | solution.py:26
  165.1 13.0 %collective-permute-start.37 = (bf16[64,2048]{1,0:T(8,128)(2,1)}, bf16[64,2048]{1,0:T(8,128)(2,1)S(1)}, u32[]{:S(2)}, u32[]{:S(2)}) collective-permute-start(bf16[64,2048]{1,0:T(8,128)(2,1)} %get-tuple-element.58), channel_id=1, source_target_pairs={{0,1},{1,0},{2,3},{3,2},{4,5},{5,4},{6,7},{7,6},{8,9},{9,8},{10,11... | collective-permute-start | bytes 786440 | tf_op jit(solution)/shard_map/ppermute | solution.py:26
  165.9 13.8 %collective-permute-start.40 = (bf16[64,2048]{1,0:T(8,128)(2,1)}, bf16[64,2048]{1,0:T(8,128)(2,1)S(1)}, u32[]{:S(2)}, u32[]{:S(2)}) collective-permute-start(bf16[64,2048]{1,0:T(8,128)(2,1)} %get-tuple-element.60), channel_id=1, source_target_pairs={{0,16},{8,24},{16,0},{24,8},{1,17},{9,25},{17,1},{25,9},{2,18},{10... | collective-permute-start | bytes 786440 | tf_op jit(solution)/shard_map/ppermute | solution.py:26
  169.8 12.1 %collective-permute-start.42 = (bf16[64,2048]{1,0:T(8,128)(2,1)}, bf16[64,2048]{1,0:T(8,128)(2,1)S(1)}, u32[]{:S(2)}, u32[]{:S(2)}) collective-permute-start(bf16[64,2048]{1,0:T(8,128)(2,1)} %get-tuple-element.62), channel_id=1, source_target_pairs={{0,1},{1,0},{2,3},{3,2},{4,5},{5,4},{6,7},{7,6},{8,9},{9,8},{10,11... | collective-permute-start | bytes 786440 | tf_op jit(solution)/shard_map/ppermute | solution.py:26
  172.6 11.8 %collective-permute-start.45 = (bf16[64,2048]{1,0:T(8,128)(2,1)S(1)}, bf16[64,2048]{1,0:T(8,128)(2,1)S(1)}, u32[]{:S(2)}, u32[]{:S(2)}) collective-permute-start(bf16[64,2048]{1,0:T(8,128)(2,1)S(1)} %get-tuple-element.64), channel_id=1, source_target_pairs={{0,16},{8,24},{16,0},{24,8},{1,17},{9,25},{17,1},{25,9},{2,18},{10... | collective-permute-start | bytes 786440 | tf_op jit(solution)/shard_map/ppermute | solution.py:26
  175.4 9.9 %collective-permute-start.47 = (bf16[64,2048]{1,0:T(8,128)(2,1)}, bf16[64,2048]{1,0:T(8,128)(2,1)S(1)}, u32[]{:S(2)}, u32[]{:S(2)}) collective-permute-start(bf16[64,2048]{1,0:T(8,128)(2,1)} %get-tuple-element.66), channel_id=1, source_target_pairs={{0,1},{1,0},{2,3},{3,2},{4,5},{5,4},{6,7},{7,6},{8,9},{9,8},{10,11... | collective-permute-start | bytes 786440 | tf_op jit(solution)/shard_map/ppermute | solution.py:26
  190.3 13.4 %collective-permute-start.39 = (bf16[64,2048]{1,0:T(8,128)(2,1)S(1)}, bf16[64,2048]{1,0:T(8,128)(2,1)S(1)}, u32[]{:S(2)}, u32[]{:S(2)}) collective-permute-start(bf16[64,2048]{1,0:T(8,128)(2,1)S(1)} %pad_maximum_fusion.1), channel_id=1, source_target_pairs={{0,4},{1,5},{2,6},{3,7},{4,0},{5,1},{6,2},{7,3},{8,12},{9,13},{10,... | collective-permute-start | bytes 786440 | tf_op jit(solution)/shard_map/ppermute | solution.py:26
  191.3 12.5 %collective-permute-start.44 = (bf16[64,2048]{1,0:T(8,128)(2,1)S(1)}, bf16[64,2048]{1,0:T(8,128)(2,1)S(1)}, u32[]{:S(2)}, u32[]{:S(2)}) collective-permute-start(bf16[64,2048]{1,0:T(8,128)(2,1)S(1)} %pad_maximum_fusion.2), channel_id=1, source_target_pairs={{0,2},{1,3},{2,0},{3,1},{4,6},{5,7},{6,4},{7,5},{8,10},{9,11},{10,... | collective-permute-start | bytes 786440 | tf_op jit(solution)/shard_map/ppermute | solution.py:26
  (54 other events, 846.7 us)

commit v2 on v1

v2 whole, which is shorter than its diff:
```python
import functools
import math

import jax
import jax.numpy as jnp
from jax import lax
from jax.experimental import pallas as pl
from jax.experimental.pallas import tpu as pltpu
from jax.sharding import PartitionSpec as P

QH = 32
KVH = 4
HD = 128
TOPK = 8
MASKED = -1e30
EXPERT_MIB = 46
NEAR_MIB = 58
FAR_MIB = 54
EXP2_SCALE = math.log2(math.e) / math.sqrt(HD)
NT = (((1,), (1,)), ((), ()))
TN = (((0,), (0,)), ((), ()))
VMEM = pl.BlockSpec(memory_space=pltpu.VMEM)
SMEM = pl.BlockSpec(memory_space=pltpu.SMEM)
ANY = pl.BlockSpec(memory_space=pl.ANY)
f32 = jnp.float32
bf16 = jnp.bfloat16


def swap(rows, axis, bits):
    return lax.ppermute(rows, axis, [(i, i ^ bits) for i in range(lax.axis_size(axis))])


def params(mib):
    return pltpu.CompilerParams(vmem_limit_bytes=mib << 20)


def pack_kernel(nseq, me_ref, q_ref, nk_ref, nv_ref, ck_ref, cv_ref, *refs):
    heads, caches, sem = refs[:nseq], refs[nseq : 2 * nseq], refs[-1]
    qcols = QH // nseq * HD
    copies = []
    for k in range(nseq):
        dest = me_ref[0] ^ k
        qat = pl.ds(pl.multiple_of(dest * qcols, HD), qcols)
        kvat = pl.ds(pl.multiple_of(dest * KVH // nseq * HD, HD), HD)
        pairs = (
            (q_ref.at[:, qat], heads[k].at[:, :qcols]),
            (nk_ref.at[:, kvat], heads[k].at[:, qcols : qcols + HD]),
            (nv_ref.at[:, kvat], heads[k].at[:, qcols + HD :]),
            (ck_ref.at[:, kvat], caches[k].at[:, :HD]),
            (cv_ref.at[:, kvat], caches[k].at[:, HD:]),
        )
        copies += [pltpu.make_async_copy(a, b, sem.at[k, i]) for i, (a, b) in enumerate(pairs)]
    for copy in copies:
        copy.start()
    for copy in copies:
        copy.wait()


def pack(me, arrays, nseq):
    tokens, slots = arrays[0].shape[0], arrays[-1].shape[0]
    shapes = [jax.ShapeDtypeStruct((tokens, (QH // nseq + 2) * HD), bf16)] * nseq
    shapes += [jax.ShapeDtypeStruct((slots, 2 * HD), bf16)] * nseq
    outs = pl.pallas_call(
        functools.partial(pack_kernel, nseq),
        out_shape=shapes,
        in_specs=[SMEM] + [ANY] * len(arrays),
        out_specs=[VMEM] * len(shapes),
        scratch_shapes=[pltpu.SemaphoreType.DMA((nseq, len(arrays)))],
        compiler_params=params(61),
        name="pack_heads",
    )(me, *arrays)
    return outs[:nseq], outs[nseq:]


def head_rows(heads, start):
    return jnp.concatenate([ref[:, start : start + HD] for ref in heads], 0)


def slot_bias(me, length, ks, slots):
    parts = []
    for k in ks:
        pos = (me ^ k) * slots + lax.broadcasted_iota(jnp.int32, (1, slots), 1)
        parts.append(jnp.where(pos < length, f32(0.0), f32(MASKED)))
    return jnp.concatenate(parts, 1)


def near_kernel(nseq, me_ref, len_ref, *refs):
    heads, caches = refs[:nseq], refs[nseq : nseq + 2]
    peak_ref, sum_ref, acc_ref = refs[nseq + 2 :]
    group = QH // nseq
    qcols = group * HD
    me = me_ref[0]
    slots, tokens = caches[0].shape[0], heads[0].shape[0]
    qtok = nseq * tokens
    bias = slot_bias(me, len_ref[0], (0, 1), slots)
    keys = jnp.concatenate([ref[:, :HD] for ref in caches], 0)
    vals = jnp.concatenate([ref[:, HD:] for ref in caches], 0)
    new_keys, new_vals = head_rows(heads, qcols), head_rows(heads, qcols + HD)
    row = lax.broadcasted_iota(jnp.int32, (qtok, qtok), 0)
    col = lax.broadcasted_iota(jnp.int32, (qtok, qtok), 1)
    qpos = (me ^ (row // tokens)) * tokens + row % tokens
    kpos = (me ^ (col // tokens)) * tokens + col % tokens
    new_bias = jnp.where(kpos <= qpos, f32(0.0), f32(MASKED))
    for g in range(group):
        q = head_rows(heads, g * HD)
        s = lax.dot_general(q, keys, NT, preferred_element_type=f32) + bias
        t = lax.dot_general(q, new_keys, NT, preferred_element_type=f32) + new_bias
        peak = jnp.maximum(jnp.max(s, axis=1, keepdims=True), jnp.max(t, axis=1, keepdims=True))
        p = jnp.exp2((s - peak) * f32(EXP2_SCALE))
        r = jnp.exp2((t - peak) * f32(EXP2_SCALE))
        peak_ref[:, g : g + 1] = peak
        sum_ref[:, g : g + 1] = jnp.sum(p, axis=1, keepdims=True) + jnp.sum(r, axis=1, keepdims=True)
        acc = jnp.dot(p.astype(bf16), vals, preferred_element_type=f32)
        acc += jnp.dot(r.astype(bf16), new_vals, preferred_element_type=f32)
        acc_ref[:, g * HD : (g + 1) * HD] = acc


def far_kernel(nseq, me_ref, len_ref, *refs):
    heads, caches = refs[:nseq], refs[nseq : 2 * nseq - 2]
    peak_ref, sum_ref, acc_ref, w_hbm = refs[2 * nseq - 2 : 2 * nseq + 2]
    outs = refs[2 * nseq + 2 : -3]
    attn_ref, w_ref, sem = refs[-3:]
    load = pltpu.make_async_copy(w_hbm, w_ref, sem)
    load.start()
    group = QH // nseq
    slots, tokens = caches[0].shape[0], heads[0].shape[0]
    bias = slot_bias(me_ref[0], len_ref[0], range(2, nseq), slots)
    keys = jnp.concatenate([ref[:, :HD] for ref in caches], 0)
    vals = jnp.concatenate([ref[:, HD:] for ref in caches], 0)
    for g in range(group):
        at = slice(g * HD, (g + 1) * HD)
        q = head_rows(heads, g * HD)
        s = lax.dot_general(q, keys, NT, preferred_element_type=f32) + bias
        old = peak_ref[:, g : g + 1]
        peak = jnp.maximum(jnp.max(s, axis=1, keepdims=True), old)
        fade = jnp.exp2((old - peak) * f32(EXP2_SCALE))
        p = jnp.exp2((s - peak) * f32(EXP2_SCALE))
        total = sum_ref[:, g : g + 1] * fade + jnp.sum(p, axis=1, keepdims=True)
        acc = acc_ref[:, at] * fade + jnp.dot(p.astype(bf16), vals, preferred_element_type=f32)
        attn_ref[:, at] = (acc / total).astype(bf16)
    load.wait()
    send, near, far = outs
    places = []
    for k in range(nseq):
        if k % 2:
            places.append((send, k // 2 * tokens))
        else:
            places.append((far, (k // 2 - 1) * tokens) if k else (near, 0))
    step = 512
    for at in range(0, w_ref.shape[1], step):
        cols = slice(at, at + step)
        total = jnp.dot(attn_ref[...], w_ref[:, cols], preferred_element_type=f32)
        for k, (out, row) in enumerate(places):
            out[row : row + tokens, cols] = total[k * tokens : (k + 1) * tokens]


def project_attention(
    me, length, queries, new_keys, new_values, cache_keys, cache_values, out_weight, weights
):
    nseq = lax.axis_size("seq")
    tokens = queries.shape[0]
    width = out_weight.shape[1]
    group = QH // nseq
    qtok = nseq * tokens
    heads, caches = pack(me, (queries, new_keys, new_values, cache_keys, cache_values), nseq)
    order = sorted(range(1, nseq), reverse=True)
    heads = {0: heads[0]} | {k: swap(heads[k], "seq", k) for k in order}
    caches = {0: caches[0]} | {k: swap(caches[k], "seq", k) for k in order}
    heads, weights = lax.optimization_barrier((heads, weights))
    others = [swap(w, "seq", 1) for w in weights[:2]]
    heads = [heads[k] for k in range(nseq)]
    caches = [caches[k] for k in range(nseq)]
    state = pl.pallas_call(
        functools.partial(near_kernel, nseq),
        out_shape=[
            jax.ShapeDtypeStruct((qtok, HD), f32),
            jax.ShapeDtypeStruct((qtok, HD), f32),
            jax.ShapeDtypeStruct((qtok, group * HD), f32),
        ],
        in_specs=[SMEM] * 2 + [VMEM] * (nseq + 2),
        out_specs=[VMEM] * 3,
        compiler_params=params(NEAR_MIB),
        name="attend_near",
    )(me, length, *heads, *caches[:2])
    half = nseq // 2 * tokens
    parts = pl.pallas_call(
        functools.partial(far_kernel, nseq),
        out_shape=[
            jax.ShapeDtypeStruct((half, width), f32),
            jax.ShapeDtypeStruct((tokens, width), f32),
            jax.ShapeDtypeStruct((half - tokens, width), f32),
        ],
        in_specs=[SMEM] * 2 + [VMEM] * (2 * nseq + 1) + [ANY],
        out_specs=[VMEM] * 3,
        scratch_shapes=[
            pltpu.VMEM((qtok, group * HD), bf16),
            pltpu.VMEM(out_weight.shape, bf16),
            pltpu.SemaphoreType.DMA,
        ],
        compiler_params=params(FAR_MIB),
        name="attend_far",
    )(me, length, *heads, *caches[2:], *state, out_weight)
    (send, near, far), others = lax.optimization_barrier((parts, others))
    got = swap(send, "seq", 1)
    if weights:
        got, last = lax.optimization_barrier((got, weights[2]))
        others.append(swap(last, "seq", 1))
    terms = [near, got[:tokens]]
    for at in range(tokens, half, tokens):
        both = far[at - tokens : at] + got[at : at + tokens]
        terms.append(swap(both.astype(bf16), "seq", 2 * at // tokens))
    return terms, [*weights, *others]


def norm_kernel(nterms, res_ref, *refs):
    gain_ref, router_ref, ids_ref, mixed_ref, rows_ref = refs[nterms:]
    tokens, width = res_ref.shape
    mixed = res_ref[...].astype(f32)
    for ref in refs[:nterms]:
        mixed += ref[...].astype(f32)
    mixed_ref[...] = mixed
    meansq = jnp.mean(mixed * mixed, axis=1, keepdims=True)
    normed = (mixed / jnp.sqrt(meansq + 1e-06) * gain_ref[...]).astype(bf16)
    rows_ref[:, :width] = normed
    logits = lax.dot_general(router_ref[...], normed, NT, preferred_element_type=f32)
    nexp = logits.shape[0]
    expert = lax.broadcasted_iota(jnp.int32, (nexp, tokens), 0)
    chosen = expert == ids_ref[0:1, :]
    for k in range(1, ids_ref.shape[0]):
        chosen = jnp.logical_or(chosen, expert == ids_ref[k : k + 1, :])
    expo = jnp.where(chosen, jnp.exp(logits), f32(0.0))
    gates = expo / jnp.sum(expo, axis=0, keepdims=True)
    high = gates.astype(bf16)
    low = (gates - high.astype(f32)).astype(bf16)
    extra = rows_ref.shape[1] - width
    row = lax.broadcasted_iota(jnp.int32, (nexp, extra), 0)
    col = lax.broadcasted_iota(jnp.int32, (nexp, extra), 1)
    spread = lax.dot_general(high, (col == row).astype(bf16), TN, preferred_element_type=f32)
    spread += lax.dot_general(low, (col == row + nexp).astype(bf16), TN, preferred_element_type=f32)
    rows_ref[:, width:] = spread.astype(bf16)


def norm_rows(residual, terms, gain, router, ids):
    tokens, width = residual.shape
    extra = -(-2 * router.shape[1] // 128) * 128
    return pl.pallas_call(
        functools.partial(norm_kernel, len(terms)),
        out_shape=[
            jax.ShapeDtypeStruct((tokens, width), f32),
            jax.ShapeDtypeStruct((tokens, width + extra), bf16),
        ],
        in_specs=[VMEM] * (4 + len(terms)),
        out_specs=[VMEM] * 2,
        compiler_params=params(16),
        name="norm_and_route",
    )(residual, *terms, gain.reshape(1, width), router.T, ids.T)


def gather_plane(col, kz, sides, first=None):
    right = [swap(col, "seq", 2 * kx) for kx in range(1, sides)]
    up = swap(col, "exp", 1)
    if first:
        right, up, first = lax.optimization_barrier((right, up, first))
    if kz % 2:
        over = [swap(r, "exp", 1) for r in right]
    else:
        over = [swap(up, "seq", 2 * kx) for kx in range(1, sides)]
    return [col, *right, up, *over], first


def plane_layout(mode, sides, tokens):
    half = tokens // 2
    rows, moves = [], []
    if mode == "halves":
        rows = [2 * half, sides * half, (sides - 1) * 2 * half, sides * half]
        for ky in range(2):
            for kx in range(sides):
                row = (ky * sides + kx) * tokens
                top = (2, ((kx - 1) * 2 + ky) * half) if kx else (0, ky * half)
                moves.append((row, half, *top))
                moves.append((row + half, half, 3 if ky else 1, kx * half))
    elif mode == "x":
        rows = [2 * tokens, (sides - 1) * 2 * tokens]
        for ky in range(2):
            for kx in range(sides):
                to = (1, ((kx - 1) * 2 + ky) * tokens) if kx else (0, ky * tokens)
                moves.append(((ky * sides + kx) * tokens, tokens, *to))
    else:
        rows = [sides * tokens, sides * tokens]
        for ky in range(2):
            for kx in range(sides):
                moves.append(((ky * sides + kx) * tokens, tokens, ky, kx * tokens))
    return rows, moves


def expert_kernel(layouts, per_group, tokens, cap, nexp, mine_ref, *refs):
    planes = len(layouts)
    pieces = planes * per_group
    blocks = refs[:pieces]
    weights = (refs[pieces : pieces + 3], refs[pieces + 3 : pieces + 6])
    nouts = sum(len(rows) for rows, _ in layouts)
    outs = refs[pieces + 6 : pieces + 6 + nouts]
    got_ref, x_ref, act_ref, hot_ref, wide_ref, down_ref, sem, got_sem = refs[pieces + 6 + nouts :]
    copies = [
        pltpu.make_async_copy(
            blocks[g * per_group + i],
            got_ref.at[g, i * tokens : (i + 1) * tokens],
            got_sem.at[g, i],
        )
        for g in range(planes)
        for i in range(per_group)
    ]
    for copy in copies:
        copy.start()
    loads = [
        [
            pltpu.make_async_copy(ws[0].at[0], wide_ref.at[i, 0], sem.at[i, 0]),
            pltpu.make_async_copy(ws[1].at[0], wide_ref.at[i, 1], sem.at[i, 1]),
            pltpu.make_async_copy(ws[2].at[0], down_ref.at[i], sem.at[i, 2]),
        ]
        for i, ws in enumerate(weights)
    ]
    loads[0][0].start()
    loads[0][1].start()
    width = x_ref.shape[2]
    hidden = act_ref.shape[1]
    ext = got_ref.shape[2] - width
    gtok = per_group * tokens
    grows = per_group * cap
    step = 256
    ecol = lax.broadcasted_iota(jnp.int32, (8, ext), 1)
    erow = lax.broadcasted_iota(jnp.int32, (8, ext), 0)
    want = jnp.where(erow == 0, mine_ref[0], jnp.where(erow == 1, mine_ref[1], -ext))
    pick = jnp.logical_or(ecol == want, ecol == want + nexp).astype(bf16)
    trow = lax.broadcasted_iota(jnp.int32, (gtok, gtok), 0)
    tcol = lax.broadcasted_iota(jnp.int32, (gtok, gtok), 1)
    before = jnp.logical_and(trow < tcol, trow // tokens == tcol // tokens).astype(bf16)
    block = lax.broadcasted_iota(jnp.int32, (8, gtok), 1) // tokens
    slot = lax.broadcasted_iota(jnp.int32, (grows, gtok), 0).astype(f32)
    row_gates = [[], []]
    for g in range(planes):
        for copy in copies[g * per_group : (g + 1) * per_group]:
            copy.wait()
        tail = got_ref[g, :, width:]
        gates = lax.dot_general(pick, tail, NT, preferred_element_type=f32)
        chosen = gates > 0.0
        rank = jnp.dot(chosen.astype(bf16), before, preferred_element_type=f32)
        target = jnp.where(chosen, (block * cap).astype(f32) + rank, f32(-1.0))
        hot = jnp.concatenate(
            [(slot == target[i : i + 1, :]).astype(f32) for i in range(2)], 0
        ).astype(bf16)
        hot_ref[g] = hot
        for at in range(0, width, step):
            part = got_ref[g, :, at : at + step]
            got = jnp.dot(hot, part, preferred_element_type=f32).astype(bf16)
            for i in range(2):
                x_ref[i, g * grows : (g + 1) * grows, at : at + step] = got[
                    i * grows : (i + 1) * grows
                ]
        got = jnp.dot(hot, tail, preferred_element_type=f32)
        for i in range(2):
            sel = pick[i : i + 1, :].astype(f32)
            row_gates[i].append(
                jnp.sum(got[i * grows : (i + 1) * grows] * sel, axis=1, keepdims=True)
            )
    loads[0][2].start()
    for i in range(2):
        x = x_ref[i]
        loads[i][0].wait()
        loads[i][1].wait()
        if i == 0:
            loads[1][0].start()
            loads[1][1].start()
        for at in range(0, hidden, step):
            cols = slice(at, at + step)
            gate = jnp.dot(x, wide_ref[i, 0, :, cols], preferred_element_type=f32)
            upv = jnp.dot(x, wide_ref[i, 1, :, cols], preferred_element_type=f32)
            act_ref[:, cols] = (gate / (1.0 + jnp.exp(-gate)) * upv).astype(bf16)
        loads[i][2].wait()
        if i == 0:
            loads[1][2].start()
        row_gate = jnp.concatenate(row_gates[i], 0)
        for at in range(0, width, step):
            cols = slice(at, at + step)
            y = jnp.dot(act_ref[...], down_ref[i, :, cols], preferred_element_type=f32)
            x_ref[i, :, cols] = (y * row_gate).astype(bf16)
    first = 0
    for g, (rows, moves) in enumerate(layouts):
        for at in range(0, width, step):
            cols = slice(at, at + step)
            y = jnp.concatenate(
                [x_ref[i, g * grows : (g + 1) * grows, cols] for i in range(2)], 0
            )
            total = lax.dot_general(hot_ref[g], y, TN, preferred_element_type=f32).astype(bf16)
            for row, count, out, to in moves:
                outs[first + out][to : to + count, cols] = total[row : row + count]
        first += len(rows)


def expert_terms(blocks, modes, sides, mine, weights, cap, nexp):
    planes, per_group = len(blocks), len(blocks[0])
    tokens, wide = blocks[0][0].shape
    _, width, hidden = weights[0].shape
    grows = per_group * cap
    rows = planes * grows
    layouts = [plane_layout(mode, sides, tokens) for mode in modes]
    out_shape = [jax.ShapeDtypeStruct((n, width), bf16) for ns, _ in layouts for n in ns]
    outs = pl.pallas_call(
        functools.partial(expert_kernel, layouts, per_group, tokens, cap, nexp),
        out_shape=out_shape,
        in_specs=[SMEM] + [ANY] * (planes * per_group + len(weights)),
        out_specs=[VMEM] * len(out_shape),
        scratch_shapes=[
            pltpu.VMEM((planes, per_group * tokens, wide), bf16),
            pltpu.VMEM((2, rows, width), bf16),
            pltpu.VMEM((rows, hidden), bf16),
            pltpu.VMEM((planes, 2 * grows, per_group * tokens), bf16),
            pltpu.VMEM((2, 2, width, hidden), bf16),
            pltpu.VMEM((2, hidden, width), bf16),
            pltpu.SemaphoreType.DMA((2, 3)),
            pltpu.SemaphoreType.DMA((planes, per_group)),
        ],
        compiler_params=params(EXPERT_MIB),
        cost_estimate=pl.CostEstimate(
            flops=12 * rows * width * hidden, bytes_accessed=8 * rows * width, transcendentals=0
        ),
        name="experts",
    )(mine, *[block for plane in blocks for block in plane], *weights)
    terms, at = [], 0
    for ns, _ in layouts:
        terms.append(outs[at : at + len(ns)])
        at += len(ns)
    return terms


def add(*terms):
    total = terms[0].astype(f32)
    for term in terms[1:]:
        total = total + term.astype(f32)
    return total


def plane_sum(term, mode, sides):
    if mode == "halves":
        top = plane_sum(term[::2], "x", sides)
        low = plane_sum(term[1::2], "y", sides)
        return jnp.concatenate([top, low], 0)
    keep, send = term
    if mode == "x":
        size = keep.shape[0] // 2
        got = [swap(send[i * 2 * size : (i + 1) * 2 * size], "seq", 2 * i + 2) for i in range(sides - 1)]
        last = swap(add(keep[size:], *[g[size:] for g in got]).astype(bf16), "exp", 1)
        return add(keep[:size], *[g[:size] for g in got], last)
    size = keep.shape[0] // sides
    got = swap(send, "exp", 1)
    last = []
    for kx in range(1, sides):
        at = slice(kx * size, (kx + 1) * size)
        last.append(swap(add(keep[at], got[at]).astype(bf16), "seq", 2 * kx))
    return add(keep[:size], got[:size], *last)


def return_terms(terms, modes, sides):
    sums = [None] * len(terms)
    for kz in reversed(range(len(terms))):
        sums[kz] = plane_sum(terms[kz], modes[kz], sides)
    own = [sums[0]]
    for kz in range(1, len(terms)):
        if kz == 1 or kz % 2 == 0:
            part = sums[kz]
            if kz > 1 and kz + 1 < len(terms):
                part = add(part, swap(sums[kz + 1].astype(bf16), "exp", 2))
            own.append(swap(part.astype(bf16), "exp", 2 * kz))
    return own


def experts_by_chip(rows, width, weights, nexp):
    nseq, nplace = lax.axis_size("seq"), lax.axis_size("exp")
    cap = 3 * rows.shape[0] * TOPK // (2 * nexp)
    planes, sides = nplace // 2, nseq // 2
    me = lax.axis_index("seq") * nplace + lax.axis_index("exp")
    other = (lax.axis_index("seq") ^ 1) * nplace + lax.axis_index("exp")
    mine = jnp.stack([me, other]).astype(jnp.int32)
    columns = [rows]
    for kz in range(1, planes):
        odd = kz > 1 and kz % 2
        columns.append(swap(columns[kz - 1], "exp", 2) if odd else swap(rows, "exp", 2 * kz))
    modes = ["y", "x"] + ["halves"] * (planes - 2)
    terms = []
    for at in range(0, planes, 2):
        even, _ = gather_plane(columns[at], at, sides)
        odd, terms = gather_plane(columns[at + 1], at + 1, sides, terms)
        two = modes[at : at + 2]
        terms = [*terms, *expert_terms([even, odd], two, sides, mine, weights, cap, nexp)]
    return return_terms(terms, modes, sides)


def experts_by_device(rows, width, ids, gate_proj, up_proj, down_proj, nexp):
    tokens = rows.shape[0]
    normed = rows[:, :width]
    gates = rows[:, width : width + nexp].astype(f32) + rows[
        :, width + nexp : width + 2 * nexp
    ].astype(f32)
    gates = jnp.take_along_axis(gates, ids, axis=1)
    capacity = 3 * tokens * TOPK // (2 * nexp)
    flat = ids.reshape(-1)
    member = (flat[:, None] == jnp.arange(nexp, dtype=jnp.int32)[None, :]).astype(jnp.int32)
    rank = jnp.sum((jnp.cumsum(member, axis=0) - 1) * member, axis=1)
    slot = flat * capacity + rank
    place = slot[:, None] == jnp.arange(nexp * capacity, dtype=jnp.int32)[None, :]
    route = jnp.any(place.reshape(tokens, TOPK, nexp * capacity), axis=1).astype(bf16)
    packed = jnp.einsum("ts,td->sd", route, normed, preferred_element_type=f32).astype(bf16)
    outgoing = packed.reshape(nexp, capacity, width)
    taken = lax.all_to_all(outgoing, ("seq", "exp"), split_axis=0, concat_axis=0, tiled=True)
    taken = taken.reshape(-1, width)
    gate = jnp.dot(taken, gate_proj[0], preferred_element_type=f32)
    upv = jnp.dot(taken, up_proj[0], preferred_element_type=f32)
    act = (jax.nn.silu(gate) * upv).astype(bf16)
    result = jnp.dot(act, down_proj[0], preferred_element_type=f32).astype(bf16)
    result = result.reshape(nexp, capacity, width)
    back = lax.all_to_all(result, ("seq", "exp"), split_axis=0, concat_axis=0, tiled=True)
    gathered = back.reshape(nexp * capacity, width)[slot].reshape(tokens, TOPK, width)
    return [jnp.sum(gates[:, :, None] * gathered.astype(f32), axis=1)]


def body(
    queries,
    new_keys,
    new_values,
    cache_keys,
    cache_values,
    cache_len,
    residual_in,
    out_weight,
    norm_gain,
    router_weight,
    expert_ids,
    gate_proj,
    up_proj,
    down_proj,
):
    nseq, nplace = lax.axis_size("seq"), lax.axis_size("exp")
    tokens, width = residual_in.shape[1:]
    nexp = router_weight.shape[1]
    by_chip = nseq * nplace <= 32
    me = lax.axis_index("seq").astype(jnp.int32).reshape(1)
    weights = [gate_proj, up_proj, down_proj]
    parts, pairs = project_attention(
        me,
        cache_len,
        queries[0],
        new_keys[0],
        new_values[0],
        cache_keys[0],
        cache_values[0],
        out_weight,
        weights if by_chip else [],
    )
    mixed, rows = norm_rows(
        residual_in[0], parts, norm_gain, router_weight, expert_ids[0]
    )
    if by_chip:
        rows, pairs = lax.optimization_barrier((rows, pairs))
        terms = experts_by_chip(rows, width, pairs, nexp)
    else:
        terms = experts_by_device(rows, width, expert_ids[0], *weights, nexp)
    return add(mixed, *terms).astype(bf16).reshape(1, tokens, width)


def solution(mesh):
    in_specs = (
        P("exp", "seq", None),
        P("exp", "seq", None),
        P("exp", "seq", None),
        P("exp", "seq", None),
        P("exp", "seq", None),
        P("exp"),
        P("exp", "seq", None),
        P("seq", None),
        P(),
        P(),
        P("exp", "seq", None),
        P(("seq", "exp"), None, None),
        P(("seq", "exp"), None, None),
        P(("seq", "exp"), None, None),
    )
    out_specs = P("exp", "seq", None)
    return jax.shard_map(body, mesh=mesh, in_specs=in_specs, out_specs=out_specs, check_vma=False)
```

time: 205 us -> 159 us (0.78)
  starting transfers between devices: 68.1 us -> 48.2 us
  waiting for transfers between devices: 80.7 us -> 61.9 us
  other arithmetic: 7.24 us -> 2.8 us
  local copies, waits for them, and re-layouts: 9.24 us -> 6.65 us
    ppermute x49 -> x41, starting transfers between devices: 68.1 us -> 48.2 us  [swap(): lax.ppermute(rows, axis, [(i, i ^ bits) for i in range(lax.axis_size(axis...]
    ppermute x49 -> x41, waiting for transfers between devices: 80.7 us -> 61.9 us  [swap(): lax.ppermute(rows, axis, [(i, i ^ bits) for i in range(lax.axis_size(axis...]
    convert_element_type x15 -> x9, other arithmetic: 6.14 us -> 1.6 us  [the longest x1 1.16 us: project_attention(): terms.append(swap(both.astype(bf16), 'seq', 2 * at // tokens))]
    pallas_call x2 -> x3, Pallas kernels: 22.7 us -> 18.9 us  [the longest x2 18.3 us: expert_terms(): pl.pallas_call(functools.partial(expert_kernel, layouts, per_group, token...]
    pallas_call x1, Pallas kernels: 4 us -> 6.97 us  [project_attention(): pl.pallas_call(functools.partial(near_kernel, nseq), out_shape=[jax.Shape...]
    pallas_call x1, Pallas kernels: 0.24 us -> 2.91 us  [pack(): pl.pallas_call(functools.partial(pack_kernel, nseq), out_shape=shapes, in...]
    unnamed x60 -> x40, local copies, waits for them, and re-layouts: 7.85 us -> 6.65 us
  transfers between devices with their start and end apart: 49 -> 41, of which waited for: 25 -> 20; matrix products, arithmetic and copies ran while one was open for 4% -> 1% of each run, Pallas kernels for 2% -> 22%
where the time goes in v2:
time: 159 us
  waiting for transfers between devices  61.9 us (39%)
  starting transfers between devices  48.2 us (30%)
  Pallas kernels  38.3 us (24%)
  local copies, waits for them, and re-layouts  6.65 us (4%)
  other arithmetic  2.8 us (2%)
    ppermute x41, waiting for transfers between devices, swap(): lax.ppermute(rows, axis, [(i, i ^ bits) for i in range(lax.axis_size(axis...  61.9 us
    ppermute x41, starting transfers between devices, swap(): lax.ppermute(rows, axis, [(i, i ^ bits) for i in range(lax.axis_size(axis...  48.2 us
    pallas_call x2, Pallas kernels, expert_terms(): pl.pallas_call(functools.partial(expert_kernel, layouts, per_group, token...  18.3 us
    pallas_call x1, Pallas kernels, project_attention(): pl.pallas_call(functools.partial(far_kernel, nseq), out_shape=[jax.ShapeD...  9.54 us
    pallas_call x1, Pallas kernels, project_attention(): pl.pallas_call(functools.partial(near_kernel, nseq), out_shape=[jax.Shape...  6.97 us
    unnamed x40, local copies, waits for them, and re-layouts  6.65 us
  transfers between devices with their start and end apart: 41, of which 20 were waited for; matrix products, arithmetic and copies ran while one was open for 1% of the time, Pallas kernels for 22%

profile of v2, /device:TPU:0, one launch (start us, length us, event | category | flops | bytes accessed | tf_op | source)
XLA Modules:
  0.0 158.9 jit_solution(18316985363625879708)
XLA Ops:
  0.0 2.9 %pack_heads.1 = (bf16[64,1280]{1,0:T(8,128)(2,1)}, bf16[64,1280]{1,0:T(8,128)(2,1)}, bf16[64,1280]{1,0:T(8,128)(2,1)}, bf16[64,1280]{1,0:T(8,128)(2,1)}, bf16[51...) custom-call(s32[1]{0:T(128)} %bitcast.1.me_ref, ...), custom_call_target="tpu_custom_call" | custom-call | tf_op jit(solution)/shard_map/pack_heads/pallas_call | solution.py:63
  3.4 2.6 %collective-permute-start.1 = (bf16[64,1280]{1,0:T(8,128)(2,1)}, bf16[64,1280]{1,0:T(8,128)(2,1)S(1)}, u32[]{:S(2)}, u32[]{:S(2)}) collective-permute-start(bf16[64,1280]{1,0:T(8,128)(2,1)} %get-tuple-element.62), channel_id=1, source_target_pairs={{0,16},{8,24},{16,0},{24,8},{1,17},{9,25},{17,1},{25,9},{2,18},{10... | collective-permute-start | bytes 491528 | tf_op jit(solution)/shard_map/ppermute | solution.py:30
  6.1 5.2 %collective-permute-done.1.refs_2_ = bf16[64,1280]{1,0:T(8,128)(2,1)S(1)} collective-permute-done((bf16[64,1280]{1,0:T(8,128)(2,1)}, bf16[64,1280]{1,0:T(8,128)(2,1)S(1)}, u32[]{:S(2)}, u32[]{:S(2)}) %collective-permute-start.1) | collective-permute-done | bytes 163872 | tf_op jit(solution)/shard_map/ppermute | solution.py:30
  11.3 3.0 %collective-permute-done.2.refs_3_ = bf16[64,1280]{1,0:T(8,128)(2,1)S(1)} collective-permute-done((bf16[64,1280]{1,0:T(8,128)(2,1)}, bf16[64,1280]{1,0:T(8,128)(2,1)S(1)}, u32[]{:S(2)}, u32[]{:S(2)}) %collective-permute-start.2) | collective-permute-done | bytes 163872 | tf_op jit(solution)/shard_map/ppermute | solution.py:30
  17.3 3.6 %collective-permute-done.5.refs_5_ = bf16[512,256]{1,0:T(8,128)(2,1)S(1)} collective-permute-done((bf16[512,256]{1,0:T(8,128)(2,1)}, bf16[512,256]{1,0:T(8,128)(2,1)S(1)}, u32[]{:S(2)}, u32[]{:S(2)}) %collective-permute-start.5) | collective-permute-done | bytes 262176 | tf_op jit(solution)/shard_map/ppermute | solution.py:30
  21.6 7.0 %attend_near.1 = (f32[256,128]{1,0:T(8,128)}, f32[256,128]{1,0:T(8,128)}, f32[256,1024]{1,0:T(8,128)}) custom-call(s32[1]{0:T(128)} %bitcast.1.me_ref, s32[1]{0:T(128)S(6)} %copy.15.len_ref, bf16[64,1280]{1,0:T(8,128)(2,1)} %get-tuple-element.64.refs_0_, bf16[64,1280]{1,0:T(8,128)(2,1)} %copy-done.14, bf16[64,1280]{1,0:T(8,128)(2,1)} %copy-done.15, ...), custom_call_target="tpu_custom_call" | custom-call | tf_op jit(solution)/shard_map/attend_near/pallas_call | solution.py:173
  29.5 9.5 %attend_far.1 = (f32[128,2048]{1,0:T(8,128)}, f32[64,2048]{1,0:T(8,128)}, f32[64,2048]{1,0:T(8,128)}) custom-call(s32[1]{0:T(128)} %bitcast.1.me_ref, s32[1]{0:T(128)S(6)} %copy.15.len_ref, bf16[64,1280]{1,0:T(8,128)(2,1)} %get-tuple-element.64.refs_0_, bf16[64,1280]{1,0:T(8,128)(2,1)} %copy-done.14, bf16[64,1280]{1,0:T(8,128)(2,1)} %copy-done.15, ...), custom_call_target="tpu_custom_call" | custom-call | tf_op jit(solution)/shard_map/attend_far/pallas_call | solution.py:186
  39.5 2.5 %collective-permute-done.8 = f32[128,2048]{1,0:T(8,128)S(1)} collective-permute-done((f32[128,2048]{1,0:T(8,128)}, f32[128,2048]{1,0:T(8,128)S(1)}, u32[]{:S(2)}, u32[]{:S(2)}) %collective-permute-start.8) | collective-permute-done | bytes 1048608 | tf_op jit(solution)/shard_map/ppermute | solution.py:30
  45.2 6.8 %collective-permute-done.9.refs_2_ = bf16[64,2048]{1,0:T(8,128)(2,1)S(1)} collective-permute-done((bf16[64,2048]{1,0:T(8,128)(2,1)S(1)}, bf16[64,2048]{1,0:T(8,128)(2,1)S(1)}, u32[]{:S(2)}, u32[]{:S(2)}) %collective-permute-start.9) | collective-permute-done | bytes 262176 | tf_op jit(solution)/shard_map/ppermute | solution.py:30
  57.7 2.6 %collective-permute-start.11 = (bf16[64,2176]{1,0:T(8,128)(2,1)S(1)}, bf16[64,2176]{1,0:T(8,128)(2,1)S(1)}, u32[]{:S(2)}, u32[]{:S(2)}) collective-permute-start(bf16[64,2176]{1,0:T(8,128)(2,1)S(1)} %get-tuple-element.90.refs_0_), channel_id=1, source_target_pairs={{0,4},{1,5},{2,6},{3,7},{4,0},{5,1},{6,2},{7,3},{8,12},{9,13},{10,... | collective-permute-start | bytes 835592 | tf_op jit(solution)/shard_map/ppermute | solution.py:30
  62.5 4.6 %collective-permute-done.18.refs_4_ = bf16[64,2176]{1,0:T(8,128)(2,1)} collective-permute-done((bf16[64,2176]{1,0:T(8,128)(2,1)S(1)}, bf16[64,2176]{1,0:T(8,128)(2,1)}, u32[]{:S(2)}, u32[]{:S(2)}) %collective-permute-start.18) | collective-permute-done | bytes 278560 | tf_op jit(solution)/shard_map/ppermute | solution.py:30
  69.1 2.9 %collective-permute-done.11.refs_0_ = bf16[64,2176]{1,0:T(8,128)(2,1)S(1)} collective-permute-done((bf16[64,2176]{1,0:T(8,128)(2,1)S(1)}, bf16[64,2176]{1,0:T(8,128)(2,1)S(1)}, u32[]{:S(2)}, u32[]{:S(2)}) %collective-permute-start.11) | collective-permute-done | bytes 278560 | tf_op jit(solution)/shard_map/ppermute | solution.py:30
  76.3 3.3 %collective-permute-start.21 = (bf16[64,2176]{1,0:T(8,128)(2,1)}, bf16[64,2176]{1,0:T(8,128)(2,1)}, u32[]{:S(2)}, u32[]{:S(2)}) collective-permute-start(bf16[64,2176]{1,0:T(8,128)(2,1)} %collective-permute-done.19.refs_5_), channel_id=1, source_target_pairs={{0,1},{1,0},{2,3},{3,2},{4,5},{5,4},{6,7},{7,6},{8,9},{9,8},{10,11... | collective-permute-start | bytes 835592 | tf_op jit(solution)/shard_map/ppermute | solution.py:30
  82.1 2.8 %collective-permute-start.14 = (bf16[64,2176]{1,0:T(8,128)(2,1)}, bf16[64,2176]{1,0:T(8,128)(2,1)S(1)}, u32[]{:S(2)}, u32[]{:S(2)}) collective-permute-start(bf16[64,2176]{1,0:T(8,128)(2,1)} %collective-permute-done.12.refs_4_), channel_id=1, source_target_pairs={{0,1},{1,0},{2,3},{3,2},{4,5},{5,4},{6,7},{7,6},{8,9},{9,8},{10,11... | collective-permute-start | bytes 835592 | tf_op jit(solution)/shard_map/ppermute | solution.py:30
  85.0 2.9 %collective-permute-done.28.refs_2_ = bf16[64,2176]{1,0:T(8,128)(2,1)} collective-permute-done((bf16[64,2176]{1,0:T(8,128)(2,1)S(1)}, bf16[64,2176]{1,0:T(8,128)(2,1)}, u32[]{:S(2)}, u32[]{:S(2)}) %collective-permute-start.28) | collective-permute-done | bytes 278560 | tf_op jit(solution)/shard_map/ppermute | solution.py:30
  89.4 3.7 %collective-permute-done.21.refs_7_ = bf16[64,2176]{1,0:T(8,128)(2,1)} collective-permute-done((bf16[64,2176]{1,0:T(8,128)(2,1)}, bf16[64,2176]{1,0:T(8,128)(2,1)}, u32[]{:S(2)}, u32[]{:S(2)}) %collective-permute-start.21) | collective-permute-done | bytes 278560 | tf_op jit(solution)/shard_map/ppermute | solution.py:30
  95.0 9.2 %experts.2 = (bf16[128,2048]{1,0:T(8,128)(2,1)S(1)}, bf16[128,2048]{1,0:T(8,128)(2,1)S(1)}, bf16[128,2048]{1,0:T(8,128)(2,1)S(1)}, bf16[128,2048]{1,0:T(8,128)(2,1)S(1)}) custom-call(s32[2]{0:T(128)S(1)} %pad_add_fusion.mine_ref, bf16[64,2176]{1,0:T(8,128)(2,1)S(1)} %copy-done.5, bf16[64,2176]{1,0:T(8,128)(2,1)S(1)} %copy-done.7, ...), custom_call_target="tpu_custom_call" | custom-call | flops 3623878656 | bytes 3145728 | tf_op jit(solution)/shard_map/experts/pallas_call | solution.py:408
  107.8 4.5 %collective-permute-done.30.refs_7_ = bf16[64,2176]{1,0:T(8,128)(2,1)S(1)} collective-permute-done((bf16[64,2176]{1,0:T(8,128)(2,1)S(1)}, bf16[64,2176]{1,0:T(8,128)(2,1)S(1)}, u32[]{:S(2)}, u32[]{:S(2)}) %collective-permute-start.30) | collective-permute-done | bytes 278560 | tf_op jit(solution)/shard_map/ppermute | solution.py:30
  112.3 9.1 %experts.3 = (bf16[64,2048]{1,0:T(8,128)(2,1)S(1)}, bf16[64,2048]{1,0:T(8,128)(2,1)S(1)}, bf16[64,2048]{1,0:T(8,128)(2,1)S(1)}, bf16[64,2048]{1,0:T(8,128)(2,1)S...) custom-call(s32[2]{0:T(128)S(1)} %pad_add_fusion.mine_ref, ...), custom_call_target="tpu_custom_call" | custom-call | flops 3623878656 | bytes 3145728 | tf_op jit(solution)/shard_map/experts/pallas_call | solution.py:408
  136.5 2.4 %collective-permute-done.36 = bf16[32,2048]{1,0:T(8,128)(2,1)S(1)} collective-permute-done((bf16[32,2048]{1,0:T(8,128)(2,1)S(1)}, bf16[32,2048]{1,0:T(8,128)(2,1)S(1)}, u32[]{:S(2)}, u32[]{:S(2)}) %collective-permute-start.36) | collective-permute-done | bytes 131104 | tf_op jit(solution)/shard_map/ppermute | solution.py:30
  140.7 3.2 %collective-permute-done.34 = bf16[32,2048]{1,0:T(8,128)(2,1)S(1)} collective-permute-done((bf16[32,2048]{1,0:T(8,128)(2,1)S(1)}, bf16[32,2048]{1,0:T(8,128)(2,1)S(1)}, u32[]{:S(2)}, u32[]{:S(2)}) %collective-permute-start.34) | collective-permute-done | bytes 131104 | tf_op jit(solution)/shard_map/ppermute | solution.py:30
  144.2 3.2 %collective-permute-done.39 = bf16[64,2048]{1,0:T(8,128)(2,1)S(1)} collective-permute-done((bf16[64,2048]{1,0:T(8,128)(2,1)S(1)}, bf16[64,2048]{1,0:T(8,128)(2,1)S(1)}, u32[]{:S(2)}, u32[]{:S(2)}) %collective-permute-start.39) | collective-permute-done | bytes 262176 | tf_op jit(solution)/shard_map/ppermute | solution.py:30
  147.4 3.4 %collective-permute-start.40 = (bf16[64,2048]{1,0:T(8,128)(2,1)S(1)}, bf16[64,2048]{1,0:T(8,128)(2,1)S(1)}, u32[]{:S(2)}, u32[]{:S(2)}) collective-permute-start(bf16[64,2048]{1,0:T(8,128)(2,1)S(1)} %fusion), channel_id=1, source_target_pairs={{0,4},{1,5},{2,6},{3,7},{4,0},{5,1},{6,2},{7,3},{8,12},{9,13},{10,... | collective-permute-start | bytes 786440 | tf_op jit(solution)/shard_map/ppermute | solution.py:30
  150.8 7.2 %collective-permute-done.40 = bf16[64,2048]{1,0:T(8,128)(2,1)S(1)} collective-permute-done((bf16[64,2048]{1,0:T(8,128)(2,1)S(1)}, bf16[64,2048]{1,0:T(8,128)(2,1)S(1)}, u32[]{:S(2)}, u32[]{:S(2)}) %collective-permute-start.40) | collective-permute-done | bytes 262176 | tf_op jit(solution)/shard_map/ppermute | solution.py:30
  (120 shorter events, 50.0 us)
Async XLA Ops:
  14.3 24.8 %collective-permute-start.6 = (bf16[1,2048,768]{2,1,0:T(8,128)(2,1)}, bf16[1,2048,768]{2,1,0:T(8,128)(2,1)}, u32[]{:S(2)}, u32[]{:S(2)}) collective-permute-start(bf16[1,2048,768]{2,1,0:T(8,128)(2,1)} %refs_8_.1), channel_id=1, source_target_pairs={{0,8},{8,0},{16,24},{24,16},{1,9},{9,1},{17,25},{25,17},{2,10},{10... | collective-permute-start | bytes 9437192 | tf_op jit(solution)/shard_map/ppermute | solution.py:30
  14.4 24.7 %collective-permute-start.7 = (bf16[1,2048,768]{2,1,0:T(8,128)(2,1)}, bf16[1,2048,768]{2,1,0:T(8,128)(2,1)}, u32[]{:S(2)}, u32[]{:S(2)}) collective-permute-start(bf16[1,2048,768]{2,1,0:T(8,128)(2,1)} %refs_9_.3), channel_id=1, source_target_pairs={{0,8},{8,0},{16,24},{24,16},{1,9},{9,1},{17,25},{25,17},{2,10},{10... | collective-permute-start | bytes 9437192 | tf_op jit(solution)/shard_map/ppermute | solution.py:30
  14.9 13.7 %collective-permute-start.3 = (bf16[512,256]{1,0:T(8,128)(2,1)}, bf16[512,256]{1,0:T(8,128)(2,1)S(1)}, u32[]{:S(2)}, u32[]{:S(2)}) collective-permute-start(bf16[512,256]{1,0:T(8,128)(2,1)} %get-tuple-element.68), channel_id=1, source_target_pairs={{0,16},{8,24},{16,0},{24,8},{1,17},{9,25},{17,1},{25,9},{2,18},{10... | collective-permute-start | bytes 786440 | tf_op jit(solution)/shard_map/ppermute | solution.py:30
  16.6 12.2 %collective-permute-start.4 = (bf16[512,256]{1,0:T(8,128)(2,1)}, bf16[512,256]{1,0:T(8,128)(2,1)S(1)}, u32[]{:S(2)}, u32[]{:S(2)}) collective-permute-start(bf16[512,256]{1,0:T(8,128)(2,1)} %get-tuple-element.69), channel_id=1, source_target_pairs={{0,24},{8,16},{16,8},{24,0},{1,25},{9,17},{17,9},{25,1},{2,26},{10... | collective-permute-start | bytes 786440 | tf_op jit(solution)/shard_map/ppermute | solution.py:30
  42.0 12.5 %collective-permute-start.10 = (bf16[1,768,2048]{2,1,0:T(8,128)(2,1)S(1)}, bf16[1,768,2048]{2,1,0:T(8,128)(2,1)S(1)}, u32[]{:S(2)}, u32[]{:S(2)}) collective-permute-start(bf16[1,768,2048]{2,1,0:T(8,128)(2,1)S(1)} %copy-done.12), channel_id=1, source_target_pairs={{0,8},{8,0},{16,24},{24,16},{1,9},{9,1},{17,25},{25,17},{2,10},{10... | collective-permute-start | bytes 9437192 | tf_op jit(solution)/shard_map/ppermute | solution.py:30
  54.5 12.6 %collective-permute-start.18 = (bf16[64,2176]{1,0:T(8,128)(2,1)S(1)}, bf16[64,2176]{1,0:T(8,128)(2,1)}, u32[]{:S(2)}, u32[]{:S(2)}) collective-permute-start(bf16[64,2176]{1,0:T(8,128)(2,1)S(1)} %get-tuple-element.90.refs_0_), channel_id=1, source_target_pairs={{0,2},{1,3},{2,0},{3,1},{4,6},{5,7},{6,4},{7,5},{8,10},{9,11},{10,... | collective-permute-start | bytes 835592 | tf_op jit(solution)/shard_map/ppermute | solution.py:30
  56.1 12.5 %collective-permute-start.16 = (bf16[64,2176]{1,0:T(8,128)(2,1)S(1)}, bf16[64,2176]{1,0:T(8,128)(2,1)}, u32[]{:S(2)}, u32[]{:S(2)}) collective-permute-start(bf16[64,2176]{1,0:T(8,128)(2,1)S(1)} %get-tuple-element.90.refs_0_), channel_id=1, source_target_pairs={{0,1},{1,0},{2,3},{3,2},{4,5},{5,4},{6,7},{7,6},{8,9},{9,8},{10,11... | collective-permute-start | bytes 835592 | tf_op jit(solution)/shard_map/ppermute | solution.py:30
  57.7 14.3 %collective-permute-start.11 = (bf16[64,2176]{1,0:T(8,128)(2,1)S(1)}, bf16[64,2176]{1,0:T(8,128)(2,1)S(1)}, u32[]{:S(2)}, u32[]{:S(2)}) collective-permute-start(bf16[64,2176]{1,0:T(8,128)(2,1)S(1)} %get-tuple-element.90.refs_0_), channel_id=1, source_target_pairs={{0,4},{1,5},{2,6},{3,7},{4,0},{5,1},{6,2},{7,3},{8,12},{9,13},{10,... | collective-permute-start | bytes 835592 | tf_op jit(solution)/shard_map/ppermute | solution.py:30
  60.3 12.4 %collective-permute-start.15 = (bf16[64,2176]{1,0:T(8,128)(2,1)S(1)}, bf16[64,2176]{1,0:T(8,128)(2,1)S(1)}, u32[]{:S(2)}, u32[]{:S(2)}) collective-permute-start(bf16[64,2176]{1,0:T(8,128)(2,1)S(1)} %get-tuple-element.90.refs_0_), channel_id=1, source_target_pairs={{0,16},{8,24},{16,0},{24,8},{1,17},{9,25},{17,1},{25,9},{2,18},{10... | collective-permute-start | bytes 835592 | tf_op jit(solution)/shard_map/ppermute | solution.py:30
  68.7 11.4 %collective-permute-start.17 = (bf16[64,2176]{1,0:T(8,128)(2,1)}, bf16[64,2176]{1,0:T(8,128)(2,1)}, u32[]{:S(2)}, u32[]{:S(2)}) collective-permute-start(bf16[64,2176]{1,0:T(8,128)(2,1)} %collective-permute-done.16.refs_2_), channel_id=1, source_target_pairs={{0,16},{8,24},{16,0},{24,8},{1,17},{9,25},{17,1},{25,9},{2,18},{10... | collective-permute-start | bytes 835592 | tf_op jit(solution)/shard_map/ppermute | solution.py:30
  72.0 9.7 %collective-permute-start.12 = (bf16[64,2176]{1,0:T(8,128)(2,1)S(1)}, bf16[64,2176]{1,0:T(8,128)(2,1)}, u32[]{:S(2)}, u32[]{:S(2)}) collective-permute-start(bf16[64,2176]{1,0:T(8,128)(2,1)S(1)} %collective-permute-done.11.refs_0_), channel_id=1, source_target_pairs={{0,2},{1,3},{2,0},{3,1},{4,6},{5,7},{6,4},{7,5},{8,10},{9,11},{10,... | collective-permute-start | bytes 835592 | tf_op jit(solution)/shard_map/ppermute | solution.py:30
  72.0 10.1 %collective-permute-start.20 = (bf16[64,2176]{1,0:T(8,128)(2,1)}, bf16[64,2176]{1,0:T(8,128)(2,1)}, u32[]{:S(2)}, u32[]{:S(2)}) collective-permute-start(bf16[64,2176]{1,0:T(8,128)(2,1)} %collective-permute-done.18.refs_4_), channel_id=1, source_target_pairs={{0,1},{1,0},{2,3},{3,2},{4,5},{5,4},{6,7},{7,6},{8,9},{9,8},{10,11... | collective-permute-start | bytes 835592 | tf_op jit(solution)/shard_map/ppermute | solution.py:30
  73.3 14.5 %collective-permute-start.28 = (bf16[64,2176]{1,0:T(8,128)(2,1)S(1)}, bf16[64,2176]{1,0:T(8,128)(2,1)}, u32[]{:S(2)}, u32[]{:S(2)}) collective-permute-start(bf16[64,2176]{1,0:T(8,128)(2,1)S(1)} %collective-permute-done.11.refs_0_), channel_id=1, source_target_pairs={{0,1},{1,0},{2,3},{3,2},{4,5},{5,4},{6,7},{7,6},{8,9},{9,8},{10,11... | collective-permute-start | bytes 835592 | tf_op jit(solution)/shard_map/ppermute | solution.py:30
  76.3 16.7 %collective-permute-start.21 = (bf16[64,2176]{1,0:T(8,128)(2,1)}, bf16[64,2176]{1,0:T(8,128)(2,1)}, u32[]{:S(2)}, u32[]{:S(2)}) collective-permute-start(bf16[64,2176]{1,0:T(8,128)(2,1)} %collective-permute-done.19.refs_5_), channel_id=1, source_target_pairs={{0,1},{1,0},{2,3},{3,2},{4,5},{5,4},{6,7},{7,6},{8,9},{9,8},{10,11... | collective-permute-start | bytes 835592 | tf_op jit(solution)/shard_map/ppermute | solution.py:30
  80.1 27.7 %collective-permute-start.27 = (bf16[64,2176]{1,0:T(8,128)(2,1)S(1)}, bf16[64,2176]{1,0:T(8,128)(2,1)S(1)}, u32[]{:S(2)}, u32[]{:S(2)}) collective-permute-start(bf16[64,2176]{1,0:T(8,128)(2,1)S(1)} %collective-permute-done.11.refs_0_), channel_id=1, source_target_pairs={{0,16},{8,24},{16,0},{24,8},{1,17},{9,25},{17,1},{25,9},{2,18},{10... | collective-permute-start | bytes 835592 | tf_op jit(solution)/shard_map/ppermute | solution.py:30
  81.7 22.5 %collective-permute-start.13 = (bf16[64,2176]{1,0:T(8,128)(2,1)}, bf16[64,2176]{1,0:T(8,128)(2,1)S(1)}, u32[]{:S(2)}, u32[]{:S(2)}) collective-permute-start(bf16[64,2176]{1,0:T(8,128)(2,1)} %collective-permute-done.12.refs_4_), channel_id=1, source_target_pairs={{0,16},{8,24},{16,0},{24,8},{1,17},{9,25},{17,1},{25,9},{2,18},{10... | collective-permute-start | bytes 835592 | tf_op jit(solution)/shard_map/ppermute | solution.py:30
  82.1 22.0 %collective-permute-start.14 = (bf16[64,2176]{1,0:T(8,128)(2,1)}, bf16[64,2176]{1,0:T(8,128)(2,1)S(1)}, u32[]{:S(2)}, u32[]{:S(2)}) collective-permute-start(bf16[64,2176]{1,0:T(8,128)(2,1)} %collective-permute-done.12.refs_4_), channel_id=1, source_target_pairs={{0,1},{1,0},{2,3},{3,2},{4,5},{5,4},{6,7},{7,6},{8,9},{9,8},{10,11... | collective-permute-start | bytes 835592 | tf_op jit(solution)/shard_map/ppermute | solution.py:30
  87.9 19.9 %collective-permute-start.29 = (bf16[64,2176]{1,0:T(8,128)(2,1)}, bf16[64,2176]{1,0:T(8,128)(2,1)S(1)}, u32[]{:S(2)}, u32[]{:S(2)}) collective-permute-start(bf16[64,2176]{1,0:T(8,128)(2,1)} %collective-permute-done.28.refs_2_), channel_id=1, source_target_pairs={{0,16},{8,24},{16,0},{24,8},{1,17},{9,25},{17,1},{25,9},{2,18},{10... | collective-permute-start | bytes 835592 | tf_op jit(solution)/shard_map/ppermute | solution.py:30
  105.7 19.6 %collective-permute-start.22 = (bf16[128,2048]{1,0:T(8,128)(2,1)S(1)}, bf16[128,2048]{1,0:T(8,128)(2,1)S(1)}, u32[]{:S(2)}, u32[]{:S(2)}) collective-permute-start(bf16[128,2048]{1,0:T(8,128)(2,1)S(1)} %get-tuple-element.102), channel_id=1, source_target_pairs={{0,1},{1,0},{2,3},{3,2},{4,5},{5,4},{6,7},{7,6},{8,9},{9,8},{10,11... | collective-permute-start | bytes 1572872 | tf_op jit(solution)/shard_map/ppermute | solution.py:30
  106.3 19.3 %collective-permute-start.24 = (bf16[128,2048]{1,0:T(8,128)(2,1)S(1)}, bf16[128,2048]{1,0:T(8,128)(2,1)S(1)}, u32[]{:S(2)}, u32[]{:S(2)}) collective-permute-start(bf16[128,2048]{1,0:T(8,128)(2,1)S(1)} %get-tuple-element.104), channel_id=1, source_target_pairs={{0,16},{8,24},{16,0},{24,8},{1,17},{9,25},{17,1},{25,9},{2,18},{10... | collective-permute-start | bytes 1572872 | tf_op jit(solution)/shard_map/ppermute | solution.py:30
  125.2 9.5 %collective-permute-start.33 = (bf16[64,2048]{1,0:T(8,128)(2,1)S(1)}, bf16[64,2048]{1,0:T(8,128)(2,1)S(1)}, u32[]{:S(2)}, u32[]{:S(2)}) collective-permute-start(bf16[64,2048]{1,0:T(8,128)(2,1)S(1)} %get-tuple-element.110), channel_id=1, source_target_pairs={{0,1},{1,0},{2,3},{3,2},{4,5},{5,4},{6,7},{7,6},{8,9},{9,8},{10,11... | collective-permute-start | bytes 786440 | tf_op jit(solution)/shard_map/ppermute | solution.py:30
  125.6 25.2 %collective-permute-start.23 = (bf16[64,2048]{1,0:T(8,128)(2,1)S(1)}, bf16[64,2048]{1,0:T(8,128)(2,1)S(1)}, u32[]{:S(2)}, u32[]{:S(2)}) collective-permute-start(bf16[64,2048]{1,0:T(8,128)(2,1)S(1)} %add_convert_fusion.3), channel_id=1, source_target_pairs={{0,16},{8,24},{16,0},{24,8},{1,17},{9,25},{17,1},{25,9},{2,18},{10... | collective-permute-start | bytes 786440 | tf_op jit(solution)/shard_map/ppermute | solution.py:30
  128.9 15.1 %collective-permute-start.25 = (bf16[64,2048]{1,0:T(8,128)(2,1)S(1)}, bf16[64,2048]{1,0:T(8,128)(2,1)S(1)}, u32[]{:S(2)}, u32[]{:S(2)}) collective-permute-start(bf16[64,2048]{1,0:T(8,128)(2,1)S(1)} %add_convert_fusion.2), channel_id=1, source_target_pairs={{0,1},{1,0},{2,3},{3,2},{4,5},{5,4},{6,7},{7,6},{8,9},{9,8},{10,11... | collective-permute-start | bytes 786440 | tf_op jit(solution)/shard_map/ppermute | solution.py:30
  147.4 10.5 %collective-permute-start.40 = (bf16[64,2048]{1,0:T(8,128)(2,1)S(1)}, bf16[64,2048]{1,0:T(8,128)(2,1)S(1)}, u32[]{:S(2)}, u32[]{:S(2)}) collective-permute-start(bf16[64,2048]{1,0:T(8,128)(2,1)S(1)} %fusion), channel_id=1, source_target_pairs={{0,4},{1,5},{2,6},{3,7},{4,0},{5,1},{6,2},{7,3},{8,12},{9,13},{10,... | collective-permute-start | bytes 786440 | tf_op jit(solution)/shard_map/ppermute | solution.py:30
  (37 other events, 359.2 us)

commit v3 on v2

--- a/solution.py
+++ b/solution.py
@@ -14,8 +14,11 @@
 TOPK = 8
 MASKED = -1e30
 EXPERT_MIB = 46
-NEAR_MIB = 58
-FAR_MIB = 54
+CLOSE = 0
+CALL = 4
+NEAR_MIB = 14
+FAR_MIB = 14
+NORM_MIB = 16
 EXP2_SCALE = math.log2(math.e) / math.sqrt(HD)
 NT = (((1,), (1,)), ((), ()))
 TN = (((0,), (0,)), ((), ()))
@@ -86,7 +89,7 @@
 
 def near_kernel(nseq, me_ref, len_ref, *refs):
     heads, caches = refs[:nseq], refs[nseq : nseq + 2]
-    peak_ref, sum_ref, acc_ref = refs[nseq + 2 :]
+    peak_ref, sum_ref, acc_ref = refs[nseq + 3 :]
     group = QH // nseq
     qcols = group * HD
     me = me_ref[0]
@@ -117,11 +120,9 @@
 
 def far_kernel(nseq, me_ref, len_ref, *refs):
     heads, caches = refs[:nseq], refs[nseq : 2 * nseq - 2]
-    peak_ref, sum_ref, acc_ref, w_hbm = refs[2 * nseq - 2 : 2 * nseq + 2]
-    outs = refs[2 * nseq + 2 : -3]
-    attn_ref, w_ref, sem = refs[-3:]
-    load = pltpu.make_async_copy(w_hbm, w_ref, sem)
-    load.start()
+    peak_ref, sum_ref, acc_ref, w_ref = refs[2 * nseq - 2 : 2 * nseq + 2]
+    outs = refs[2 * nseq + 2 : -1]
+    attn_ref = refs[-1]
     group = QH // nseq
     slots, tokens = caches[0].shape[0], heads[0].shape[0]
     bias = slot_bias(me_ref[0], len_ref[0], range(2, nseq), slots)
@@ -138,7 +139,6 @@
         total = sum_ref[:, g : g + 1] * fade + jnp.sum(p, axis=1, keepdims=True)
         acc = acc_ref[:, at] * fade + jnp.dot(p.astype(bf16), vals, preferred_element_type=f32)
         attn_ref[:, at] = (acc / total).astype(bf16)
-    load.wait()
     send, near, far = outs
     places = []
     for k in range(nseq):
@@ -165,9 +165,13 @@
     heads, caches = pack(me, (queries, new_keys, new_values, cache_keys, cache_values), nseq)
     order = sorted(range(1, nseq), reverse=True)
     heads = {0: heads[0]} | {k: swap(heads[k], "seq", k) for k in order}
-    caches = {0: caches[0]} | {k: swap(caches[k], "seq", k) for k in order}
-    heads, weights = lax.optimization_barrier((heads, weights))
     others = [swap(w, "seq", 1) for w in weights[:2]]
+    caches = {0: caches[0], 1: swap(caches[1], "seq", 1)} | dict(enumerate(caches[2:], 2))
+    far_heads = [heads[k] for k in range(2, nseq)]
+    far_caches = [caches[k] for k in range(2, nseq)]
+    far_heads, far_caches, others = lax.optimization_barrier((far_heads, far_caches, others))
+    for k in range(2, nseq):
+        heads[k], caches[k] = far_heads[k - 2], swap(far_caches[k - 2], "seq", k)
     heads = [heads[k] for k in range(nseq)]
     caches = [caches[k] for k in range(nseq)]
     state = pl.pallas_call(
@@ -177,11 +181,11 @@
             jax.ShapeDtypeStruct((qtok, HD), f32),
             jax.ShapeDtypeStruct((qtok, group * HD), f32),
         ],
-        in_specs=[SMEM] * 2 + [VMEM] * (nseq + 2),
+        in_specs=[SMEM] * 2 + [VMEM] * (nseq + 3),
         out_specs=[VMEM] * 3,
         compiler_params=params(NEAR_MIB),
         name="attend_near",
-    )(me, length, *heads, *caches[:2])
+    )(me, length, *heads, *caches[:2], out_weight)
     half = nseq // 2 * tokens
     parts = pl.pallas_call(
         functools.partial(far_kernel, nseq),
@@ -190,21 +194,16 @@
             jax.ShapeDtypeStruct((tokens, width), f32),
             jax.ShapeDtypeStruct((half - tokens, width), f32),
         ],
-        in_specs=[SMEM] * 2 + [VMEM] * (2 * nseq + 1) + [ANY],
+        in_specs=[SMEM] * 2 + [VMEM] * (2 * nseq + 2),
         out_specs=[VMEM] * 3,
-        scratch_shapes=[
-            pltpu.VMEM((qtok, group * HD), bf16),
-            pltpu.VMEM(out_weight.shape, bf16),
-            pltpu.SemaphoreType.DMA,
-        ],
+        scratch_shapes=[pltpu.VMEM((qtok, group * HD), bf16)],
         compiler_params=params(FAR_MIB),
         name="attend_far",
     )(me, length, *heads, *caches[2:], *state, out_weight)
-    (send, near, far), others = lax.optimization_barrier((parts, others))
+    send, near, far = parts
     got = swap(send, "seq", 1)
-    if weights:
-        got, last = lax.optimization_barrier((got, weights[2]))
-        others.append(swap(last, "seq", 1))
+    got, rest = lax.optimization_barrier((got, weights[2:]))
+    others += [swap(w, "seq", 1) for w in rest]
     terms = [near, got[:tokens]]
     for at in range(tokens, half, tokens):
         both = far[at - tokens : at] + got[at : at + tokens]
@@ -251,45 +250,53 @@
         ],
         in_specs=[VMEM] * (4 + len(terms)),
         out_specs=[VMEM] * 2,
-        compiler_params=params(16),
+        compiler_params=params(NORM_MIB),
         name="norm_and_route",
     )(residual, *terms, gain.reshape(1, width), router.T, ids.T)
 
 
-def gather_plane(col, kz, sides, first=None):
-    right = [swap(col, "seq", 2 * kx) for kx in range(1, sides)]
-    up = swap(col, "exp", 1)
-    if first:
-        right, up, first = lax.optimization_barrier((right, up, first))
-    if kz % 2:
-        over = [swap(r, "exp", 1) for r in right]
-    else:
-        over = [swap(up, "seq", 2 * kx) for kx in range(1, sides)]
-    return [col, *right, up, *over], first
-
-
-def plane_layout(mode, sides, tokens):
+def gather_rows(rows, weights, planes, sides):
+    columns = [rows]
+    for kz in range(1, planes):
+        odd = kz > 1 and kz % 2
+        columns.append(swap(columns[kz - 1], "exp", 2) if odd else swap(rows, "exp", 2 * kz))
+        if kz == CLOSE:
+            columns[kz], weights = lax.optimization_barrier((columns[kz], weights))
+    blocks = []
+    for kz, col in enumerate(columns):
+        right = [swap(col, "seq", 2 * kx) for kx in range(1, sides)]
+        up = swap(col, "exp", 1)
+        if kz % 2:
+            over = [swap(block, "exp", 2) for block in blocks[-1][sides + 1 :]]
+        elif kz % 4:
+            over = [swap(block, "exp", 1) for block in right]
+        else:
+            over = [swap(up, "seq", 2 * kx) for kx in range(1, sides)]
+        blocks.append([col, *right, up, *over])
+    return blocks, weights
+
+
+def plane_layout(odd, sides, tokens):
     half = tokens // 2
-    rows, moves = [], []
-    if mode == "halves":
-        rows = [2 * half, sides * half, (sides - 1) * 2 * half, sides * half]
+    moves = []
+    if odd:
+        rows = [tokens, (sides - 1) * tokens, tokens, (sides - 1) * tokens]
         for ky in range(2):
             for kx in range(sides):
-                row = (ky * sides + kx) * tokens
-                top = (2, ((kx - 1) * 2 + ky) * half) if kx else (0, ky * half)
-                moves.append((row, half, *top))
-                moves.append((row + half, half, 3 if ky else 1, kx * half))
-    elif mode == "x":
-        rows = [2 * tokens, (sides - 1) * 2 * tokens]
-        for ky in range(2):
-            for kx in range(sides):
-                to = (1, ((kx - 1) * 2 + ky) * tokens) if kx else (0, ky * tokens)
+                to = (2 * ky + (kx > 0), max(kx - 1, 0) * tokens)
                 moves.append(((ky * sides + kx) * tokens, tokens, *to))
-    else:
-        rows = [sides * tokens, sides * tokens]
-        for ky in range(2):
-            for kx in range(sides):
-                moves.append(((ky * sides + kx) * tokens, tokens, ky, kx * tokens))
+        return rows, moves
+    rows = [2 * half, sides * half, (sides - 1) * half, half, (sides - 1) * tokens]
+    for ky in range(2):
+        for kx in range(sides):
+            row = (ky * sides + kx) * tokens
+            if ky and kx:
+                moves.append((row, tokens, 4, (kx - 1) * tokens))
+                continue
+            top = (2, (kx - 1) * half) if kx else (0, ky * half)
+            low = (3, 0) if ky else (1, kx * half)
+            moves.append((row, half, *top))
+            moves.append((row + half, half, *low))
     return rows, moves
 
 
@@ -397,13 +404,13 @@
         first += len(rows)
 
 
-def expert_terms(blocks, modes, sides, mine, weights, cap, nexp):
+def expert_terms(blocks, sides, mine, weights, cap, nexp):
     planes, per_group = len(blocks), len(blocks[0])
     tokens, wide = blocks[0][0].shape
     _, width, hidden = weights[0].shape
     grows = per_group * cap
     rows = planes * grows
-    layouts = [plane_layout(mode, sides, tokens) for mode in modes]
+    layouts = [plane_layout(g % 2, sides, tokens) for g in range(planes)]
     out_shape = [jax.ShapeDtypeStruct((n, width), bf16) for ns, _ in layouts for n in ns]
     outs = pl.pallas_call(
         functools.partial(expert_kernel, layouts, per_group, tokens, cap, nexp),
@@ -440,37 +447,43 @@
     return total
 
 
-def plane_sum(term, mode, sides):
-    if mode == "halves":
-        top = plane_sum(term[::2], "x", sides)
-        low = plane_sum(term[1::2], "y", sides)
-        return jnp.concatenate([top, low], 0)
-    keep, send = term
-    if mode == "x":
-        size = keep.shape[0] // 2
-        got = [swap(send[i * 2 * size : (i + 1) * 2 * size], "seq", 2 * i + 2) for i in range(sides - 1)]
-        last = swap(add(keep[size:], *[g[size:] for g in got]).astype(bf16), "exp", 1)
-        return add(keep[:size], *[g[:size] for g in got], last)
-    size = keep.shape[0] // sides
-    got = swap(send, "exp", 1)
-    last = []
+def even_sum(term, over, sides):
+    keep_a, keep_b, send_a, send_b, own_over = term
+    half = send_b.shape[0]
+    over = [
+        add(own_over[i * 2 * half : (i + 1) * 2 * half], o).astype(bf16) for i, o in enumerate(over)
+    ]
+    got_a = [
+        swap(jnp.concatenate([send_a[i * half : (i + 1) * half], o[:half]], 0), "seq", 2 * i + 2)
+        for i, o in enumerate(over)
+    ]
+    got_b = swap(jnp.concatenate([send_b, *[o[half:] for o in over]], 0), "exp", 1)
+    next_a = swap(add(keep_a[half:], *[g[half:] for g in got_a]).astype(bf16), "exp", 1)
+    next_b = []
     for kx in range(1, sides):
-        at = slice(kx * size, (kx + 1) * size)
-        last.append(swap(add(keep[at], got[at]).astype(bf16), "seq", 2 * kx))
-    return add(keep[:size], got[:size], *last)
-
-
-def return_terms(terms, modes, sides):
-    sums = [None] * len(terms)
-    for kz in reversed(range(len(terms))):
-        sums[kz] = plane_sum(terms[kz], modes[kz], sides)
-    own = [sums[0]]
-    for kz in range(1, len(terms)):
-        if kz == 1 or kz % 2 == 0:
-            part = sums[kz]
-            if kz > 1 and kz + 1 < len(terms):
-                part = add(part, swap(sums[kz + 1].astype(bf16), "exp", 2))
-            own.append(swap(part.astype(bf16), "exp", 2 * kz))
+        at = slice(kx * half, (kx + 1) * half)
+        next_b.append(swap(add(keep_b[at], got_b[at]).astype(bf16), "seq", 2 * kx))
+    top = add(keep_a[:half], *[g[:half] for g in got_a], next_a)
+    low = add(keep_b[:half], got_b[:half], *next_b)
+    return jnp.concatenate([top, low], 0)
+
+
+def pair_sum(even, odd, sides):
+    keep, right, up, over = odd
+    size = keep.shape[0]
+    parts = [slice(i * size, (i + 1) * size) for i in range(sides - 1)]
+    over = [swap(over[at], "exp", 2) for at in parts]
+    got = [swap(right[at], "seq", 2 * i + 2) for i, at in enumerate(parts)]
+    got.append(swap(up, "exp", 1))
+    return even_sum(even, over, sides), add(keep, *got)
+
+
+def return_terms(terms, sides):
+    own = []
+    for kz in reversed(range(0, len(terms), 2)):
+        even, odd = pair_sum(terms[kz], terms[kz + 1], sides)
+        got = swap(odd.astype(bf16), "exp", 2)
+        own += [swap(add(even, got).astype(bf16), "exp", 2 * kz)] if kz else [even, got]
     return own
 
 
@@ -481,18 +494,11 @@
     me = lax.axis_index("seq") * nplace + lax.axis_index("exp")
     other = (lax.axis_index("seq") ^ 1) * nplace + lax.axis_index("exp")
     mine = jnp.stack([me, other]).astype(jnp.int32)
-    columns = [rows]
-    for kz in range(1, planes):
-        odd = kz > 1 and kz % 2
-        columns.append(swap(columns[kz - 1], "exp", 2) if odd else swap(rows, "exp", 2 * kz))
-    modes = ["y", "x"] + ["halves"] * (planes - 2)
+    blocks, weights = gather_rows(rows, weights, planes, sides)
     terms = []
-    for at in range(0, planes, 2):
-        even, _ = gather_plane(columns[at], at, sides)
-        odd, terms = gather_plane(columns[at + 1], at + 1, sides, terms)
-        two = modes[at : at + 2]
-        terms = [*terms, *expert_terms([even, odd], two, sides, mine, weights, cap, nexp)]
-    return return_terms(terms, modes, sides)
+    for at in range(0, planes, CALL):
+        terms += expert_terms(blocks[at : at + CALL], sides, mine, weights, cap, nexp)
+    return return_terms(terms, sides)
 
 
 def experts_by_device(rows, width, ids, gate_proj, up_proj, down_proj, nexp):

time: 159 us -> 150 us (0.943)
  Pallas kernels: 38.3 us -> 28.4 us
  starting transfers between devices: 48.2 us -> 52.1 us
  local copies, waits for them, and re-layouts: 6.65 us -> 4.12 us
    pallas_call x2 -> x1, Pallas kernels: 18.3 us -> 13.6 us  [expert_terms(): pl.pallas_call(functools.partial(expert_kernel, layouts, per_group, token...]
    ppermute x41 -> x43, starting transfers between devices: 48.2 us -> 52.1 us  [swap(): lax.ppermute(rows, axis, [(i, i ^ bits) for i in range(lax.axis_size(axis...]
    pallas_call x1, Pallas kernels: 9.54 us -> 6.54 us  [project_attention(): pl.pallas_call(functools.partial(far_kernel, nseq), out_shape=[jax.ShapeD...]
    unnamed x40 -> x20, local copies, waits for them, and re-layouts: 6.65 us -> 4.09 us
    pallas_call x1, Pallas kernels: 6.97 us -> 4.74 us  [project_attention(): pl.pallas_call(functools.partial(near_kernel, nseq), out_shape=[jax.Shape...]
    ppermute x41 -> x43, waiting for transfers between devices: 61.9 us -> 62.3 us  [swap(): lax.ppermute(rows, axis, [(i, i ^ bits) for i in range(lax.axis_size(axis...]
  transfers between devices with their start and end apart: 41 -> 43, of which waited for: 20 -> 19; matrix products, arithmetic and copies ran while one was open for 1% -> 1% of each run, Pallas kernels for 22% -> 6%
where the time goes in v3:
time: 150 us
  waiting for transfers between devices  62.3 us (42%)
  starting transfers between devices  52.1 us (35%)
  Pallas kernels  28.4 us (19%)
  local copies, waits for them, and re-layouts  4.12 us (3%)
  other arithmetic  1.81 us (1%)
    ppermute x43, waiting for transfers between devices, swap(): lax.ppermute(rows, axis, [(i, i ^ bits) for i in range(lax.axis_size(axis...  62.3 us
    ppermute x43, starting transfers between devices, swap(): lax.ppermute(rows, axis, [(i, i ^ bits) for i in range(lax.axis_size(axis...  52.1 us
    pallas_call x1, Pallas kernels, expert_terms(): pl.pallas_call(functools.partial(expert_kernel, layouts, per_group, token...  13.6 us
    pallas_call x1, Pallas kernels, project_attention(): pl.pallas_call(functools.partial(far_kernel, nseq), out_shape=[jax.ShapeD...  6.54 us
    pallas_call x1, Pallas kernels, project_attention(): pl.pallas_call(functools.partial(near_kernel, nseq), out_shape=[jax.Shape...  4.74 us
    unnamed x20, local copies, waits for them, and re-layouts  4.09 us
  transfers between devices with their start and end apart: 43, of which 19 were waited for; matrix products, arithmetic and copies ran while one was open for 1% of the time, Pallas kernels for 6%

profile of v3, /device:TPU:0, one launch (start us, length us, event | category | flops | bytes accessed | tf_op | source)
XLA Modules:
  0.0 149.6 jit_solution(8973738937696856242)
XLA Ops:
  0.5 2.9 %pack_heads.1 = (bf16[64,1280]{1,0:T(8,128)(2,1)}, bf16[64,1280]{1,0:T(8,128)(2,1)}, bf16[64,1280]{1,0:T(8,128)(2,1)}, bf16[64,1280]{1,0:T(8,128)(2,1)}, bf16[51...) custom-call(s32[1]{0:T(128)} %bitcast.1.me_ref, ...), custom_call_target="tpu_custom_call" | custom-call | tf_op jit(solution)/shard_map/pack_heads/pallas_call | solution.py:66
  3.4 3.0 %collective-permute-start.1 = (bf16[64,1280]{1,0:T(8,128)(2,1)}, bf16[64,1280]{1,0:T(8,128)(2,1)S(1)}, u32[]{:S(2)}, u32[]{:S(2)}) collective-permute-start(bf16[64,1280]{1,0:T(8,128)(2,1)} %get-tuple-element.56), channel_id=1, source_target_pairs={{0,16},{8,24},{16,0},{24,8},{1,17},{9,25},{17,1},{25,9},{2,18},{10... | collective-permute-start | bytes 491528 | tf_op jit(solution)/shard_map/ppermute | solution.py:33
  6.6 5.0 %collective-permute-done.1.refs_2_ = bf16[64,1280]{1,0:T(8,128)(2,1)S(1)} collective-permute-done((bf16[64,1280]{1,0:T(8,128)(2,1)}, bf16[64,1280]{1,0:T(8,128)(2,1)S(1)}, u32[]{:S(2)}, u32[]{:S(2)}) %collective-permute-start.1) | collective-permute-done | bytes 163872 | tf_op jit(solution)/shard_map/ppermute | solution.py:33
  11.7 2.2 %collective-permute-done.2.refs_3_ = bf16[64,1280]{1,0:T(8,128)(2,1)S(1)} collective-permute-done((bf16[64,1280]{1,0:T(8,128)(2,1)}, bf16[64,1280]{1,0:T(8,128)(2,1)S(1)}, u32[]{:S(2)}, u32[]{:S(2)}) %collective-permute-start.2) | collective-permute-done | bytes 163872 | tf_op jit(solution)/shard_map/ppermute | solution.py:33
  17.4 2.2 %copy-done = bf16[1024,2048]{1,0:T(8,128)(2,1)S(1)} copy-done((bf16[1024,2048]{1,0:T(8,128)(2,1)S(1)}, bf16[1024,2048]{1,0:T(8,128)(2,1)}, u32[]{:S(2)}) %copy-start) | copy-done | bytes 4194328
  21.4 4.7 %attend_near.1 = (f32[256,128]{1,0:T(8,128)S(1)}, f32[256,128]{1,0:T(8,128)S(1)}, f32[256,1024]{1,0:T(8,128)S(1)}) custom-call(s32[1]{0:T(128)} %bitcast.1.me_ref, s32[1]{0:T(128)S(6)} %copy.15.len_ref, bf16[64,1280]{1,0:T(8,128)(2,1)S(1)} %copy-done.2, bf16[64,1280]{1,0:T(8,128)(2,1)S(1)} %collective-permute-done.refs_1_, ...), custom_call_target="tpu_custom_call" | custom-call | tf_op jit(solution)/shard_map/attend_near/pallas_call | solution.py:177
  28.0 6.5 %attend_far.1 = (f32[128,2048]{1,0:T(8,128)S(1)}, f32[64,2048]{1,0:T(8,128)S(1)}, f32[64,2048]{1,0:T(8,128)S(1)}) custom-call(s32[1]{0:T(128)} %bitcast.1.me_ref, s32[1]{0:T(128)S(6)} %copy.15.len_ref, bf16[64,1280]{1,0:T(8,128)(2,1)S(1)} %copy-done.2, bf16[64,1280]{1,0:T(8,128)(2,1)S(1)} %collective-permute-done.refs_1_, ...), custom_call_target="tpu_custom_call" | custom-call | tf_op jit(solution)/shard_map/attend_far/pallas_call | solution.py:190
  34.9 2.4 %collective-permute-done.8 = f32[128,2048]{1,0:T(8,128)S(1)} collective-permute-done((f32[128,2048]{1,0:T(8,128)S(1)}, f32[128,2048]{1,0:T(8,128)S(1)}, u32[]{:S(2)}, u32[]{:S(2)}) %collective-permute-start.8) | collective-permute-done | bytes 1048608 | tf_op jit(solution)/shard_map/ppermute | solution.py:33
  37.6 2.0 %collective-permute-start.9 = (bf16[64,2048]{1,0:T(8,128)(2,1)S(1)}, bf16[64,2048]{1,0:T(8,128)(2,1)S(1)}, u32[]{:S(2)}, u32[]{:S(2)}) collective-permute-start(bf16[64,2048]{1,0:T(8,128)(2,1)S(1)} %get-tuple-element.103), channel_id=1, source_target_pairs={{0,16},{8,24},{16,0},{24,8},{1,17},{9,25},{17,1},{25,9},{2,18},{10... | collective-permute-start | bytes 786440 | tf_op jit(solution)/shard_map/ppermute | solution.py:33
  39.6 6.8 %collective-permute-done.9.refs_2_ = bf16[64,2048]{1,0:T(8,128)(2,1)S(1)} collective-permute-done((bf16[64,2048]{1,0:T(8,128)(2,1)S(1)}, bf16[64,2048]{1,0:T(8,128)(2,1)S(1)}, u32[]{:S(2)}, u32[]{:S(2)}) %collective-permute-start.9) | collective-permute-done | bytes 262176 | tf_op jit(solution)/shard_map/ppermute | solution.py:33
  47.1 2.8 %collective-permute-start.18 = (bf16[64,2176]{1,0:T(8,128)(2,1)S(1)}, bf16[64,2176]{1,0:T(8,128)(2,1)S(1)}, u32[]{:S(2)}, u32[]{:S(2)}) collective-permute-start(bf16[64,2176]{1,0:T(8,128)(2,1)S(1)} %get-tuple-element.78.refs_0_), channel_id=1, source_target_pairs={{0,4},{1,5},{2,6},{3,7},{4,0},{5,1},{6,2},{7,3},{8,12},{9,13},{10,... | collective-permute-start | bytes 835592 | tf_op jit(solution)/shard_map/ppermute | solution.py:33
  54.6 7.8 %collective-permute-done.18.refs_8_ = bf16[64,2176]{1,0:T(8,128)(2,1)S(1)} collective-permute-done((bf16[64,2176]{1,0:T(8,128)(2,1)S(1)}, bf16[64,2176]{1,0:T(8,128)(2,1)S(1)}, u32[]{:S(2)}, u32[]{:S(2)}) %collective-permute-start.18) | collective-permute-done | bytes 278560 | tf_op jit(solution)/shard_map/ppermute | solution.py:33
  67.1 4.6 %collective-permute-done.19.refs_9_ = bf16[64,2176]{1,0:T(8,128)(2,1)S(1)} collective-permute-done((bf16[64,2176]{1,0:T(8,128)(2,1)S(1)}, bf16[64,2176]{1,0:T(8,128)(2,1)S(1)}, u32[]{:S(2)}, u32[]{:S(2)}) %collective-permute-start.19) | collective-permute-done | bytes 278560 | tf_op jit(solution)/shard_map/ppermute | solution.py:33
  73.2 2.0 %collective-permute-start.15 = (bf16[64,2176]{1,0:T(8,128)(2,1)S(1)}, bf16[64,2176]{1,0:T(8,128)(2,1)}, u32[]{:S(2)}, u32[]{:S(2)}) collective-permute-start(bf16[64,2176]{1,0:T(8,128)(2,1)S(1)} %collective-permute-done.14.refs_4_), channel_id=1, source_target_pairs={{0,16},{8,24},{16,0},{24,8},{1,17},{9,25},{17,1},{25,9},{2,18},{10... | collective-permute-start | bytes 835592 | tf_op jit(solution)/shard_map/ppermute | solution.py:33
  75.7 4.5 %collective-permute-done.16.refs_6_ = bf16[64,2176]{1,0:T(8,128)(2,1)S(1)} collective-permute-done((bf16[64,2176]{1,0:T(8,128)(2,1)S(1)}, bf16[64,2176]{1,0:T(8,128)(2,1)S(1)}, u32[]{:S(2)}, u32[]{:S(2)}) %collective-permute-start.16) | collective-permute-done | bytes 278560 | tf_op jit(solution)/shard_map/ppermute | solution.py:33
  82.1 4.1 %collective-permute-done.21.refs_11_ = bf16[64,2176]{1,0:T(8,128)(2,1)} collective-permute-done((bf16[64,2176]{1,0:T(8,128)(2,1)S(1)}, bf16[64,2176]{1,0:T(8,128)(2,1)}, u32[]{:S(2)}, u32[]{:S(2)}) %collective-permute-start.21) | collective-permute-done | bytes 278560 | tf_op jit(solution)/shard_map/ppermute | solution.py:33
  87.8 2.8 %collective-permute-done.24.refs_14_ = bf16[64,2176]{1,0:T(8,128)(2,1)} collective-permute-done((bf16[64,2176]{1,0:T(8,128)(2,1)S(1)}, bf16[64,2176]{1,0:T(8,128)(2,1)}, u32[]{:S(2)}, u32[]{:S(2)}) %collective-permute-start.24) | collective-permute-done | bytes 278560 | tf_op jit(solution)/shard_map/ppermute | solution.py:33
  90.6 2.6 %collective-permute-done.25.refs_15_ = bf16[64,2176]{1,0:T(8,128)(2,1)} collective-permute-done((bf16[64,2176]{1,0:T(8,128)(2,1)}, bf16[64,2176]{1,0:T(8,128)(2,1)}, u32[]{:S(2)}, u32[]{:S(2)}) %collective-permute-start.25) | collective-permute-done | bytes 278560 | tf_op jit(solution)/shard_map/ppermute | solution.py:33
  93.2 13.6 %experts.1 = (bf16[64,2048]{1,0:T(8,128)(2,1)S(1)}, bf16[64,2048]{1,0:T(8,128)(2,1)S(1)}, bf16[32,2048]{1,0:T(8,128)(2,1)S(1)}, bf16[32,2048]{1,0:T(8,128)(2,1)S...) custom-call(s32[2]{0:T(128)S(1)} %pad_add_fusion.mine_ref, ...), custom_call_target="tpu_custom_call" | custom-call | flops 7247757312 | bytes 6291456 | tf_op jit(solution)/shard_map/experts/pallas_call | solution.py:415
  112.4 3.0 %collective-permute-done.26 = bf16[64,2048]{1,0:T(8,128)(2,1)S(1)} collective-permute-done((bf16[64,2048]{1,0:T(8,128)(2,1)S(1)}, bf16[64,2048]{1,0:T(8,128)(2,1)S(1)}, u32[]{:S(2)}, u32[]{:S(2)}) %collective-permute-start.26) | collective-permute-done | bytes 262176 | tf_op jit(solution)/shard_map/ppermute | solution.py:33
  126.6 2.1 %collective-permute-done.29 = bf16[64,2048]{1,0:T(8,128)(2,1)S(1)} collective-permute-done((bf16[64,2048]{1,0:T(8,128)(2,1)S(1)}, bf16[64,2048]{1,0:T(8,128)(2,1)S(1)}, u32[]{:S(2)}, u32[]{:S(2)}) %collective-permute-start.29) | collective-permute-done | bytes 262176 | tf_op jit(solution)/shard_map/ppermute | solution.py:33
  134.4 2.2 %collective-permute-start.39 = (bf16[32,2048]{1,0:T(8,128)(2,1)S(1)}, bf16[32,2048]{1,0:T(8,128)(2,1)S(1)}, u32[]{:S(2)}, u32[]{:S(2)}) collective-permute-start(bf16[32,2048]{1,0:T(8,128)(2,1)S(1)} %add_convert_fusion.5), channel_id=1, source_target_pairs={{0,16},{8,24},{16,0},{24,8},{1,17},{9,25},{17,1},{25,9},{2,18},{10... | collective-permute-start | bytes 393224 | tf_op jit(solution)/shard_map/ppermute | solution.py:33
  138.0 3.5 %collective-permute-start.34 = (bf16[64,2048]{1,0:T(8,128)(2,1)S(1)}, bf16[64,2048]{1,0:T(8,128)(2,1)S(1)}, u32[]{:S(2)}, u32[]{:S(2)}) collective-permute-start(bf16[64,2048]{1,0:T(8,128)(2,1)S(1)} %fusion), channel_id=1, source_target_pairs={{0,4},{1,5},{2,6},{3,7},{4,0},{5,1},{6,2},{7,3},{8,12},{9,13},{10,... | collective-permute-start | bytes 786440 | tf_op jit(solution)/shard_map/ppermute | solution.py:33
  141.7 7.0 %collective-permute-done.34 = bf16[64,2048]{1,0:T(8,128)(2,1)S(1)} collective-permute-done((bf16[64,2048]{1,0:T(8,128)(2,1)S(1)}, bf16[64,2048]{1,0:T(8,128)(2,1)S(1)}, u32[]{:S(2)}, u32[]{:S(2)}) %collective-permute-start.34) | collective-permute-done | bytes 262176 | tf_op jit(solution)/shard_map/ppermute | solution.py:33
  (109 shorter events, 48.0 us)
Async XLA Ops:
  0.0 13.9 %collective-permute-start.3 = (bf16[1,2048,768]{2,1,0:T(8,128)(2,1)}, bf16[1,2048,768]{2,1,0:T(8,128)(2,1)}, u32[]{:S(2)}, u32[]{:S(2)}) collective-permute-start(bf16[1,2048,768]{2,1,0:T(8,128)(2,1)} %refs_16_), channel_id=1, source_target_pairs={{0,8},{8,0},{16,24},{24,16},{1,9},{9,1},{17,25},{25,17},{2,10},{10... | collective-permute-start | bytes 9437192 | tf_op jit(solution)/shard_map/ppermute | solution.py:33
  0.5 13.4 %collective-permute-start.4 = (bf16[1,2048,768]{2,1,0:T(8,128)(2,1)}, bf16[1,2048,768]{2,1,0:T(8,128)(2,1)}, u32[]{:S(2)}, u32[]{:S(2)}) collective-permute-start(bf16[1,2048,768]{2,1,0:T(8,128)(2,1)} %refs_17_), channel_id=1, source_target_pairs={{0,8},{8,0},{16,24},{24,16},{1,9},{9,1},{17,25},{25,17},{2,10},{10... | collective-permute-start | bytes 9437192 | tf_op jit(solution)/shard_map/ppermute | solution.py:33
  6.4 10.9 %collective-permute-start.7 = (bf16[512,256]{1,0:T(8,128)(2,1)}, bf16[512,256]{1,0:T(8,128)(2,1)S(1)}, u32[]{:S(2)}, u32[]{:S(2)}) collective-permute-start(bf16[512,256]{1,0:T(8,128)(2,1)} %get-tuple-element.65), channel_id=1, source_target_pairs={{0,8},{8,0},{16,24},{24,16},{1,9},{9,1},{17,25},{25,17},{2,10},{10... | collective-permute-start | bytes 786440 | tf_op jit(solution)/shard_map/ppermute | solution.py:33
  13.9 12.3 %collective-permute-start.5 = (bf16[512,256]{1,0:T(8,128)(2,1)}, bf16[512,256]{1,0:T(8,128)(2,1)S(1)}, u32[]{:S(2)}, u32[]{:S(2)}) collective-permute-start(bf16[512,256]{1,0:T(8,128)(2,1)} %get-tuple-element.62), channel_id=1, source_target_pairs={{0,16},{8,24},{16,0},{24,8},{1,17},{9,25},{17,1},{25,9},{2,18},{10... | collective-permute-start | bytes 786440 | tf_op jit(solution)/shard_map/ppermute | solution.py:33
  15.3 12.6 %collective-permute-start.6 = (bf16[512,256]{1,0:T(8,128)(2,1)}, bf16[512,256]{1,0:T(8,128)(2,1)S(1)}, u32[]{:S(2)}, u32[]{:S(2)}) collective-permute-start(bf16[512,256]{1,0:T(8,128)(2,1)} %get-tuple-element.63), channel_id=1, source_target_pairs={{0,24},{8,16},{16,8},{24,0},{1,25},{9,17},{17,9},{25,1},{2,26},{10... | collective-permute-start | bytes 786440 | tf_op jit(solution)/shard_map/ppermute | solution.py:33
  47.1 15.3 %collective-permute-start.18 = (bf16[64,2176]{1,0:T(8,128)(2,1)S(1)}, bf16[64,2176]{1,0:T(8,128)(2,1)S(1)}, u32[]{:S(2)}, u32[]{:S(2)}) collective-permute-start(bf16[64,2176]{1,0:T(8,128)(2,1)S(1)} %get-tuple-element.78.refs_0_), channel_id=1, source_target_pairs={{0,4},{1,5},{2,6},{3,7},{4,0},{5,1},{6,2},{7,3},{8,12},{9,13},{10,... | collective-permute-start | bytes 835592 | tf_op jit(solution)/shard_map/ppermute | solution.py:33
  49.9 14.6 %collective-permute-start.14 = (bf16[64,2176]{1,0:T(8,128)(2,1)S(1)}, bf16[64,2176]{1,0:T(8,128)(2,1)S(1)}, u32[]{:S(2)}, u32[]{:S(2)}) collective-permute-start(bf16[64,2176]{1,0:T(8,128)(2,1)S(1)} %get-tuple-element.78.refs_0_), channel_id=1, source_target_pairs={{0,2},{1,3},{2,0},{3,1},{4,6},{5,7},{6,4},{7,5},{8,10},{9,11},{10,... | collective-permute-start | bytes 835592 | tf_op jit(solution)/shard_map/ppermute | solution.py:33
  51.5 14.6 %collective-permute-start.12 = (bf16[64,2176]{1,0:T(8,128)(2,1)S(1)}, bf16[64,2176]{1,0:T(8,128)(2,1)S(1)}, u32[]{:S(2)}, u32[]{:S(2)}) collective-permute-start(bf16[64,2176]{1,0:T(8,128)(2,1)S(1)} %get-tuple-element.78.refs_0_), channel_id=1, source_target_pairs={{0,1},{1,0},{2,3},{3,2},{4,5},{5,4},{6,7},{7,6},{8,9},{9,8},{10,11... | collective-permute-start | bytes 835592 | tf_op jit(solution)/shard_map/ppermute | solution.py:33
  53.0 13.6 %collective-permute-start.11 = (bf16[64,2176]{1,0:T(8,128)(2,1)S(1)}, bf16[64,2176]{1,0:T(8,128)(2,1)S(1)}, u32[]{:S(2)}, u32[]{:S(2)}) collective-permute-start(bf16[64,2176]{1,0:T(8,128)(2,1)S(1)} %get-tuple-element.78.refs_0_), channel_id=1, source_target_pairs={{0,16},{8,24},{16,0},{24,8},{1,17},{9,25},{17,1},{25,9},{2,18},{10... | collective-permute-start | bytes 835592 | tf_op jit(solution)/shard_map/ppermute | solution.py:33
  64.6 10.6 %collective-permute-start.20 = (bf16[64,2176]{1,0:T(8,128)(2,1)S(1)}, bf16[64,2176]{1,0:T(8,128)(2,1)S(1)}, u32[]{:S(2)}, u32[]{:S(2)}) collective-permute-start(bf16[64,2176]{1,0:T(8,128)(2,1)S(1)} %collective-permute-done.18.refs_8_), channel_id=1, source_target_pairs={{0,1},{1,0},{2,3},{3,2},{4,5},{5,4},{6,7},{7,6},{8,9},{9,8},{10,11... | collective-permute-start | bytes 835592 | tf_op jit(solution)/shard_map/ppermute | solution.py:33
  66.1 14.0 %collective-permute-start.16 = (bf16[64,2176]{1,0:T(8,128)(2,1)S(1)}, bf16[64,2176]{1,0:T(8,128)(2,1)S(1)}, u32[]{:S(2)}, u32[]{:S(2)}) collective-permute-start(bf16[64,2176]{1,0:T(8,128)(2,1)S(1)} %collective-permute-done.14.refs_4_), channel_id=1, source_target_pairs={{0,1},{1,0},{2,3},{3,2},{4,5},{5,4},{6,7},{7,6},{8,9},{9,8},{10,11... | collective-permute-start | bytes 835592 | tf_op jit(solution)/shard_map/ppermute | solution.py:33
  66.6 14.0 %collective-permute-start.13 = (bf16[64,2176]{1,0:T(8,128)(2,1)S(1)}, bf16[64,2176]{1,0:T(8,128)(2,1)S(1)}, u32[]{:S(2)}, u32[]{:S(2)}) collective-permute-start(bf16[64,2176]{1,0:T(8,128)(2,1)S(1)} %collective-permute-done.12.refs_2_), channel_id=1, source_target_pairs={{0,16},{8,24},{16,0},{24,8},{1,17},{9,25},{17,1},{25,9},{2,18},{10... | collective-permute-start | bytes 835592 | tf_op jit(solution)/shard_map/ppermute | solution.py:33
  71.7 14.6 %collective-permute-start.21 = (bf16[64,2176]{1,0:T(8,128)(2,1)S(1)}, bf16[64,2176]{1,0:T(8,128)(2,1)}, u32[]{:S(2)}, u32[]{:S(2)}) collective-permute-start(bf16[64,2176]{1,0:T(8,128)(2,1)S(1)} %collective-permute-done.19.refs_9_), channel_id=1, source_target_pairs={{0,1},{1,0},{2,3},{3,2},{4,5},{5,4},{6,7},{7,6},{8,9},{9,8},{10,11... | collective-permute-start | bytes 835592 | tf_op jit(solution)/shard_map/ppermute | solution.py:33
  73.2 14.6 %collective-permute-start.15 = (bf16[64,2176]{1,0:T(8,128)(2,1)S(1)}, bf16[64,2176]{1,0:T(8,128)(2,1)}, u32[]{:S(2)}, u32[]{:S(2)}) collective-permute-start(bf16[64,2176]{1,0:T(8,128)(2,1)S(1)} %collective-permute-done.14.refs_4_), channel_id=1, source_target_pairs={{0,16},{8,24},{16,0},{24,8},{1,17},{9,25},{17,1},{25,9},{2,18},{10... | collective-permute-start | bytes 835592 | tf_op jit(solution)/shard_map/ppermute | solution.py:33
  75.1 15.5 %collective-permute-start.24 = (bf16[64,2176]{1,0:T(8,128)(2,1)S(1)}, bf16[64,2176]{1,0:T(8,128)(2,1)}, u32[]{:S(2)}, u32[]{:S(2)}) collective-permute-start(bf16[64,2176]{1,0:T(8,128)(2,1)S(1)} %collective-permute-done.22.refs_12_), channel_id=1, source_target_pairs={{0,1},{1,0},{2,3},{3,2},{4,5},{5,4},{6,7},{7,6},{8,9},{9,8},{10,11... | collective-permute-start | bytes 835592 | tf_op jit(solution)/shard_map/ppermute | solution.py:33
  80.1 10.5 %collective-permute-start.23 = (bf16[64,2176]{1,0:T(8,128)(2,1)S(1)}, bf16[64,2176]{1,0:T(8,128)(2,1)}, u32[]{:S(2)}, u32[]{:S(2)}) collective-permute-start(bf16[64,2176]{1,0:T(8,128)(2,1)S(1)} %collective-permute-done.22.refs_12_), channel_id=1, source_target_pairs={{0,16},{8,24},{16,0},{24,8},{1,17},{9,25},{17,1},{25,9},{2,18},{10... | collective-permute-start | bytes 835592 | tf_op jit(solution)/shard_map/ppermute | solution.py:33
  80.6 10.0 %collective-permute-start.17 = (bf16[64,2176]{1,0:T(8,128)(2,1)S(1)}, bf16[64,2176]{1,0:T(8,128)(2,1)}, u32[]{:S(2)}, u32[]{:S(2)}) collective-permute-start(bf16[64,2176]{1,0:T(8,128)(2,1)S(1)} %collective-permute-done.13.refs_3_), channel_id=1, source_target_pairs={{0,2},{1,3},{2,0},{3,1},{4,6},{5,7},{6,4},{7,5},{8,10},{9,11},{10,... | collective-permute-start | bytes 835592 | tf_op jit(solution)/shard_map/ppermute | solution.py:33
  112.0 11.1 %collective-permute-start.40 = (bf16[64,2048]{1,0:T(8,128)(2,1)S(1)}, bf16[64,2048]{1,0:T(8,128)(2,1)S(1)}, u32[]{:S(2)}, u32[]{:S(2)}) collective-permute-start(bf16[64,2048]{1,0:T(8,128)(2,1)S(1)} %get-tuple-element.101), channel_id=1, source_target_pairs={{0,16},{8,24},{16,0},{24,8},{1,17},{9,25},{17,1},{25,9},{2,18},{10... | collective-permute-start | bytes 786440 | tf_op jit(solution)/shard_map/ppermute | solution.py:33
  117.5 11.3 %collective-permute-start.29 = (bf16[64,2048]{1,0:T(8,128)(2,1)S(1)}, bf16[64,2048]{1,0:T(8,128)(2,1)S(1)}, u32[]{:S(2)}, u32[]{:S(2)}) collective-permute-start(bf16[64,2048]{1,0:T(8,128)(2,1)S(1)} %pad_maximum_fusion.1), channel_id=1, source_target_pairs={{0,1},{1,0},{2,3},{3,2},{4,5},{5,4},{6,7},{7,6},{8,9},{9,8},{10,11... | collective-permute-start | bytes 786440 | tf_op jit(solution)/shard_map/ppermute | solution.py:33
  119.1 11.1 %collective-permute-start.27 = (bf16[64,2048]{1,0:T(8,128)(2,1)S(1)}, bf16[64,2048]{1,0:T(8,128)(2,1)S(1)}, u32[]{:S(2)}, u32[]{:S(2)}) collective-permute-start(bf16[64,2048]{1,0:T(8,128)(2,1)S(1)} %pad_maximum_fusion), channel_id=1, source_target_pairs={{0,16},{8,24},{16,0},{24,8},{1,17},{9,25},{17,1},{25,9},{2,18},{10... | collective-permute-start | bytes 786440 | tf_op jit(solution)/shard_map/ppermute | solution.py:33
  120.3 17.7 %collective-permute-start.33 = (bf16[64,2048]{1,0:T(8,128)(2,1)S(1)}, bf16[64,2048]{1,0:T(8,128)(2,1)S(1)}, u32[]{:S(2)}, u32[]{:S(2)}) collective-permute-start(bf16[64,2048]{1,0:T(8,128)(2,1)S(1)} %add_convert_fusion.2), channel_id=1, source_target_pairs={{0,2},{1,3},{2,0},{3,1},{4,6},{5,7},{6,4},{7,5},{8,10},{9,11},{10,... | collective-permute-start | bytes 786440 | tf_op jit(solution)/shard_map/ppermute | solution.py:33
  123.1 9.9 %collective-permute-start.38 = (bf16[64,2048]{1,0:T(8,128)(2,1)S(1)}, bf16[64,2048]{1,0:T(8,128)(2,1)S(1)}, u32[]{:S(2)}, u32[]{:S(2)}) collective-permute-start(bf16[64,2048]{1,0:T(8,128)(2,1)S(1)} %pad_maximum_fusion.3), channel_id=1, source_target_pairs={{0,1},{1,0},{2,3},{3,2},{4,5},{5,4},{6,7},{7,6},{8,9},{9,8},{10,11... | collective-permute-start | bytes 786440 | tf_op jit(solution)/shard_map/ppermute | solution.py:33
  128.7 13.0 %collective-permute-start.42 = (bf16[64,2048]{1,0:T(8,128)(2,1)S(1)}, bf16[64,2048]{1,0:T(8,128)(2,1)S(1)}, u32[]{:S(2)}, u32[]{:S(2)}) collective-permute-start(bf16[64,2048]{1,0:T(8,128)(2,1)S(1)} %add_convert_fusion), channel_id=1, source_target_pairs={{0,2},{1,3},{2,0},{3,1},{4,6},{5,7},{6,4},{7,5},{8,10},{9,11},{10,... | collective-permute-start | bytes 786440 | tf_op jit(solution)/shard_map/ppermute | solution.py:33
  138.0 10.7 %collective-permute-start.34 = (bf16[64,2048]{1,0:T(8,128)(2,1)S(1)}, bf16[64,2048]{1,0:T(8,128)(2,1)S(1)}, u32[]{:S(2)}, u32[]{:S(2)}) collective-permute-start(bf16[64,2048]{1,0:T(8,128)(2,1)S(1)} %fusion), channel_id=1, source_target_pairs={{0,4},{1,5},{2,6},{3,7},{4,0},{5,1},{6,2},{7,3},{8,12},{9,13},{10,... | collective-permute-start | bytes 786440 | tf_op jit(solution)/shard_map/ppermute | solution.py:33
  (29 other events, 276.1 us)

commit v4 on v3

--- a/solution.py
+++ b/solution.py
@@ -14,8 +14,13 @@
 TOPK = 8
 MASKED = -1e30
 EXPERT_MIB = 46
-CLOSE = 0
+GATHER = ("c2", "c1", "y0", "x0", "x2", "c3", "y2", "y1", "d0", "d2", "x1", "y3", "x3", "d1", "d3")
+TAKE = tuple(range(16))
 CALL = 4
+HOLD = 3
+GATE = 0
+WAIT = 0
+DIRECT = ()
 NEAR_MIB = 14
 FAR_MIB = 14
 NORM_MIB = 16
@@ -33,46 +38,44 @@
     return lax.ppermute(rows, axis, [(i, i ^ bits) for i in range(lax.axis_size(axis))])
 
 
+def swap_both(rows, seq_bits, exp_bits):
+    nseq, nplace = lax.axis_size("seq"), lax.axis_size("exp")
+    bits = seq_bits * nplace + exp_bits
+    return lax.ppermute(rows, ("seq", "exp"), [(i, i ^ bits) for i in range(nseq * nplace)])
+
+
 def params(mib):
     return pltpu.CompilerParams(vmem_limit_bytes=mib << 20)
 
 
-def pack_kernel(nseq, me_ref, q_ref, nk_ref, nv_ref, ck_ref, cv_ref, *refs):
-    heads, caches, sem = refs[:nseq], refs[nseq : 2 * nseq], refs[-1]
-    qcols = QH // nseq * HD
+def pack_kernel(nseq, widths, me_ref, *refs):
+    ins, outs, sem = refs[: len(widths)], refs[len(widths) : -1], refs[-1]
     copies = []
     for k in range(nseq):
-        dest = me_ref[0] ^ k
-        qat = pl.ds(pl.multiple_of(dest * qcols, HD), qcols)
-        kvat = pl.ds(pl.multiple_of(dest * KVH // nseq * HD, HD), HD)
-        pairs = (
-            (q_ref.at[:, qat], heads[k].at[:, :qcols]),
-            (nk_ref.at[:, kvat], heads[k].at[:, qcols : qcols + HD]),
-            (nv_ref.at[:, kvat], heads[k].at[:, qcols + HD :]),
-            (ck_ref.at[:, kvat], caches[k].at[:, :HD]),
-            (cv_ref.at[:, kvat], caches[k].at[:, HD:]),
-        )
-        copies += [pltpu.make_async_copy(a, b, sem.at[k, i]) for i, (a, b) in enumerate(pairs)]
+        dest, to = me_ref[0] ^ k, 0
+        for i, cols in enumerate(widths):
+            start = dest * cols if ins[i].shape[1] == cols * nseq else dest * KVH // nseq * HD
+            start = pl.ds(pl.multiple_of(start, HD), cols)
+            pair = ins[i].at[:, start], outs[k].at[:, to : to + cols]
+            copies.append(pltpu.make_async_copy(*pair, sem.at[k, i]))
+            to += cols
     for copy in copies:
         copy.start()
     for copy in copies:
         copy.wait()
 
 
-def pack(me, arrays, nseq):
-    tokens, slots = arrays[0].shape[0], arrays[-1].shape[0]
-    shapes = [jax.ShapeDtypeStruct((tokens, (QH // nseq + 2) * HD), bf16)] * nseq
-    shapes += [jax.ShapeDtypeStruct((slots, 2 * HD), bf16)] * nseq
-    outs = pl.pallas_call(
-        functools.partial(pack_kernel, nseq),
-        out_shape=shapes,
+def pack(me, arrays, widths, nseq):
+    shape = jax.ShapeDtypeStruct((arrays[0].shape[0], sum(widths)), bf16)
+    return pl.pallas_call(
+        functools.partial(pack_kernel, nseq, widths),
+        out_shape=[shape] * nseq,
         in_specs=[SMEM] + [ANY] * len(arrays),
-        out_specs=[VMEM] * len(shapes),
+        out_specs=[VMEM] * nseq,
         scratch_shapes=[pltpu.SemaphoreType.DMA((nseq, len(arrays)))],
         compiler_params=params(61),
         name="pack_heads",
     )(me, *arrays)
-    return outs[:nseq], outs[nseq:]
 
 
 def head_rows(heads, start):
@@ -118,13 +121,12 @@
         acc_ref[:, g * HD : (g + 1) * HD] = acc
 
 
-def far_kernel(nseq, me_ref, len_ref, *refs):
-    heads, caches = refs[:nseq], refs[nseq : 2 * nseq - 2]
-    peak_ref, sum_ref, acc_ref, w_ref = refs[2 * nseq - 2 : 2 * nseq + 2]
-    outs = refs[2 * nseq + 2 : -1]
-    attn_ref = refs[-1]
+def far_kernel(nseq, ks, me_ref, len_ref, *refs):
+    heads, caches = refs[: len(ks)], refs[len(ks) : len(ks) + nseq - 2]
+    peak_ref, sum_ref, acc_ref, w_ref, even_ref, odd_ref, attn_ref = refs[len(ks) + nseq - 2 :]
     group = QH // nseq
     slots, tokens = caches[0].shape[0], heads[0].shape[0]
+    mine = slice(ks[0] * tokens, (ks[-1] + 1) * tokens)
     bias = slot_bias(me_ref[0], len_ref[0], range(2, nseq), slots)
     keys = jnp.concatenate([ref[:, :HD] for ref in caches], 0)
     vals = jnp.concatenate([ref[:, HD:] for ref in caches], 0)
@@ -132,26 +134,21 @@
         at = slice(g * HD, (g + 1) * HD)
         q = head_rows(heads, g * HD)
         s = lax.dot_general(q, keys, NT, preferred_element_type=f32) + bias
-        old = peak_ref[:, g : g + 1]
+        old = peak_ref[mine, g : g + 1]
         peak = jnp.maximum(jnp.max(s, axis=1, keepdims=True), old)
         fade = jnp.exp2((old - peak) * f32(EXP2_SCALE))
         p = jnp.exp2((s - peak) * f32(EXP2_SCALE))
-        total = sum_ref[:, g : g + 1] * fade + jnp.sum(p, axis=1, keepdims=True)
-        acc = acc_ref[:, at] * fade + jnp.dot(p.astype(bf16), vals, preferred_element_type=f32)
+        total = sum_ref[mine, g : g + 1] * fade + jnp.sum(p, axis=1, keepdims=True)
+        acc = acc_ref[mine, at] * fade + jnp.dot(p.astype(bf16), vals, preferred_element_type=f32)
         attn_ref[:, at] = (acc / total).astype(bf16)
-    send, near, far = outs
-    places = []
-    for k in range(nseq):
-        if k % 2:
-            places.append((send, k // 2 * tokens))
-        else:
-            places.append((far, (k // 2 - 1) * tokens) if k else (near, 0))
     step = 512
     for at in range(0, w_ref.shape[1], step):
         cols = slice(at, at + step)
         total = jnp.dot(attn_ref[...], w_ref[:, cols], preferred_element_type=f32)
-        for k, (out, row) in enumerate(places):
-            out[row : row + tokens, cols] = total[k * tokens : (k + 1) * tokens]
+        for i in range(len(ks)):
+            to = slice(i // 2 * tokens, (i // 2 + 1) * tokens)
+            out = odd_ref if i % 2 else even_ref
+            out[to, cols] = total[i * tokens : (i + 1) * tokens].astype(out.dtype)
 
 
 def project_attention(
@@ -162,16 +159,19 @@
     width = out_weight.shape[1]
     group = QH // nseq
     qtok = nseq * tokens
-    heads, caches = pack(me, (queries, new_keys, new_values, cache_keys, cache_values), nseq)
+    heads = pack(me, (queries, new_keys, new_values), (group * HD, HD, HD), nseq)
     order = sorted(range(1, nseq), reverse=True)
     heads = {0: heads[0]} | {k: swap(heads[k], "seq", k) for k in order}
     others = [swap(w, "seq", 1) for w in weights[:2]]
+    held = heads[1], cache_keys, cache_values
+    heads[1], cache_keys, cache_values = lax.optimization_barrier(held)
+    caches = pack(me, (cache_keys, cache_values), (HD, HD), nseq)
     caches = {0: caches[0], 1: swap(caches[1], "seq", 1)} | dict(enumerate(caches[2:], 2))
-    far_heads = [heads[k] for k in range(2, nseq)]
-    far_caches = [caches[k] for k in range(2, nseq)]
-    far_heads, far_caches, others = lax.optimization_barrier((far_heads, far_caches, others))
     for k in range(2, nseq):
-        heads[k], caches[k] = far_heads[k - 2], swap(far_caches[k - 2], "seq", k)
+        hold = (heads[k], caches[k], others if k == HOLD else [])
+        heads[k], cache, held = lax.optimization_barrier(hold)
+        others = held or others
+        caches[k] = swap(cache, "seq", k)
     heads = [heads[k] for k in range(nseq)]
     caches = [caches[k] for k in range(nseq)]
     state = pl.pallas_call(
@@ -186,27 +186,26 @@
         compiler_params=params(NEAR_MIB),
         name="attend_near",
     )(me, length, *heads, *caches[:2], out_weight)
-    half = nseq // 2 * tokens
-    parts = pl.pallas_call(
-        functools.partial(far_kernel, nseq),
-        out_shape=[
-            jax.ShapeDtypeStruct((half, width), f32),
-            jax.ShapeDtypeStruct((tokens, width), f32),
-            jax.ShapeDtypeStruct((half - tokens, width), f32),
-        ],
-        in_specs=[SMEM] * 2 + [VMEM] * (2 * nseq + 2),
-        out_specs=[VMEM] * 3,
-        scratch_shapes=[pltpu.VMEM((qtok, group * HD), bf16)],
-        compiler_params=params(FAR_MIB),
-        name="attend_far",
-    )(me, length, *heads, *caches[2:], *state, out_weight)
-    send, near, far = parts
-    got = swap(send, "seq", 1)
+
+    def project(ks, state):
+        shape = (len(ks) // 2 * tokens, width)
+        return pl.pallas_call(
+            functools.partial(far_kernel, nseq, ks),
+            out_shape=[jax.ShapeDtypeStruct(shape, f32), jax.ShapeDtypeStruct(shape, bf16)],
+            in_specs=[SMEM] * 2 + [VMEM] * (len(ks) + nseq + 2),
+            out_specs=[VMEM] * 2,
+            scratch_shapes=[pltpu.VMEM((len(ks) * tokens, group * HD), bf16)],
+            compiler_params=params(FAR_MIB),
+            name="attend_far",
+        )(me, length, *[heads[k] for k in ks], *caches[2:], *state, out_weight)
+
+    even, odd = project(list(range(nseq)), state)
+    got = swap(odd, "seq", 1)
     got, rest = lax.optimization_barrier((got, weights[2:]))
     others += [swap(w, "seq", 1) for w in rest]
-    terms = [near, got[:tokens]]
-    for at in range(tokens, half, tokens):
-        both = far[at - tokens : at] + got[at : at + tokens]
+    terms = [even[:tokens], got[:tokens]]
+    for at in range(tokens, got.shape[0], tokens):
+        both = add(even[at : at + tokens], got[at : at + tokens])
         terms.append(swap(both.astype(bf16), "seq", 2 * at // tokens))
     return terms, [*weights, *others]
 
@@ -255,55 +254,45 @@
     )(residual, *terms, gain.reshape(1, width), router.T, ids.T)
 
 
-def gather_rows(rows, weights, planes, sides):
-    columns = [rows]
-    for kz in range(1, planes):
-        odd = kz > 1 and kz % 2
-        columns.append(swap(columns[kz - 1], "exp", 2) if odd else swap(rows, "exp", 2 * kz))
-        if kz == CLOSE:
-            columns[kz], weights = lax.optimization_barrier((columns[kz], weights))
-    blocks = []
-    for kz, col in enumerate(columns):
-        right = [swap(col, "seq", 2 * kx) for kx in range(1, sides)]
-        up = swap(col, "exp", 1)
-        if kz % 2:
-            over = [swap(block, "exp", 2) for block in blocks[-1][sides + 1 :]]
-        elif kz % 4:
-            over = [swap(block, "exp", 1) for block in right]
+def gather_rows(rows, planes, sides):
+    at = {("c", 0): [rows]}
+    steps = [(kind, kz) for kz in range(planes) for kind in "cxyd" if (kind, kz) not in at]
+    if planes == 4:
+        steps = [(step[0], int(step[1])) for step in GATHER]
+    for kind, kz in steps:
+        if kind == "c":
+            near = kz > 1 and kz % 2
+            got = [swap(at["c", kz - 1][0], "exp", 2) if near else swap(rows, "exp", 2 * kz)]
+        elif kind == "x":
+            got = [swap(at["c", kz][0], "seq", 2 * kx) for kx in range(1, sides)]
+        elif kind == "y":
+            got = [swap(at["c", kz][0], "exp", 1)]
+        elif kz % 2:
+            got = [swap(block, "exp", 2) for block in at["d", kz - 1]]
+        elif kz in DIRECT:
+            got = [swap_both(at["c", kz][0], 2 * kx, 1) for kx in range(1, sides)]
+        elif kz % 4 == 0:
+            got = [swap(at["y", kz][0], "seq", 2 * kx) for kx in range(1, sides)]
         else:
-            over = [swap(up, "seq", 2 * kx) for kx in range(1, sides)]
-        blocks.append([col, *right, up, *over])
-    return blocks, weights
-
-
-def plane_layout(odd, sides, tokens):
-    half = tokens // 2
+            got = [swap(block, "exp", 1) for block in at["x", kz]]
+        at[kind, kz] = got
+    return [[block for kind in "cxyd" for block in at[kind, kz]] for kz in range(planes)]
+
+
+def plane_layout(sides, tokens):
+    rows = [tokens, (sides - 1) * tokens, tokens, (sides - 1) * tokens]
     moves = []
-    if odd:
-        rows = [tokens, (sides - 1) * tokens, tokens, (sides - 1) * tokens]
-        for ky in range(2):
-            for kx in range(sides):
-                to = (2 * ky + (kx > 0), max(kx - 1, 0) * tokens)
-                moves.append(((ky * sides + kx) * tokens, tokens, *to))
-        return rows, moves
-    rows = [2 * half, sides * half, (sides - 1) * half, half, (sides - 1) * tokens]
     for ky in range(2):
         for kx in range(sides):
-            row = (ky * sides + kx) * tokens
-            if ky and kx:
-                moves.append((row, tokens, 4, (kx - 1) * tokens))
-                continue
-            top = (2, (kx - 1) * half) if kx else (0, ky * half)
-            low = (3, 0) if ky else (1, kx * half)
-            moves.append((row, half, *top))
-            moves.append((row + half, half, *low))
+            to = (2 * ky + (kx > 0), max(kx - 1, 0) * tokens)
+            moves.append(((ky * sides + kx) * tokens, tokens, *to))
     return rows, moves
 
 
-def expert_kernel(layouts, per_group, tokens, cap, nexp, mine_ref, *refs):
+def expert_kernel(layouts, take, per_group, tokens, cap, nexp, mine_ref, *refs):
     planes = len(layouts)
     pieces = planes * per_group
-    blocks = refs[:pieces]
+    blocks = [refs[take.index(i)] for i in range(pieces)]
     weights = (refs[pieces : pieces + 3], refs[pieces + 3 : pieces + 6])
     nouts = sum(len(rows) for rows, _ in layouts)
     outs = refs[pieces + 6 : pieces + 6 + nouts]
@@ -410,10 +399,12 @@
     _, width, hidden = weights[0].shape
     grows = per_group * cap
     rows = planes * grows
-    layouts = [plane_layout(g % 2, sides, tokens) for g in range(planes)]
+    layouts = [plane_layout(sides, tokens)] * planes
     out_shape = [jax.ShapeDtypeStruct((n, width), bf16) for ns, _ in layouts for n in ns]
+    flat = [block for plane in blocks for block in plane]
+    take = TAKE if len(flat) == len(TAKE) else tuple(range(len(flat)))
     outs = pl.pallas_call(
-        functools.partial(expert_kernel, layouts, per_group, tokens, cap, nexp),
+        functools.partial(expert_kernel, layouts, take, per_group, tokens, cap, nexp),
         out_shape=out_shape,
         in_specs=[SMEM] + [ANY] * (planes * per_group + len(weights)),
         out_specs=[VMEM] * len(out_shape),
@@ -432,7 +423,7 @@
             flops=12 * rows * width * hidden, bytes_accessed=8 * rows * width, transcendentals=0
         ),
         name="experts",
-    )(mine, *[block for plane in blocks for block in plane], *weights)
+    )(mine, *[flat[i] for i in take], *weights)
     terms, at = [], 0
     for ns, _ in layouts:
         terms.append(outs[at : at + len(ns)])
@@ -447,42 +438,30 @@
     return total
 
 
-def even_sum(term, over, sides):
-    keep_a, keep_b, send_a, send_b, own_over = term
-    half = send_b.shape[0]
-    over = [
-        add(own_over[i * 2 * half : (i + 1) * 2 * half], o).astype(bf16) for i, o in enumerate(over)
-    ]
-    got_a = [
-        swap(jnp.concatenate([send_a[i * half : (i + 1) * half], o[:half]], 0), "seq", 2 * i + 2)
-        for i, o in enumerate(over)
-    ]
-    got_b = swap(jnp.concatenate([send_b, *[o[half:] for o in over]], 0), "exp", 1)
-    next_a = swap(add(keep_a[half:], *[g[half:] for g in got_a]).astype(bf16), "exp", 1)
-    next_b = []
-    for kx in range(1, sides):
-        at = slice(kx * half, (kx + 1) * half)
-        next_b.append(swap(add(keep_b[at], got_b[at]).astype(bf16), "seq", 2 * kx))
-    top = add(keep_a[:half], *[g[:half] for g in got_a], next_a)
-    low = add(keep_b[:half], got_b[:half], *next_b)
-    return jnp.concatenate([top, low], 0)
-
-
-def pair_sum(even, odd, sides):
-    keep, right, up, over = odd
-    size = keep.shape[0]
+def pair_sum(even, odd, later, sides):
+    size = even[0].shape[0]
     parts = [slice(i * size, (i + 1) * size) for i in range(sides - 1)]
-    over = [swap(over[at], "exp", 2) for at in parts]
-    got = [swap(right[at], "seq", 2 * i + 2) for i, at in enumerate(parts)]
-    got.append(swap(up, "exp", 1))
-    return even_sum(even, over, sides), add(keep, *got)
+    over = [swap(odd[3][at], "exp", 2) for at in parts]
+    odd_got = [swap(odd[1][at], "seq", 2 * i + 2) for i, at in enumerate(parts)]
+    odd_got.append(swap(odd[2], "exp", 1))
+    even_got = [swap(even[1][at], "seq", 2 * i + 2) for i, at in enumerate(parts)]
+    even_got.append(swap(even[2], "exp", 1))
+    if later:
+        over, odd_got, later = lax.optimization_barrier((over, odd_got, later))
+    over = [add(even[3][at], o).astype(bf16) for at, o in zip(parts, over)]
+    if WAIT and later:
+        over, later = lax.optimization_barrier((over, later))
+    even_got += [swap_both(o, 2 * i + 2, 1) for i, o in enumerate(over)]
+    return add(even[0], *even_got), add(odd[0], *odd_got), later
 
 
 def return_terms(terms, sides):
     own = []
     for kz in reversed(range(0, len(terms), 2)):
-        even, odd = pair_sum(terms[kz], terms[kz + 1], sides)
+        even, odd, terms[:kz] = pair_sum(terms[kz], terms[kz + 1], terms[:kz], sides)
         got = swap(odd.astype(bf16), "exp", 2)
+        if kz and GATE:
+            got, terms[:kz] = lax.optimization_barrier((got, terms[:kz]))
         own += [swap(add(even, got).astype(bf16), "exp", 2 * kz)] if kz else [even, got]
     return own
 
@@ -494,7 +473,7 @@
     me = lax.axis_index("seq") * nplace + lax.axis_index("exp")
     other = (lax.axis_index("seq") ^ 1) * nplace + lax.axis_index("exp")
     mine = jnp.stack([me, other]).astype(jnp.int32)
-    blocks, weights = gather_rows(rows, weights, planes, sides)
+    blocks = gather_rows(rows, planes, sides)
     terms = []
     for at in range(0, planes, CALL):
         terms += expert_terms(blocks[at : at + CALL], sides, mine, weights, cap, nexp)

time: 150 us -> 144 us (0.960)
  waiting for transfers between devices: 62.3 us -> 55.6 us
  Pallas kernels: 28.4 us -> 29.9 us
    ppermute x43 -> x39, waiting for transfers between devices: 62.3 us -> 52.4 us  [swap(): lax.ppermute(rows, axis, [(i, i ^ bits) for i in range(lax.axis_size(axis...]
    ppermute x0 -> x2, waiting for transfers between devices: none -> 3.2 us  [swap_both(): lax.ppermute(rows, ('seq', 'exp'), [(i, i ^ bits) for i in range(nseq * n...]
    ppermute x43 -> x39, starting transfers between devices: 52.1 us -> 49.9 us  [swap(): lax.ppermute(rows, axis, [(i, i ^ bits) for i in range(lax.axis_size(axis...]
    ppermute x0 -> x2, starting transfers between devices: none -> 2.19 us  [swap_both(): lax.ppermute(rows, ('seq', 'exp'), [(i, i ^ bits) for i in range(nseq * n...]
    pallas_call x3 -> x4, Pallas kernels: 23 us -> 24.6 us  [the longest x1 13.6 us: expert_terms(): pl.pallas_call(functools.partial(expert_kernel, layouts, take, per_group,...]
  transfers between devices with their start and end apart: 43 -> 41, of which waited for: 19 -> 22; matrix products, arithmetic and copies ran while one was open for 1% -> 0% of each run, Pallas kernels for 6% -> 7%
where the time goes in v4:
time: 144 us
  waiting for transfers between devices  55.6 us (39%)
  starting transfers between devices  52 us (36%)
  Pallas kernels  29.9 us (21%)
  local copies, waits for them, and re-layouts  4.1 us (3%)
  other arithmetic  1.63 us (1%)
    ppermute x39, waiting for transfers between devices, swap(): lax.ppermute(rows, axis, [(i, i ^ bits) for i in range(lax.axis_size(axis...  52.4 us
    ppermute x39, starting transfers between devices, swap(): lax.ppermute(rows, axis, [(i, i ^ bits) for i in range(lax.axis_size(axis...  49.9 us
    pallas_call x1, Pallas kernels, expert_terms(): pl.pallas_call(functools.partial(expert_kernel, layouts, take, per_group,...  13.6 us
    pallas_call x1, Pallas kernels, project(): pl.pallas_call(functools.partial(far_kernel, nseq, ks), out_shape=[jax.Sh...  6.53 us
    pallas_call x1, Pallas kernels, project_attention(): pl.pallas_call(functools.partial(near_kernel, nseq), out_shape=[jax.Shape...  4.71 us
    pallas_call x2, Pallas kernels, pack(): pl.pallas_call(functools.partial(pack_kernel, nseq, widths), out_shape=[s...  4.46 us
    unnamed x20, local copies, waits for them, and re-layouts  4.08 us
    ppermute x2, waiting for transfers between devices, swap_both(): lax.ppermute(rows, ('seq', 'exp'), [(i, i ^ bits) for i in range(nseq * n...  3.2 us
  transfers between devices with their start and end apart: 41, of which 22 were waited for; matrix products, arithmetic and copies ran while one was open for 0% of the time, Pallas kernels for 7%

profile of v4, /device:TPU:0, one launch (start us, length us, event | category | flops | bytes accessed | tf_op | source)
XLA Modules:
  0.0 144.1 jit_solution(14887412689677450759)
XLA Ops:
  0.5 2.1 %pack_heads.2 = (bf16[64,1280]{1,0:T(8,128)(2,1)}, bf16[64,1280]{1,0:T(8,128)(2,1)}, bf16[64,1280]{1,0:T(8,128)(2,1)}, bf16[64,1280]{1,0:T(8,128)(2,1)}) custom-call(s32[1]{0:T(128)} %bitcast.1.me_ref, bf16[64,4096]{1,0:T(8,128)(2,1)} %bitcast.20, bf16[64,512]{1,0:T(8,128)(2,1)} %bitcast.23, bf16[64,512]{1,0:T(8,128)(2,1)} %bitcast.24), custom_call_target="tpu_custom_call" | custom-call | tf_op jit(solution)/shard_map/pack_heads/pallas_call | solution.py:70
  3.2 2.6 %collective-permute-start.1 = (bf16[64,1280]{1,0:T(8,128)(2,1)}, bf16[64,1280]{1,0:T(8,128)(2,1)S(1)}, u32[]{:S(2)}, u32[]{:S(2)}) collective-permute-start(bf16[64,1280]{1,0:T(8,128)(2,1)} %get-tuple-element.68), channel_id=1, source_target_pairs={{0,16},{8,24},{16,0},{24,8},{1,17},{9,25},{17,1},{25,9},{2,18},{10... | collective-permute-start | bytes 491528 | tf_op jit(solution)/shard_map/ppermute | solution.py:38
  6.4 2.3 %pack_heads.3 = (bf16[512,256]{1,0:T(8,128)(2,1)}, bf16[512,256]{1,0:T(8,128)(2,1)}, bf16[512,256]{1,0:T(8,128)(2,1)}, bf16[512,256]{1,0:T(8,128)(2,1)}) custom-call(s32[1]{0:T(128)} %bitcast.1.me_ref, bf16[512,512]{1,0:T(8,128)(2,1)} %bitcast.21, bf16[512,512]{1,0:T(8,128)(2,1)} %bitcast.22), custom_call_target="tpu_custom_call" | custom-call | tf_op jit(solution)/shard_map/pack_heads/pallas_call | solution.py:70
  8.8 2.2 %collective-permute-done.1.refs_2_ = bf16[64,1280]{1,0:T(8,128)(2,1)S(1)} collective-permute-done((bf16[64,1280]{1,0:T(8,128)(2,1)}, bf16[64,1280]{1,0:T(8,128)(2,1)S(1)}, u32[]{:S(2)}, u32[]{:S(2)}) %collective-permute-start.1) | collective-permute-done | bytes 163872 | tf_op jit(solution)/shard_map/ppermute | solution.py:38
  16.1 2.2 %copy-done = bf16[1024,2048]{1,0:T(8,128)(2,1)S(1)} copy-done((bf16[1024,2048]{1,0:T(8,128)(2,1)S(1)}, bf16[1024,2048]{1,0:T(8,128)(2,1)}, u32[]{:S(2)}) %copy-start) | copy-done | bytes 4194328
  20.2 4.7 %attend_near.1 = (f32[256,128]{1,0:T(8,128)S(1)}, f32[256,128]{1,0:T(8,128)S(1)}, f32[256,1024]{1,0:T(8,128)S(1)}) custom-call(s32[1]{0:T(128)} %bitcast.1.me_ref, s32[1]{0:T(128)S(6)} %copy.15.len_ref, bf16[64,1280]{1,0:T(8,128)(2,1)S(1)} %copy-done.2, bf16[64,1280]{1,0:T(8,128)(2,1)S(1)} %collective-permute-done.refs_1_, ...), custom_call_target="tpu_custom_call" | custom-call | tf_op jit(solution)/shard_map/attend_near/pallas_call | solution.py:177
  25.5 6.5 %attend_far.1 = (f32[128,2048]{1,0:T(8,128)S(1)}, bf16[128,2048]{1,0:T(8,128)(2,1)S(1)}) custom-call(s32[1]{0:T(128)} %bitcast.1.me_ref, s32[1]{0:T(128)S(6)} %copy.15.len_ref, bf16[64,1280]{1,0:T(8,128)(2,1)S(1)} %copy-done.2, bf16[64,1280]{1,0:T(8,128)(2,1)S(1)} %collective-permute-done.refs_1_, bf16[64,1280]{1,0:T(8,128)(2,1)S(1)} %collective-permute-done.1.refs_2_, ...), custom_call_target="tpu_custom_call" | custom-call | tf_op jit(solution)/shard_map/attend_far/pallas_call | solution.py:192
  36.1 6.9 %collective-permute-done.9.refs_2_ = bf16[64,2048]{1,0:T(8,128)(2,1)S(1)} collective-permute-done((bf16[64,2048]{1,0:T(8,128)(2,1)S(1)}, bf16[64,2048]{1,0:T(8,128)(2,1)S(1)}, u32[]{:S(2)}, u32[]{:S(2)}) %collective-permute-start.9) | collective-permute-done | bytes 262176 | tf_op jit(solution)/shard_map/ppermute | solution.py:38
  43.6 2.8 %collective-permute-start.18 = (bf16[64,2176]{1,0:T(8,128)(2,1)S(1)}, bf16[64,2176]{1,0:T(8,128)(2,1)S(1)}, u32[]{:S(2)}, u32[]{:S(2)}) collective-permute-start(bf16[64,2176]{1,0:T(8,128)(2,1)S(1)} %get-tuple-element.91.refs_0_), channel_id=1, source_target_pairs={{0,4},{1,5},{2,6},{3,7},{4,0},{5,1},{6,2},{7,3},{8,12},{9,13},{10,... | collective-permute-start | bytes 835592 | tf_op jit(solution)/shard_map/ppermute | solution.py:38
  51.0 7.8 %collective-permute-done.18.refs_8_ = bf16[64,2176]{1,0:T(8,128)(2,1)S(1)} collective-permute-done((bf16[64,2176]{1,0:T(8,128)(2,1)S(1)}, bf16[64,2176]{1,0:T(8,128)(2,1)S(1)}, u32[]{:S(2)}, u32[]{:S(2)}) %collective-permute-start.18) | collective-permute-done | bytes 278560 | tf_op jit(solution)/shard_map/ppermute | solution.py:38
  63.5 4.4 %collective-permute-done.19.refs_9_ = bf16[64,2176]{1,0:T(8,128)(2,1)S(1)} collective-permute-done((bf16[64,2176]{1,0:T(8,128)(2,1)S(1)}, bf16[64,2176]{1,0:T(8,128)(2,1)S(1)}, u32[]{:S(2)}, u32[]{:S(2)}) %collective-permute-start.19) | collective-permute-done | bytes 278560 | tf_op jit(solution)/shard_map/ppermute | solution.py:38
  72.0 4.5 %collective-permute-done.16.refs_6_ = bf16[64,2176]{1,0:T(8,128)(2,1)S(1)} collective-permute-done((bf16[64,2176]{1,0:T(8,128)(2,1)S(1)}, bf16[64,2176]{1,0:T(8,128)(2,1)S(1)}, u32[]{:S(2)}, u32[]{:S(2)}) %collective-permute-start.16) | collective-permute-done | bytes 278560 | tf_op jit(solution)/shard_map/ppermute | solution.py:38
  78.4 4.1 %collective-permute-done.21.refs_11_ = bf16[64,2176]{1,0:T(8,128)(2,1)} collective-permute-done((bf16[64,2176]{1,0:T(8,128)(2,1)S(1)}, bf16[64,2176]{1,0:T(8,128)(2,1)}, u32[]{:S(2)}, u32[]{:S(2)}) %collective-permute-start.21) | collective-permute-done | bytes 278560 | tf_op jit(solution)/shard_map/ppermute | solution.py:38
  84.1 2.8 %collective-permute-done.24.refs_14_ = bf16[64,2176]{1,0:T(8,128)(2,1)} collective-permute-done((bf16[64,2176]{1,0:T(8,128)(2,1)S(1)}, bf16[64,2176]{1,0:T(8,128)(2,1)}, u32[]{:S(2)}, u32[]{:S(2)}) %collective-permute-start.24) | collective-permute-done | bytes 278560 | tf_op jit(solution)/shard_map/ppermute | solution.py:38
  87.0 2.7 %collective-permute-done.25.refs_15_ = bf16[64,2176]{1,0:T(8,128)(2,1)} collective-permute-done((bf16[64,2176]{1,0:T(8,128)(2,1)}, bf16[64,2176]{1,0:T(8,128)(2,1)}, u32[]{:S(2)}, u32[]{:S(2)}) %collective-permute-start.25) | collective-permute-done | bytes 278560 | tf_op jit(solution)/shard_map/ppermute | solution.py:38
  89.7 13.6 %experts.1 = (bf16[64,2048]{1,0:T(8,128)(2,1)S(1)}, bf16[64,2048]{1,0:T(8,128)(2,1)S(1)}, bf16[64,2048]{1,0:T(8,128)(2,1)S(1)}, bf16[64,2048]{1,0:T(8,128)(2,1)S...) custom-call(s32[2]{0:T(128)S(1)} %pad_add_fusion.mine_ref, ...), custom_call_target="tpu_custom_call" | custom-call | flops 7247757312 | bytes 6291456 | tf_op jit(solution)/shard_map/experts/pallas_call | solution.py:406
  109.7 3.0 %collective-permute-done.29 = bf16[64,2048]{1,0:T(8,128)(2,1)S(1)} collective-permute-done((bf16[64,2048]{1,0:T(8,128)(2,1)S(1)}, bf16[64,2048]{1,0:T(8,128)(2,1)S(1)}, u32[]{:S(2)}, u32[]{:S(2)}) %collective-permute-start.29) | collective-permute-done | bytes 262176 | tf_op jit(solution)/shard_map/ppermute | solution.py:38
  113.8 3.8 %collective-permute-start.32 = (bf16[64,2048]{1,0:T(8,128)(2,1)S(1)}, bf16[64,2048]{1,0:T(8,128)(2,1)S(1)}, u32[]{:S(2)}, u32[]{:S(2)}) collective-permute-start(bf16[64,2048]{1,0:T(8,128)(2,1)S(1)} %add_convert_fusion.4), channel_id=1, source_target_pairs={{0,2},{1,3},{2,0},{3,1},{4,6},{5,7},{6,4},{7,5},{8,10},{9,11},{10,... | collective-permute-start | bytes 786440 | tf_op jit(solution)/shard_map/ppermute | solution.py:38
  117.7 3.3 %collective-permute-start.34 = (bf16[64,2048]{1,0:T(8,128)(2,1)S(1)}, bf16[64,2048]{1,0:T(8,128)(2,1)S(1)}, u32[]{:S(2)}, u32[]{:S(2)}) collective-permute-start(bf16[64,2048]{1,0:T(8,128)(2,1)S(1)} %get-tuple-element.118), channel_id=1, source_target_pairs={{0,16},{8,24},{16,0},{24,8},{1,17},{9,25},{17,1},{25,9},{2,18},{10... | collective-permute-start | bytes 786440 | tf_op jit(solution)/shard_map/ppermute | solution.py:38
  121.4 4.4 %collective-permute-start.36 = (bf16[64,2048]{1,0:T(8,128)(2,1)S(1)}, bf16[64,2048]{1,0:T(8,128)(2,1)S(1)}, u32[]{:S(2)}, u32[]{:S(2)}) collective-permute-start(bf16[64,2048]{1,0:T(8,128)(2,1)S(1)} %get-tuple-element.121), channel_id=1, source_target_pairs={{0,2},{1,3},{2,0},{3,1},{4,6},{5,7},{6,4},{7,5},{8,10},{9,11},{10,... | collective-permute-start | bytes 786440 | tf_op jit(solution)/shard_map/ppermute | solution.py:38
  128.5 2.8 %collective-permute-done.36 = bf16[64,2048]{1,0:T(8,128)(2,1)S(1)} collective-permute-done((bf16[64,2048]{1,0:T(8,128)(2,1)S(1)}, bf16[64,2048]{1,0:T(8,128)(2,1)S(1)}, u32[]{:S(2)}, u32[]{:S(2)}) %collective-permute-start.36) | collective-permute-done | bytes 262176 | tf_op jit(solution)/shard_map/ppermute | solution.py:38
  131.3 2.2 %collective-permute-start.33 = (bf16[64,2048]{1,0:T(8,128)(2,1)S(1)}, bf16[64,2048]{1,0:T(8,128)(2,1)S(1)}, u32[]{:S(2)}, u32[]{:S(2)}) collective-permute-start(bf16[64,2048]{1,0:T(8,128)(2,1)S(1)} %add_convert_fusion.3), channel_id=1, source_target_pairs={{0,4},{1,5},{2,6},{3,7},{4,0},{5,1},{6,2},{7,3},{8,12},{9,13},{10,... | collective-permute-start | bytes 786440 | tf_op jit(solution)/shard_map/ppermute | solution.py:38
  134.3 2.1 %collective-permute-start.37 = (bf16[64,2048]{1,0:T(8,128)(2,1)S(1)}, bf16[64,2048]{1,0:T(8,128)(2,1)S(1)}, u32[]{:S(2)}, u32[]{:S(2)}) collective-permute-start(bf16[64,2048]{1,0:T(8,128)(2,1)S(1)} %add_convert_fusion.2), channel_id=1, source_target_pairs={{0,17},{1,16},{2,19},{3,18},{4,21},{5,20},{6,23},{7,22},{8,25},{9,... | collective-permute-start | bytes 786440 | tf_op jit(solution)/shard_map/ppermute | solution.py:44
  137.9 2.6 %collective-permute-done.33 = bf16[64,2048]{1,0:T(8,128)(2,1)S(1)} collective-permute-done((bf16[64,2048]{1,0:T(8,128)(2,1)S(1)}, bf16[64,2048]{1,0:T(8,128)(2,1)S(1)}, u32[]{:S(2)}, u32[]{:S(2)}) %collective-permute-start.33) | collective-permute-done | bytes 262176 | tf_op jit(solution)/shard_map/ppermute | solution.py:38
  (93 shorter events, 46.8 us)
Async XLA Ops:
  0.0 14.0 %collective-permute-start.3 = (bf16[1,2048,768]{2,1,0:T(8,128)(2,1)}, bf16[1,2048,768]{2,1,0:T(8,128)(2,1)}, u32[]{:S(2)}, u32[]{:S(2)}) collective-permute-start(bf16[1,2048,768]{2,1,0:T(8,128)(2,1)} %refs_16_), channel_id=1, source_target_pairs={{0,8},{8,0},{16,24},{24,16},{1,9},{9,1},{17,25},{25,17},{2,10},{10... | collective-permute-start | bytes 9437192 | tf_op jit(solution)/shard_map/ppermute | solution.py:38
  0.5 13.5 %collective-permute-start.4 = (bf16[1,2048,768]{2,1,0:T(8,128)(2,1)}, bf16[1,2048,768]{2,1,0:T(8,128)(2,1)}, u32[]{:S(2)}, u32[]{:S(2)}) collective-permute-start(bf16[1,2048,768]{2,1,0:T(8,128)(2,1)} %refs_17_), channel_id=1, source_target_pairs={{0,8},{8,0},{16,24},{24,16},{1,9},{9,1},{17,25},{25,17},{2,10},{10... | collective-permute-start | bytes 9437192 | tf_op jit(solution)/shard_map/ppermute | solution.py:38
  11.0 13.9 %collective-permute-start.5 = (bf16[512,256]{1,0:T(8,128)(2,1)}, bf16[512,256]{1,0:T(8,128)(2,1)S(1)}, u32[]{:S(2)}, u32[]{:S(2)}) collective-permute-start(bf16[512,256]{1,0:T(8,128)(2,1)} %get-tuple-element.76), channel_id=1, source_target_pairs={{0,16},{8,24},{16,0},{24,8},{1,17},{9,25},{17,1},{25,9},{2,18},{10... | collective-permute-start | bytes 786440 | tf_op jit(solution)/shard_map/ppermute | solution.py:38
  14.0 11.5 %collective-permute-start.6 = (bf16[512,256]{1,0:T(8,128)(2,1)}, bf16[512,256]{1,0:T(8,128)(2,1)S(1)}, u32[]{:S(2)}, u32[]{:S(2)}) collective-permute-start(bf16[512,256]{1,0:T(8,128)(2,1)} %get-tuple-element.77), channel_id=1, source_target_pairs={{0,24},{8,16},{16,8},{24,0},{1,25},{9,17},{17,9},{25,1},{2,26},{10... | collective-permute-start | bytes 786440 | tf_op jit(solution)/shard_map/ppermute | solution.py:38
  34.1 9.6 %collective-permute-start.10 = (bf16[1,768,2048]{2,1,0:T(8,128)(2,1)S(1)}, bf16[1,768,2048]{2,1,0:T(8,128)(2,1)S(1)}, u32[]{:S(2)}, u32[]{:S(2)}) collective-permute-start(bf16[1,768,2048]{2,1,0:T(8,128)(2,1)S(1)} %copy-done.8), channel_id=1, source_target_pairs={{0,8},{8,0},{16,24},{24,16},{1,9},{9,1},{17,25},{25,17},{2,10},{10... | collective-permute-start | bytes 9437192 | tf_op jit(solution)/shard_map/ppermute | solution.py:38
  43.6 15.2 %collective-permute-start.18 = (bf16[64,2176]{1,0:T(8,128)(2,1)S(1)}, bf16[64,2176]{1,0:T(8,128)(2,1)S(1)}, u32[]{:S(2)}, u32[]{:S(2)}) collective-permute-start(bf16[64,2176]{1,0:T(8,128)(2,1)S(1)} %get-tuple-element.91.refs_0_), channel_id=1, source_target_pairs={{0,4},{1,5},{2,6},{3,7},{4,0},{5,1},{6,2},{7,3},{8,12},{9,13},{10,... | collective-permute-start | bytes 835592 | tf_op jit(solution)/shard_map/ppermute | solution.py:38
  46.4 14.5 %collective-permute-start.14 = (bf16[64,2176]{1,0:T(8,128)(2,1)S(1)}, bf16[64,2176]{1,0:T(8,128)(2,1)S(1)}, u32[]{:S(2)}, u32[]{:S(2)}) collective-permute-start(bf16[64,2176]{1,0:T(8,128)(2,1)S(1)} %get-tuple-element.91.refs_0_), channel_id=1, source_target_pairs={{0,2},{1,3},{2,0},{3,1},{4,6},{5,7},{6,4},{7,5},{8,10},{9,11},{10,... | collective-permute-start | bytes 835592 | tf_op jit(solution)/shard_map/ppermute | solution.py:38
  48.0 14.5 %collective-permute-start.12 = (bf16[64,2176]{1,0:T(8,128)(2,1)S(1)}, bf16[64,2176]{1,0:T(8,128)(2,1)S(1)}, u32[]{:S(2)}, u32[]{:S(2)}) collective-permute-start(bf16[64,2176]{1,0:T(8,128)(2,1)S(1)} %get-tuple-element.91.refs_0_), channel_id=1, source_target_pairs={{0,1},{1,0},{2,3},{3,2},{4,5},{5,4},{6,7},{7,6},{8,9},{9,8},{10,11... | collective-permute-start | bytes 835592 | tf_op jit(solution)/shard_map/ppermute | solution.py:38
  49.5 13.4 %collective-permute-start.11 = (bf16[64,2176]{1,0:T(8,128)(2,1)S(1)}, bf16[64,2176]{1,0:T(8,128)(2,1)S(1)}, u32[]{:S(2)}, u32[]{:S(2)}) collective-permute-start(bf16[64,2176]{1,0:T(8,128)(2,1)S(1)} %get-tuple-element.91.refs_0_), channel_id=1, source_target_pairs={{0,16},{8,24},{16,0},{24,8},{1,17},{9,25},{17,1},{25,9},{2,18},{10... | collective-permute-start | bytes 835592 | tf_op jit(solution)/shard_map/ppermute | solution.py:38
  60.9 10.5 %collective-permute-start.20 = (bf16[64,2176]{1,0:T(8,128)(2,1)S(1)}, bf16[64,2176]{1,0:T(8,128)(2,1)S(1)}, u32[]{:S(2)}, u32[]{:S(2)}) collective-permute-start(bf16[64,2176]{1,0:T(8,128)(2,1)S(1)} %collective-permute-done.18.refs_8_), channel_id=1, source_target_pairs={{0,1},{1,0},{2,3},{3,2},{4,5},{5,4},{6,7},{7,6},{8,9},{9,8},{10,11... | collective-permute-start | bytes 835592 | tf_op jit(solution)/shard_map/ppermute | solution.py:38
  62.4 14.1 %collective-permute-start.16 = (bf16[64,2176]{1,0:T(8,128)(2,1)S(1)}, bf16[64,2176]{1,0:T(8,128)(2,1)S(1)}, u32[]{:S(2)}, u32[]{:S(2)}) collective-permute-start(bf16[64,2176]{1,0:T(8,128)(2,1)S(1)} %collective-permute-done.14.refs_4_), channel_id=1, source_target_pairs={{0,1},{1,0},{2,3},{3,2},{4,5},{5,4},{6,7},{7,6},{8,9},{9,8},{10,11... | collective-permute-start | bytes 835592 | tf_op jit(solution)/shard_map/ppermute | solution.py:38
  63.0 14.1 %collective-permute-start.13 = (bf16[64,2176]{1,0:T(8,128)(2,1)S(1)}, bf16[64,2176]{1,0:T(8,128)(2,1)S(1)}, u32[]{:S(2)}, u32[]{:S(2)}) collective-permute-start(bf16[64,2176]{1,0:T(8,128)(2,1)S(1)} %collective-permute-done.12.refs_2_), channel_id=1, source_target_pairs={{0,16},{8,24},{16,0},{24,8},{1,17},{9,25},{17,1},{25,9},{2,18},{10... | collective-permute-start | bytes 835592 | tf_op jit(solution)/shard_map/ppermute | solution.py:38
  67.9 14.7 %collective-permute-start.21 = (bf16[64,2176]{1,0:T(8,128)(2,1)S(1)}, bf16[64,2176]{1,0:T(8,128)(2,1)}, u32[]{:S(2)}, u32[]{:S(2)}) collective-permute-start(bf16[64,2176]{1,0:T(8,128)(2,1)S(1)} %collective-permute-done.19.refs_9_), channel_id=1, source_target_pairs={{0,1},{1,0},{2,3},{3,2},{4,5},{5,4},{6,7},{7,6},{8,9},{9,8},{10,11... | collective-permute-start | bytes 835592 | tf_op jit(solution)/shard_map/ppermute | solution.py:38
  69.6 14.5 %collective-permute-start.15 = (bf16[64,2176]{1,0:T(8,128)(2,1)S(1)}, bf16[64,2176]{1,0:T(8,128)(2,1)}, u32[]{:S(2)}, u32[]{:S(2)}) collective-permute-start(bf16[64,2176]{1,0:T(8,128)(2,1)S(1)} %collective-permute-done.14.refs_4_), channel_id=1, source_target_pairs={{0,16},{8,24},{16,0},{24,8},{1,17},{9,25},{17,1},{25,9},{2,18},{10... | collective-permute-start | bytes 835592 | tf_op jit(solution)/shard_map/ppermute | solution.py:38
  71.5 15.5 %collective-permute-start.24 = (bf16[64,2176]{1,0:T(8,128)(2,1)S(1)}, bf16[64,2176]{1,0:T(8,128)(2,1)}, u32[]{:S(2)}, u32[]{:S(2)}) collective-permute-start(bf16[64,2176]{1,0:T(8,128)(2,1)S(1)} %collective-permute-done.22.refs_12_), channel_id=1, source_target_pairs={{0,1},{1,0},{2,3},{3,2},{4,5},{5,4},{6,7},{7,6},{8,9},{9,8},{10,11... | collective-permute-start | bytes 835592 | tf_op jit(solution)/shard_map/ppermute | solution.py:38
  76.5 10.5 %collective-permute-start.23 = (bf16[64,2176]{1,0:T(8,128)(2,1)S(1)}, bf16[64,2176]{1,0:T(8,128)(2,1)}, u32[]{:S(2)}, u32[]{:S(2)}) collective-permute-start(bf16[64,2176]{1,0:T(8,128)(2,1)S(1)} %collective-permute-done.22.refs_12_), channel_id=1, source_target_pairs={{0,16},{8,24},{16,0},{24,8},{1,17},{9,25},{17,1},{25,9},{2,18},{10... | collective-permute-start | bytes 835592 | tf_op jit(solution)/shard_map/ppermute | solution.py:38
  77.0 9.9 %collective-permute-start.17 = (bf16[64,2176]{1,0:T(8,128)(2,1)S(1)}, bf16[64,2176]{1,0:T(8,128)(2,1)}, u32[]{:S(2)}, u32[]{:S(2)}) collective-permute-start(bf16[64,2176]{1,0:T(8,128)(2,1)S(1)} %collective-permute-done.13.refs_3_), channel_id=1, source_target_pairs={{0,2},{1,3},{2,0},{3,1},{4,6},{5,7},{6,4},{7,5},{8,10},{9,11},{10,... | collective-permute-start | bytes 835592 | tf_op jit(solution)/shard_map/ppermute | solution.py:38
  107.4 13.7 %collective-permute-start.26 = (bf16[64,2048]{1,0:T(8,128)(2,1)S(1)}, bf16[64,2048]{1,0:T(8,128)(2,1)S(1)}, u32[]{:S(2)}, u32[]{:S(2)}) collective-permute-start(bf16[64,2048]{1,0:T(8,128)(2,1)S(1)} %get-tuple-element.99), channel_id=1, source_target_pairs={{0,16},{8,24},{16,0},{24,8},{1,17},{9,25},{17,1},{25,9},{2,18},{10... | collective-permute-start | bytes 786440 | tf_op jit(solution)/shard_map/ppermute | solution.py:38
  108.3 13.1 %collective-permute-start.27 = (bf16[64,2048]{1,0:T(8,128)(2,1)S(1)}, bf16[64,2048]{1,0:T(8,128)(2,1)S(1)}, u32[]{:S(2)}, u32[]{:S(2)}) collective-permute-start(bf16[64,2048]{1,0:T(8,128)(2,1)S(1)} %get-tuple-element.100), channel_id=1, source_target_pairs={{0,1},{1,0},{2,3},{3,2},{4,5},{5,4},{6,7},{7,6},{8,9},{9,8},{10,11... | collective-permute-start | bytes 786440 | tf_op jit(solution)/shard_map/ppermute | solution.py:38
  113.8 11.9 %collective-permute-start.32 = (bf16[64,2048]{1,0:T(8,128)(2,1)S(1)}, bf16[64,2048]{1,0:T(8,128)(2,1)S(1)}, u32[]{:S(2)}, u32[]{:S(2)}) collective-permute-start(bf16[64,2048]{1,0:T(8,128)(2,1)S(1)} %add_convert_fusion.4), channel_id=1, source_target_pairs={{0,2},{1,3},{2,0},{3,1},{4,6},{5,7},{6,4},{7,5},{8,10},{9,11},{10,... | collective-permute-start | bytes 786440 | tf_op jit(solution)/shard_map/ppermute | solution.py:38
  117.7 10.2 %collective-permute-start.31 = (bf16[64,2048]{1,0:T(8,128)(2,1)S(1)}, bf16[64,2048]{1,0:T(8,128)(2,1)S(1)}, u32[]{:S(2)}, u32[]{:S(2)}) collective-permute-start(bf16[64,2048]{1,0:T(8,128)(2,1)S(1)} %add_convert_fusion.5), channel_id=1, source_target_pairs={{0,17},{1,16},{2,19},{3,18},{4,21},{5,20},{6,23},{7,22},{8,25},{9,... | collective-permute-start | bytes 786440 | tf_op jit(solution)/shard_map/ppermute | solution.py:44
  117.7 20.2 %collective-permute-start.34 = (bf16[64,2048]{1,0:T(8,128)(2,1)S(1)}, bf16[64,2048]{1,0:T(8,128)(2,1)S(1)}, u32[]{:S(2)}, u32[]{:S(2)}) collective-permute-start(bf16[64,2048]{1,0:T(8,128)(2,1)S(1)} %get-tuple-element.118), channel_id=1, source_target_pairs={{0,16},{8,24},{16,0},{24,8},{1,17},{9,25},{17,1},{25,9},{2,18},{10... | collective-permute-start | bytes 786440 | tf_op jit(solution)/shard_map/ppermute | solution.py:38
  121.1 16.9 %collective-permute-start.35 = (bf16[64,2048]{1,0:T(8,128)(2,1)S(1)}, bf16[64,2048]{1,0:T(8,128)(2,1)S(1)}, u32[]{:S(2)}, u32[]{:S(2)}) collective-permute-start(bf16[64,2048]{1,0:T(8,128)(2,1)S(1)} %get-tuple-element.119), channel_id=1, source_target_pairs={{0,1},{1,0},{2,3},{3,2},{4,5},{5,4},{6,7},{7,6},{8,9},{9,8},{10,11... | collective-permute-start | bytes 786440 | tf_op jit(solution)/shard_map/ppermute | solution.py:38
  121.4 9.9 %collective-permute-start.36 = (bf16[64,2048]{1,0:T(8,128)(2,1)S(1)}, bf16[64,2048]{1,0:T(8,128)(2,1)S(1)}, u32[]{:S(2)}, u32[]{:S(2)}) collective-permute-start(bf16[64,2048]{1,0:T(8,128)(2,1)S(1)} %get-tuple-element.121), channel_id=1, source_target_pairs={{0,2},{1,3},{2,0},{3,1},{4,6},{5,7},{6,4},{7,5},{8,10},{9,11},{10,... | collective-permute-start | bytes 786440 | tf_op jit(solution)/shard_map/ppermute | solution.py:38
  (27 other events, 250.1 us)

commit v5 on v4

--- a/solution.py
+++ b/solution.py
@@ -14,13 +14,15 @@
 TOPK = 8
 MASKED = -1e30
 EXPERT_MIB = 46
-GATHER = ("c2", "c1", "y0", "x0", "x2", "c3", "y2", "y1", "d0", "d2", "x1", "y3", "x3", "d1", "d3")
+GATHER = ("c2", "c1", "d0", "y0", "x0", "c3", "d2", "x2", "y2", "y1", "x1", "d1", "y3", "x3", "d3")
 TAKE = tuple(range(16))
 CALL = 4
 HOLD = 3
 GATE = 0
 WAIT = 0
-DIRECT = ()
+DIRECT = (0,)
+RELAY = 0
+FIRST = -1
 NEAR_MIB = 14
 FAR_MIB = 14
 NORM_MIB = 16
@@ -259,22 +261,24 @@
     steps = [(kind, kz) for kz in range(planes) for kind in "cxyd" if (kind, kz) not in at]
     if planes == 4:
         steps = [(step[0], int(step[1])) for step in GATHER]
-    for kind, kz in steps:
+    for i, (kind, kz) in enumerate(steps):
+        if i == FIRST:
+            at = lax.optimization_barrier(at)
+        near = kz > 1 and kz % 2
         if kind == "c":
-            near = kz > 1 and kz % 2
             got = [swap(at["c", kz - 1][0], "exp", 2) if near else swap(rows, "exp", 2 * kz)]
         elif kind == "x":
             got = [swap(at["c", kz][0], "seq", 2 * kx) for kx in range(1, sides)]
         elif kind == "y":
             got = [swap(at["c", kz][0], "exp", 1)]
+        elif kz in DIRECT:
+            got = [swap_both(at["c", kz][0], 2 * kx, 1) for kx in range(1, sides)]
         elif kz % 2:
             got = [swap(block, "exp", 2) for block in at["d", kz - 1]]
-        elif kz in DIRECT:
-            got = [swap_both(at["c", kz][0], 2 * kx, 1) for kx in range(1, sides)]
-        elif kz % 4 == 0:
-            got = [swap(at["y", kz][0], "seq", 2 * kx) for kx in range(1, sides)]
+        elif RELAY:
+            got = [swap(block, "exp", 1) for block in at["x", kz]]
         else:
-            got = [swap(block, "exp", 1) for block in at["x", kz]]
+            got = [swap(block, "exp", 2 * kz) for block in at["d", 0]]
         at[kind, kz] = got
     return [[block for kind in "cxyd" for block in at[kind, kz]] for kz in range(planes)]
 

time: 144 us -> 143 us (level)
  waiting for transfers between devices: 55.6 us -> 47.4 us
  starting transfers between devices: 52 us -> 59.2 us
    ppermute x39 -> x38, waiting for transfers between devices: 52.4 us -> 46 us  [swap(): lax.ppermute(rows, axis, [(i, i ^ bits) for i in range(lax.axis_size(axis...]
    ppermute x2 -> x3, starting transfers between devices: 2.19 us -> 7.11 us  [swap_both(): lax.ppermute(rows, ('seq', 'exp'), [(i, i ^ bits) for i in range(nseq * n...]
    ppermute x39 -> x38, starting transfers between devices: 49.9 us -> 52.1 us  [swap(): lax.ppermute(rows, axis, [(i, i ^ bits) for i in range(lax.axis_size(axis...]
    ppermute x2 -> x3, waiting for transfers between devices: 3.2 us -> 1.43 us  [swap_both(): lax.ppermute(rows, ('seq', 'exp'), [(i, i ^ bits) for i in range(nseq * n...]
  transfers between devices with their start and end apart: 41 -> 41, of which waited for: 22 -> 21; matrix products, arithmetic and copies ran while one was open for 0% -> 0% of each run, Pallas kernels for 7% -> 7%
where the time goes in v5:
time: 143 us
  starting transfers between devices  59.2 us (41%)
  waiting for transfers between devices  47.4 us (33%)
  Pallas kernels  29.9 us (21%)
  local copies, waits for them, and re-layouts  4.1 us (3%)
  other arithmetic  1.63 us (1%)
    ppermute x38, starting transfers between devices, swap(): lax.ppermute(rows, axis, [(i, i ^ bits) for i in range(lax.axis_size(axis...  52.1 us
    ppermute x38, waiting for transfers between devices, swap(): lax.ppermute(rows, axis, [(i, i ^ bits) for i in range(lax.axis_size(axis...  46 us
    pallas_call x1, Pallas kernels, expert_terms(): pl.pallas_call(functools.partial(expert_kernel, layouts, take, per_group,...  13.6 us
    ppermute x3, starting transfers between devices, swap_both(): lax.ppermute(rows, ('seq', 'exp'), [(i, i ^ bits) for i in range(nseq * n...  7.11 us
    pallas_call x1, Pallas kernels, project(): pl.pallas_call(functools.partial(far_kernel, nseq, ks), out_shape=[jax.Sh...  6.53 us
    pallas_call x1, Pallas kernels, project_attention(): pl.pallas_call(functools.partial(near_kernel, nseq), out_shape=[jax.Shape...  4.71 us
    pallas_call x2, Pallas kernels, pack(): pl.pallas_call(functools.partial(pack_kernel, nseq, widths), out_shape=[s...  4.46 us
    unnamed x20, local copies, waits for them, and re-layouts  4.08 us
  transfers between devices with their start and end apart: 41, of which 21 were waited for; matrix products, arithmetic and copies ran while one was open for 0% of the time, Pallas kernels for 7%

profile of v5, /device:TPU:0, one launch (start us, length us, event | category | flops | bytes accessed | tf_op | source)
XLA Modules:
  0.0 143.1 jit_solution(18047051150883357383)
XLA Ops:
  3.2 2.6 %collective-permute-start.1 = (bf16[64,1280]{1,0:T(8,128)(2,1)}, bf16[64,1280]{1,0:T(8,128)(2,1)S(1)}, u32[]{:S(2)}, u32[]{:S(2)}) collective-permute-start(bf16[64,1280]{1,0:T(8,128)(2,1)} %get-tuple-element.68), channel_id=1, source_target_pairs={{0,16},{8,24},{16,0},{24,8},{1,17},{9,25},{17,1},{25,9},{2,18},{10... | collective-permute-start | bytes 491528 | tf_op jit(solution)/shard_map/ppermute | solution.py:40
  6.4 2.3 %pack_heads.3 = (bf16[512,256]{1,0:T(8,128)(2,1)}, bf16[512,256]{1,0:T(8,128)(2,1)}, bf16[512,256]{1,0:T(8,128)(2,1)}, bf16[512,256]{1,0:T(8,128)(2,1)}) custom-call(s32[1]{0:T(128)} %bitcast.1.me_ref, bf16[512,512]{1,0:T(8,128)(2,1)} %bitcast.21, bf16[512,512]{1,0:T(8,128)(2,1)} %bitcast.22), custom_call_target="tpu_custom_call" | custom-call | tf_op jit(solution)/shard_map/pack_heads/pallas_call | solution.py:72
  8.8 2.2 %collective-permute-done.1.refs_2_ = bf16[64,1280]{1,0:T(8,128)(2,1)S(1)} collective-permute-done((bf16[64,1280]{1,0:T(8,128)(2,1)}, bf16[64,1280]{1,0:T(8,128)(2,1)S(1)}, u32[]{:S(2)}, u32[]{:S(2)}) %collective-permute-start.1) | collective-permute-done | bytes 163872 | tf_op jit(solution)/shard_map/ppermute | solution.py:40
  20.2 4.7 %attend_near.1 = (f32[256,128]{1,0:T(8,128)S(1)}, f32[256,128]{1,0:T(8,128)S(1)}, f32[256,1024]{1,0:T(8,128)S(1)}) custom-call(s32[1]{0:T(128)} %bitcast.1.me_ref, s32[1]{0:T(128)S(6)} %copy.15.len_ref, bf16[64,1280]{1,0:T(8,128)(2,1)S(1)} %copy-done.2, bf16[64,1280]{1,0:T(8,128)(2,1)S(1)} %collective-permute-done.refs_1_, ...), custom_call_target="tpu_custom_call" | custom-call | tf_op jit(solution)/shard_map/attend_near/pallas_call | solution.py:179
  25.5 6.5 %attend_far.1 = (f32[128,2048]{1,0:T(8,128)S(1)}, bf16[128,2048]{1,0:T(8,128)(2,1)S(1)}) custom-call(s32[1]{0:T(128)} %bitcast.1.me_ref, s32[1]{0:T(128)S(6)} %copy.15.len_ref, bf16[64,1280]{1,0:T(8,128)(2,1)S(1)} %copy-done.2, bf16[64,1280]{1,0:T(8,128)(2,1)S(1)} %collective-permute-done.refs_1_, bf16[64,1280]{1,0:T(8,128)(2,1)S(1)} %collective-permute-done.1.refs_2_, ...), custom_call_target="tpu_custom_call" | custom-call | tf_op jit(solution)/shard_map/attend_far/pallas_call | solution.py:194
  36.1 6.9 %collective-permute-done.9.refs_2_ = bf16[64,2048]{1,0:T(8,128)(2,1)S(1)} collective-permute-done((bf16[64,2048]{1,0:T(8,128)(2,1)S(1)}, bf16[64,2048]{1,0:T(8,128)(2,1)S(1)}, u32[]{:S(2)}, u32[]{:S(2)}) %collective-permute-start.9) | collective-permute-done | bytes 262176 | tf_op jit(solution)/shard_map/ppermute | solution.py:40
  43.6 2.8 %collective-permute-start.18 = (bf16[64,2176]{1,0:T(8,128)(2,1)S(1)}, bf16[64,2176]{1,0:T(8,128)(2,1)S(1)}, u32[]{:S(2)}, u32[]{:S(2)}) collective-permute-start(bf16[64,2176]{1,0:T(8,128)(2,1)S(1)} %get-tuple-element.91.refs_0_), channel_id=1, source_target_pairs={{0,4},{1,5},{2,6},{3,7},{4,0},{5,1},{6,2},{7,3},{8,12},{9,13},{10,... | collective-permute-start | bytes 835592 | tf_op jit(solution)/shard_map/ppermute | solution.py:40
  48.0 2.5 %collective-permute-start.13 = (bf16[64,2176]{1,0:T(8,128)(2,1)S(1)}, bf16[64,2176]{1,0:T(8,128)(2,1)S(1)}, u32[]{:S(2)}, u32[]{:S(2)}) collective-permute-start(bf16[64,2176]{1,0:T(8,128)(2,1)S(1)} %get-tuple-element.91.refs_0_), channel_id=1, source_target_pairs={{0,17},{1,16},{2,19},{3,18},{4,21},{5,20},{6,23},{7,22},{8,25},{9,... | collective-permute-start | bytes 835592 | tf_op jit(solution)/shard_map/ppermute | solution.py:46
  51.5 7.3 %collective-permute-done.18.refs_8_ = bf16[64,2176]{1,0:T(8,128)(2,1)S(1)} collective-permute-done((bf16[64,2176]{1,0:T(8,128)(2,1)S(1)}, bf16[64,2176]{1,0:T(8,128)(2,1)S(1)}, u32[]{:S(2)}, u32[]{:S(2)}) %collective-permute-start.18) | collective-permute-done | bytes 278560 | tf_op jit(solution)/shard_map/ppermute | solution.py:40
  64.0 2.4 %collective-permute-start.21 = (bf16[64,2176]{1,0:T(8,128)(2,1)S(1)}, bf16[64,2176]{1,0:T(8,128)(2,1)}, u32[]{:S(2)}, u32[]{:S(2)}) collective-permute-start(bf16[64,2176]{1,0:T(8,128)(2,1)S(1)} %collective-permute-done.13.refs_3_), channel_id=1, source_target_pairs={{0,4},{1,5},{2,6},{3,7},{4,0},{5,1},{6,2},{7,3},{8,12},{9,13},{10,... | collective-permute-start | bytes 835592 | tf_op jit(solution)/shard_map/ppermute | solution.py:40
  66.3 4.4 %collective-permute-start.15 = (bf16[64,2176]{1,0:T(8,128)(2,1)S(1)}, bf16[64,2176]{1,0:T(8,128)(2,1)}, u32[]{:S(2)}, u32[]{:S(2)}) collective-permute-start(bf16[64,2176]{1,0:T(8,128)(2,1)S(1)} %collective-permute-done.14.refs_4_), channel_id=1, source_target_pairs={{0,16},{8,24},{16,0},{24,8},{1,17},{9,25},{17,1},{25,9},{2,18},{10... | collective-permute-start | bytes 835592 | tf_op jit(solution)/shard_map/ppermute | solution.py:40
  72.0 3.0 %collective-permute-done.16.refs_6_ = bf16[64,2176]{1,0:T(8,128)(2,1)S(1)} collective-permute-done((bf16[64,2176]{1,0:T(8,128)(2,1)S(1)}, bf16[64,2176]{1,0:T(8,128)(2,1)S(1)}, u32[]{:S(2)}, u32[]{:S(2)}) %collective-permute-start.16) | collective-permute-done | bytes 278560 | tf_op jit(solution)/shard_map/ppermute | solution.py:40
  76.5 2.8 %collective-permute-done.21.refs_11_ = bf16[64,2176]{1,0:T(8,128)(2,1)} collective-permute-done((bf16[64,2176]{1,0:T(8,128)(2,1)S(1)}, bf16[64,2176]{1,0:T(8,128)(2,1)}, u32[]{:S(2)}, u32[]{:S(2)}) %collective-permute-start.21) | collective-permute-done | bytes 278560 | tf_op jit(solution)/shard_map/ppermute | solution.py:40
  79.4 2.4 %collective-permute-done.17.refs_7_ = bf16[64,2176]{1,0:T(8,128)(2,1)} collective-permute-done((bf16[64,2176]{1,0:T(8,128)(2,1)S(1)}, bf16[64,2176]{1,0:T(8,128)(2,1)}, u32[]{:S(2)}, u32[]{:S(2)}) %collective-permute-start.17) | collective-permute-done | bytes 278560 | tf_op jit(solution)/shard_map/ppermute | solution.py:40
  82.4 4.9 %collective-permute-done.25.refs_15_ = bf16[64,2176]{1,0:T(8,128)(2,1)} collective-permute-done((bf16[64,2176]{1,0:T(8,128)(2,1)}, bf16[64,2176]{1,0:T(8,128)(2,1)}, u32[]{:S(2)}, u32[]{:S(2)}) %collective-permute-start.25) | collective-permute-done | bytes 278560 | tf_op jit(solution)/shard_map/ppermute | solution.py:40
  87.3 13.6 %experts.1 = (bf16[64,2048]{1,0:T(8,128)(2,1)S(1)}, bf16[64,2048]{1,0:T(8,128)(2,1)S(1)}, bf16[64,2048]{1,0:T(8,128)(2,1)S(1)}, bf16[64,2048]{1,0:T(8,128)(2,1)S...) custom-call(s32[2]{0:T(128)S(1)} %pad_add_fusion.mine_ref, ...), custom_call_target="tpu_custom_call" | custom-call | flops 7247757312 | bytes 6291456 | tf_op jit(solution)/shard_map/experts/pallas_call | solution.py:410
  105.1 2.3 %collective-permute-done.28 = bf16[64,2048]{1,0:T(8,128)(2,1)S(1)} collective-permute-done((bf16[64,2048]{1,0:T(8,128)(2,1)S(1)}, bf16[64,2048]{1,0:T(8,128)(2,1)S(1)}, u32[]{:S(2)}, u32[]{:S(2)}) %collective-permute-start.28) | collective-permute-done | bytes 262176 | tf_op jit(solution)/shard_map/ppermute | solution.py:40
  107.4 2.9 %collective-permute-done.29 = bf16[64,2048]{1,0:T(8,128)(2,1)S(1)} collective-permute-done((bf16[64,2048]{1,0:T(8,128)(2,1)S(1)}, bf16[64,2048]{1,0:T(8,128)(2,1)S(1)}, u32[]{:S(2)}, u32[]{:S(2)}) %collective-permute-start.29) | collective-permute-done | bytes 262176 | tf_op jit(solution)/shard_map/ppermute | solution.py:40
  110.7 2.8 %collective-permute-start.32 = (bf16[64,2048]{1,0:T(8,128)(2,1)S(1)}, bf16[64,2048]{1,0:T(8,128)(2,1)S(1)}, u32[]{:S(2)}, u32[]{:S(2)}) collective-permute-start(bf16[64,2048]{1,0:T(8,128)(2,1)S(1)} %add_convert_fusion.4), channel_id=1, source_target_pairs={{0,2},{1,3},{2,0},{3,1},{4,6},{5,7},{6,4},{7,5},{8,10},{9,11},{10,... | collective-permute-start | bytes 786440 | tf_op jit(solution)/shard_map/ppermute | solution.py:40
  117.5 3.8 %collective-permute-start.36 = (bf16[64,2048]{1,0:T(8,128)(2,1)S(1)}, bf16[64,2048]{1,0:T(8,128)(2,1)S(1)}, u32[]{:S(2)}, u32[]{:S(2)}) collective-permute-start(bf16[64,2048]{1,0:T(8,128)(2,1)S(1)} %get-tuple-element.121), channel_id=1, source_target_pairs={{0,2},{1,3},{2,0},{3,1},{4,6},{5,7},{6,4},{7,5},{8,10},{9,11},{10,... | collective-permute-start | bytes 786440 | tf_op jit(solution)/shard_map/ppermute | solution.py:40
  121.4 2.7 %collective-permute-start.38 = (bf16[64,2048]{1,0:T(8,128)(2,1)S(1)}, bf16[64,2048]{1,0:T(8,128)(2,1)S(1)}, u32[]{:S(2)}, u32[]{:S(2)}) collective-permute-start(bf16[64,2048]{1,0:T(8,128)(2,1)S(1)} %get-tuple-element.123), channel_id=1, source_target_pairs={{0,16},{8,24},{16,0},{24,8},{1,17},{9,25},{17,1},{25,9},{2,18},{10... | collective-permute-start | bytes 786440 | tf_op jit(solution)/shard_map/ppermute | solution.py:40
  125.7 5.9 %collective-permute-start.33 = (bf16[64,2048]{1,0:T(8,128)(2,1)S(1)}, bf16[64,2048]{1,0:T(8,128)(2,1)S(1)}, u32[]{:S(2)}, u32[]{:S(2)}) collective-permute-start(bf16[64,2048]{1,0:T(8,128)(2,1)S(1)} %add_convert_fusion.3), channel_id=1, source_target_pairs={{0,4},{1,5},{2,6},{3,7},{4,0},{5,1},{6,2},{7,3},{8,12},{9,13},{10,... | collective-permute-start | bytes 786440 | tf_op jit(solution)/shard_map/ppermute | solution.py:40
  131.7 3.9 %collective-permute-start.37 = (bf16[64,2048]{1,0:T(8,128)(2,1)S(1)}, bf16[64,2048]{1,0:T(8,128)(2,1)S(1)}, u32[]{:S(2)}, u32[]{:S(2)}) collective-permute-start(bf16[64,2048]{1,0:T(8,128)(2,1)S(1)} %add_convert_fusion.2), channel_id=1, source_target_pairs={{0,17},{1,16},{2,19},{3,18},{4,21},{5,20},{6,23},{7,22},{8,25},{9,... | collective-permute-start | bytes 786440 | tf_op jit(solution)/shard_map/ppermute | solution.py:46
  136.1 2.4 %collective-permute-done.33 = bf16[64,2048]{1,0:T(8,128)(2,1)S(1)} collective-permute-done((bf16[64,2048]{1,0:T(8,128)(2,1)S(1)}, bf16[64,2048]{1,0:T(8,128)(2,1)S(1)}, u32[]{:S(2)}, u32[]{:S(2)}) %collective-permute-start.33) | collective-permute-done | bytes 262176 | tf_op jit(solution)/shard_map/ppermute | solution.py:40
  (93 shorter events, 44.3 us)
Async XLA Ops:
  0.0 14.0 %collective-permute-start.3 = (bf16[1,2048,768]{2,1,0:T(8,128)(2,1)}, bf16[1,2048,768]{2,1,0:T(8,128)(2,1)}, u32[]{:S(2)}, u32[]{:S(2)}) collective-permute-start(bf16[1,2048,768]{2,1,0:T(8,128)(2,1)} %refs_16_), channel_id=1, source_target_pairs={{0,8},{8,0},{16,24},{24,16},{1,9},{9,1},{17,25},{25,17},{2,10},{10... | collective-permute-start | bytes 9437192 | tf_op jit(solution)/shard_map/ppermute | solution.py:40
  0.5 13.5 %collective-permute-start.4 = (bf16[1,2048,768]{2,1,0:T(8,128)(2,1)}, bf16[1,2048,768]{2,1,0:T(8,128)(2,1)}, u32[]{:S(2)}, u32[]{:S(2)}) collective-permute-start(bf16[1,2048,768]{2,1,0:T(8,128)(2,1)} %refs_17_), channel_id=1, source_target_pairs={{0,8},{8,0},{16,24},{24,16},{1,9},{9,1},{17,25},{25,17},{2,10},{10... | collective-permute-start | bytes 9437192 | tf_op jit(solution)/shard_map/ppermute | solution.py:40
  11.0 13.9 %collective-permute-start.5 = (bf16[512,256]{1,0:T(8,128)(2,1)}, bf16[512,256]{1,0:T(8,128)(2,1)S(1)}, u32[]{:S(2)}, u32[]{:S(2)}) collective-permute-start(bf16[512,256]{1,0:T(8,128)(2,1)} %get-tuple-element.76), channel_id=1, source_target_pairs={{0,16},{8,24},{16,0},{24,8},{1,17},{9,25},{17,1},{25,9},{2,18},{10... | collective-permute-start | bytes 786440 | tf_op jit(solution)/shard_map/ppermute | solution.py:40
  14.0 11.5 %collective-permute-start.6 = (bf16[512,256]{1,0:T(8,128)(2,1)}, bf16[512,256]{1,0:T(8,128)(2,1)S(1)}, u32[]{:S(2)}, u32[]{:S(2)}) collective-permute-start(bf16[512,256]{1,0:T(8,128)(2,1)} %get-tuple-element.77), channel_id=1, source_target_pairs={{0,24},{8,16},{16,8},{24,0},{1,25},{9,17},{17,9},{25,1},{2,26},{10... | collective-permute-start | bytes 786440 | tf_op jit(solution)/shard_map/ppermute | solution.py:40
  43.6 15.2 %collective-permute-start.18 = (bf16[64,2176]{1,0:T(8,128)(2,1)S(1)}, bf16[64,2176]{1,0:T(8,128)(2,1)S(1)}, u32[]{:S(2)}, u32[]{:S(2)}) collective-permute-start(bf16[64,2176]{1,0:T(8,128)(2,1)S(1)} %get-tuple-element.91.refs_0_), channel_id=1, source_target_pairs={{0,4},{1,5},{2,6},{3,7},{4,0},{5,1},{6,2},{7,3},{8,12},{9,13},{10,... | collective-permute-start | bytes 835592 | tf_op jit(solution)/shard_map/ppermute | solution.py:40
  46.4 13.0 %collective-permute-start.14 = (bf16[64,2176]{1,0:T(8,128)(2,1)S(1)}, bf16[64,2176]{1,0:T(8,128)(2,1)S(1)}, u32[]{:S(2)}, u32[]{:S(2)}) collective-permute-start(bf16[64,2176]{1,0:T(8,128)(2,1)S(1)} %get-tuple-element.91.refs_0_), channel_id=1, source_target_pairs={{0,2},{1,3},{2,0},{3,1},{4,6},{5,7},{6,4},{7,5},{8,10},{9,11},{10,... | collective-permute-start | bytes 835592 | tf_op jit(solution)/shard_map/ppermute | solution.py:40
  48.0 13.0 %collective-permute-start.13 = (bf16[64,2176]{1,0:T(8,128)(2,1)S(1)}, bf16[64,2176]{1,0:T(8,128)(2,1)S(1)}, u32[]{:S(2)}, u32[]{:S(2)}) collective-permute-start(bf16[64,2176]{1,0:T(8,128)(2,1)S(1)} %get-tuple-element.91.refs_0_), channel_id=1, source_target_pairs={{0,17},{1,16},{2,19},{3,18},{4,21},{5,20},{6,23},{7,22},{8,25},{9,... | collective-permute-start | bytes 835592 | tf_op jit(solution)/shard_map/ppermute | solution.py:46
  50.4 12.0 %collective-permute-start.12 = (bf16[64,2176]{1,0:T(8,128)(2,1)S(1)}, bf16[64,2176]{1,0:T(8,128)(2,1)S(1)}, u32[]{:S(2)}, u32[]{:S(2)}) collective-permute-start(bf16[64,2176]{1,0:T(8,128)(2,1)S(1)} %get-tuple-element.91.refs_0_), channel_id=1, source_target_pairs={{0,1},{1,0},{2,3},{3,2},{4,5},{5,4},{6,7},{7,6},{8,9},{9,8},{10,11... | collective-permute-start | bytes 835592 | tf_op jit(solution)/shard_map/ppermute | solution.py:40
  51.0 13.0 %collective-permute-start.11 = (bf16[64,2176]{1,0:T(8,128)(2,1)S(1)}, bf16[64,2176]{1,0:T(8,128)(2,1)S(1)}, u32[]{:S(2)}, u32[]{:S(2)}) collective-permute-start(bf16[64,2176]{1,0:T(8,128)(2,1)S(1)} %get-tuple-element.91.refs_0_), channel_id=1, source_target_pairs={{0,16},{8,24},{16,0},{24,8},{1,17},{9,25},{17,1},{25,9},{2,18},{10... | collective-permute-start | bytes 835592 | tf_op jit(solution)/shard_map/ppermute | solution.py:40
  59.4 11.3 %collective-permute-start.20 = (bf16[64,2176]{1,0:T(8,128)(2,1)S(1)}, bf16[64,2176]{1,0:T(8,128)(2,1)S(1)}, u32[]{:S(2)}, u32[]{:S(2)}) collective-permute-start(bf16[64,2176]{1,0:T(8,128)(2,1)S(1)} %collective-permute-done.18.refs_8_), channel_id=1, source_target_pairs={{0,1},{1,0},{2,3},{3,2},{4,5},{5,4},{6,7},{7,6},{8,9},{9,8},{10,11... | collective-permute-start | bytes 835592 | tf_op jit(solution)/shard_map/ppermute | solution.py:40
  62.4 12.6 %collective-permute-start.16 = (bf16[64,2176]{1,0:T(8,128)(2,1)S(1)}, bf16[64,2176]{1,0:T(8,128)(2,1)S(1)}, u32[]{:S(2)}, u32[]{:S(2)}) collective-permute-start(bf16[64,2176]{1,0:T(8,128)(2,1)S(1)} %collective-permute-done.14.refs_4_), channel_id=1, source_target_pairs={{0,1},{1,0},{2,3},{3,2},{4,5},{5,4},{6,7},{7,6},{8,9},{9,8},{10,11... | collective-permute-start | bytes 835592 | tf_op jit(solution)/shard_map/ppermute | solution.py:40
  64.0 15.3 %collective-permute-start.21 = (bf16[64,2176]{1,0:T(8,128)(2,1)S(1)}, bf16[64,2176]{1,0:T(8,128)(2,1)}, u32[]{:S(2)}, u32[]{:S(2)}) collective-permute-start(bf16[64,2176]{1,0:T(8,128)(2,1)S(1)} %collective-permute-done.13.refs_3_), channel_id=1, source_target_pairs={{0,4},{1,5},{2,6},{3,7},{4,0},{5,1},{6,2},{7,3},{8,12},{9,13},{10,... | collective-permute-start | bytes 835592 | tf_op jit(solution)/shard_map/ppermute | solution.py:40
  66.3 13.0 %collective-permute-start.15 = (bf16[64,2176]{1,0:T(8,128)(2,1)S(1)}, bf16[64,2176]{1,0:T(8,128)(2,1)}, u32[]{:S(2)}, u32[]{:S(2)}) collective-permute-start(bf16[64,2176]{1,0:T(8,128)(2,1)S(1)} %collective-permute-done.14.refs_4_), channel_id=1, source_target_pairs={{0,16},{8,24},{16,0},{24,8},{1,17},{9,25},{17,1},{25,9},{2,18},{10... | collective-permute-start | bytes 835592 | tf_op jit(solution)/shard_map/ppermute | solution.py:40
  70.8 10.9 %collective-permute-start.17 = (bf16[64,2176]{1,0:T(8,128)(2,1)S(1)}, bf16[64,2176]{1,0:T(8,128)(2,1)}, u32[]{:S(2)}, u32[]{:S(2)}) collective-permute-start(bf16[64,2176]{1,0:T(8,128)(2,1)S(1)} %collective-permute-done.13.refs_3_), channel_id=1, source_target_pairs={{0,2},{1,3},{2,0},{3,1},{4,6},{5,7},{6,4},{7,5},{8,10},{9,11},{10,... | collective-permute-start | bytes 835592 | tf_op jit(solution)/shard_map/ppermute | solution.py:40
  70.8 10.9 %collective-permute-start.24 = (bf16[64,2176]{1,0:T(8,128)(2,1)S(1)}, bf16[64,2176]{1,0:T(8,128)(2,1)}, u32[]{:S(2)}, u32[]{:S(2)}) collective-permute-start(bf16[64,2176]{1,0:T(8,128)(2,1)S(1)} %collective-permute-done.22.refs_12_), channel_id=1, source_target_pairs={{0,1},{1,0},{2,3},{3,2},{4,5},{5,4},{6,7},{7,6},{8,9},{9,8},{10,11... | collective-permute-start | bytes 835592 | tf_op jit(solution)/shard_map/ppermute | solution.py:40
  102.8 13.0 %collective-permute-start.26 = (bf16[64,2048]{1,0:T(8,128)(2,1)S(1)}, bf16[64,2048]{1,0:T(8,128)(2,1)S(1)}, u32[]{:S(2)}, u32[]{:S(2)}) collective-permute-start(bf16[64,2048]{1,0:T(8,128)(2,1)S(1)} %get-tuple-element.99), channel_id=1, source_target_pairs={{0,16},{8,24},{16,0},{24,8},{1,17},{9,25},{17,1},{25,9},{2,18},{10... | collective-permute-start | bytes 786440 | tf_op jit(solution)/shard_map/ppermute | solution.py:40
  103.3 14.3 %collective-permute-start.27 = (bf16[64,2048]{1,0:T(8,128)(2,1)S(1)}, bf16[64,2048]{1,0:T(8,128)(2,1)S(1)}, u32[]{:S(2)}, u32[]{:S(2)}) collective-permute-start(bf16[64,2048]{1,0:T(8,128)(2,1)S(1)} %get-tuple-element.100), channel_id=1, source_target_pairs={{0,1},{1,0},{2,3},{3,2},{4,5},{5,4},{6,7},{7,6},{8,9},{9,8},{10,11... | collective-permute-start | bytes 786440 | tf_op jit(solution)/shard_map/ppermute | solution.py:40
  110.7 10.6 %collective-permute-start.32 = (bf16[64,2048]{1,0:T(8,128)(2,1)S(1)}, bf16[64,2048]{1,0:T(8,128)(2,1)S(1)}, u32[]{:S(2)}, u32[]{:S(2)}) collective-permute-start(bf16[64,2048]{1,0:T(8,128)(2,1)S(1)} %add_convert_fusion.4), channel_id=1, source_target_pairs={{0,2},{1,3},{2,0},{3,1},{4,6},{5,7},{6,4},{7,5},{8,10},{9,11},{10,... | collective-permute-start | bytes 786440 | tf_op jit(solution)/shard_map/ppermute | solution.py:40
  113.6 10.5 %collective-permute-start.31 = (bf16[64,2048]{1,0:T(8,128)(2,1)S(1)}, bf16[64,2048]{1,0:T(8,128)(2,1)S(1)}, u32[]{:S(2)}, u32[]{:S(2)}) collective-permute-start(bf16[64,2048]{1,0:T(8,128)(2,1)S(1)} %add_convert_fusion.5), channel_id=1, source_target_pairs={{0,17},{1,16},{2,19},{3,18},{4,21},{5,20},{6,23},{7,22},{8,25},{9,... | collective-permute-start | bytes 786440 | tf_op jit(solution)/shard_map/ppermute | solution.py:46
  114.4 21.7 %collective-permute-start.34 = (bf16[64,2048]{1,0:T(8,128)(2,1)S(1)}, bf16[64,2048]{1,0:T(8,128)(2,1)S(1)}, u32[]{:S(2)}, u32[]{:S(2)}) collective-permute-start(bf16[64,2048]{1,0:T(8,128)(2,1)S(1)} %get-tuple-element.118), channel_id=1, source_target_pairs={{0,16},{8,24},{16,0},{24,8},{1,17},{9,25},{17,1},{25,9},{2,18},{10... | collective-permute-start | bytes 786440 | tf_op jit(solution)/shard_map/ppermute | solution.py:40
  115.9 20.2 %collective-permute-start.35 = (bf16[64,2048]{1,0:T(8,128)(2,1)S(1)}, bf16[64,2048]{1,0:T(8,128)(2,1)S(1)}, u32[]{:S(2)}, u32[]{:S(2)}) collective-permute-start(bf16[64,2048]{1,0:T(8,128)(2,1)S(1)} %get-tuple-element.119), channel_id=1, source_target_pairs={{0,1},{1,0},{2,3},{3,2},{4,5},{5,4},{6,7},{7,6},{8,9},{9,8},{10,11... | collective-permute-start | bytes 786440 | tf_op jit(solution)/shard_map/ppermute | solution.py:40
  121.4 10.3 %collective-permute-start.38 = (bf16[64,2048]{1,0:T(8,128)(2,1)S(1)}, bf16[64,2048]{1,0:T(8,128)(2,1)S(1)}, u32[]{:S(2)}, u32[]{:S(2)}) collective-permute-start(bf16[64,2048]{1,0:T(8,128)(2,1)S(1)} %get-tuple-element.123), channel_id=1, source_target_pairs={{0,16},{8,24},{16,0},{24,8},{1,17},{9,25},{17,1},{25,9},{2,18},{10... | collective-permute-start | bytes 786440 | tf_op jit(solution)/shard_map/ppermute | solution.py:40
  124.1 11.5 %collective-permute-start.39 = (bf16[64,2048]{1,0:T(8,128)(2,1)S(1)}, bf16[64,2048]{1,0:T(8,128)(2,1)S(1)}, u32[]{:S(2)}, u32[]{:S(2)}) collective-permute-start(bf16[64,2048]{1,0:T(8,128)(2,1)S(1)} %get-tuple-element.124), channel_id=1, source_target_pairs={{0,1},{1,0},{2,3},{3,2},{4,5},{5,4},{6,7},{7,6},{8,9},{9,8},{10,11... | collective-permute-start | bytes 786440 | tf_op jit(solution)/shard_map/ppermute | solution.py:40
  125.7 12.8 %collective-permute-start.33 = (bf16[64,2048]{1,0:T(8,128)(2,1)S(1)}, bf16[64,2048]{1,0:T(8,128)(2,1)S(1)}, u32[]{:S(2)}, u32[]{:S(2)}) collective-permute-start(bf16[64,2048]{1,0:T(8,128)(2,1)S(1)} %add_convert_fusion.3), channel_id=1, source_target_pairs={{0,4},{1,5},{2,6},{3,7},{4,0},{5,1},{6,2},{7,3},{8,12},{9,13},{10,... | collective-permute-start | bytes 786440 | tf_op jit(solution)/shard_map/ppermute | solution.py:40
  (27 other events, 249.3 us)

commit v6 on v4

--- a/solution.py
+++ b/solution.py
@@ -14,16 +14,10 @@
 TOPK = 8
 MASKED = -1e30
 EXPERT_MIB = 46
-GATHER = ("c2", "c1", "y0", "x0", "x2", "c3", "y2", "y1", "d0", "d2", "x1", "y3", "x3", "d1", "d3")
-TAKE = tuple(range(16))
-CALL = 4
-HOLD = 3
-GATE = 0
-WAIT = 0
-DIRECT = ()
+GATHER = ("c2", "c1", "d0", "y0", "x0", "c3", "d2", "x2", "y2", "y1", "x1", "d1", "y3", "x3", "d3")
+TAKE = (3, 14, 4, 9, 13, 11, 7, 2, 12, 8, 1, 0, 15, 6, 5, 10)
 NEAR_MIB = 14
 FAR_MIB = 14
-NORM_MIB = 16
 EXP2_SCALE = math.log2(math.e) / math.sqrt(HD)
 NT = (((1,), (1,)), ((), ()))
 TN = (((0,), (0,)), ((), ()))
@@ -168,8 +162,8 @@
     caches = pack(me, (cache_keys, cache_values), (HD, HD), nseq)
     caches = {0: caches[0], 1: swap(caches[1], "seq", 1)} | dict(enumerate(caches[2:], 2))
     for k in range(2, nseq):
-        hold = (heads[k], caches[k], others if k == HOLD else [])
-        heads[k], cache, held = lax.optimization_barrier(hold)
+        held = (heads[k], caches[k], others if k == 3 else [])
+        heads[k], cache, held = lax.optimization_barrier(held)
         others = held or others
         caches[k] = swap(cache, "seq", k)
     heads = [heads[k] for k in range(nseq)]
@@ -249,7 +243,7 @@
         ],
         in_specs=[VMEM] * (4 + len(terms)),
         out_specs=[VMEM] * 2,
-        compiler_params=params(NORM_MIB),
+        compiler_params=params(16),
         name="norm_and_route",
     )(residual, *terms, gain.reshape(1, width), router.T, ids.T)
 
@@ -260,21 +254,16 @@
     if planes == 4:
         steps = [(step[0], int(step[1])) for step in GATHER]
     for kind, kz in steps:
-        if kind == "c":
-            near = kz > 1 and kz % 2
-            got = [swap(at["c", kz - 1][0], "exp", 2) if near else swap(rows, "exp", 2 * kz)]
-        elif kind == "x":
+        if kind == "x":
             got = [swap(at["c", kz][0], "seq", 2 * kx) for kx in range(1, sides)]
         elif kind == "y":
             got = [swap(at["c", kz][0], "exp", 1)]
-        elif kz % 2:
-            got = [swap(block, "exp", 2) for block in at["d", kz - 1]]
-        elif kz in DIRECT:
-            got = [swap_both(at["c", kz][0], 2 * kx, 1) for kx in range(1, sides)]
-        elif kz % 4 == 0:
-            got = [swap(at["y", kz][0], "seq", 2 * kx) for kx in range(1, sides)]
+        elif kz == 0:
+            got = [swap_both(rows, 2 * kx, 1) for kx in range(1, sides)]
+        elif kz > 1 and kz % 2:
+            got = [swap(block, "exp", 2) for block in at[kind, kz - 1]]
         else:
-            got = [swap(block, "exp", 1) for block in at["x", kz]]
+            got = [swap(block, "exp", 2 * kz) for block in at[kind, 0]]
         at[kind, kz] = got
     return [[block for kind in "cxyd" for block in at[kind, kz]] for kz in range(planes)]
 
@@ -449,8 +438,6 @@
     if later:
         over, odd_got, later = lax.optimization_barrier((over, odd_got, later))
     over = [add(even[3][at], o).astype(bf16) for at, o in zip(parts, over)]
-    if WAIT and later:
-        over, later = lax.optimization_barrier((over, later))
     even_got += [swap_both(o, 2 * i + 2, 1) for i, o in enumerate(over)]
     return add(even[0], *even_got), add(odd[0], *odd_got), later
 
@@ -460,8 +447,6 @@
     for kz in reversed(range(0, len(terms), 2)):
         even, odd, terms[:kz] = pair_sum(terms[kz], terms[kz + 1], terms[:kz], sides)
         got = swap(odd.astype(bf16), "exp", 2)
-        if kz and GATE:
-            got, terms[:kz] = lax.optimization_barrier((got, terms[:kz]))
         own += [swap(add(even, got).astype(bf16), "exp", 2 * kz)] if kz else [even, got]
     return own
 
@@ -474,10 +459,7 @@
     other = (lax.axis_index("seq") ^ 1) * nplace + lax.axis_index("exp")
     mine = jnp.stack([me, other]).astype(jnp.int32)
     blocks = gather_rows(rows, planes, sides)
-    terms = []
-    for at in range(0, planes, CALL):
-        terms += expert_terms(blocks[at : at + CALL], sides, mine, weights, cap, nexp)
-    return return_terms(terms, sides)
+    return return_terms(expert_terms(blocks, sides, mine, weights, cap, nexp), sides)
 
 
 def experts_by_device(rows, width, ids, gate_proj, up_proj, down_proj, nexp):

time: 144 us -> 140 us (0.972)
  starting transfers between devices: 52 us -> 45.4 us
  waiting for transfers between devices: 55.6 us -> 57.9 us
    ppermute x39 -> x38, starting transfers between devices: 49.9 us -> 39.5 us  [swap(): lax.ppermute(rows, axis, [(i, i ^ bits) for i in range(lax.axis_size(axis...]
    ppermute x39 -> x38, waiting for transfers between devices: 52.4 us -> 56.9 us  [swap(): lax.ppermute(rows, axis, [(i, i ^ bits) for i in range(lax.axis_size(axis...]
    ppermute x2 -> x3, starting transfers between devices: 2.19 us -> 5.83 us  [swap_both(): lax.ppermute(rows, ('seq', 'exp'), [(i, i ^ bits) for i in range(nseq * n...]
    ppermute x2 -> x3, waiting for transfers between devices: 3.2 us -> 0.93 us  [swap_both(): lax.ppermute(rows, ('seq', 'exp'), [(i, i ^ bits) for i in range(nseq * n...]
    unnamed x20 -> x24, local copies, waits for them, and re-layouts: 4.08 us -> 4.09 us
  transfers between devices with their start and end apart: 41 -> 41, of which waited for: 22 -> 24; matrix products, arithmetic and copies ran while one was open for 0% -> 0% of each run, Pallas kernels for 7% -> 7%
where the time goes in v6:
time: 140 us
  waiting for transfers between devices  57.9 us (41%)
  starting transfers between devices  45.4 us (32%)
  Pallas kernels  29.9 us (21%)
  local copies, waits for them, and re-layouts  4.11 us (3%)
  other arithmetic  1.63 us (1%)
    ppermute x38, waiting for transfers between devices, swap(): lax.ppermute(rows, axis, [(i, i ^ bits) for i in range(lax.axis_size(axis...  56.9 us
    ppermute x38, starting transfers between devices, swap(): lax.ppermute(rows, axis, [(i, i ^ bits) for i in range(lax.axis_size(axis...  39.5 us
    pallas_call x1, Pallas kernels, expert_terms(): pl.pallas_call(functools.partial(expert_kernel, layouts, take, per_group,...  13.6 us
    pallas_call x1, Pallas kernels, project(): pl.pallas_call(functools.partial(far_kernel, nseq, ks), out_shape=[jax.Sh...  6.55 us
    ppermute x3, starting transfers between devices, swap_both(): lax.ppermute(rows, ('seq', 'exp'), [(i, i ^ bits) for i in range(nseq * n...  5.83 us
    pallas_call x1, Pallas kernels, project_attention(): pl.pallas_call(functools.partial(near_kernel, nseq), out_shape=[jax.Shape...  4.72 us
    pallas_call x2, Pallas kernels, pack(): pl.pallas_call(functools.partial(pack_kernel, nseq, widths), out_shape=[s...  4.45 us
    unnamed x24, local copies, waits for them, and re-layouts  4.09 us
  transfers between devices with their start and end apart: 41, of which 24 were waited for; matrix products, arithmetic and copies ran while one was open for 0% of the time, Pallas kernels for 7%

profile of v6, /device:TPU:0, one launch (start us, length us, event | category | flops | bytes accessed | tf_op | source)
XLA Modules:
  0.0 139.7 jit_solution(4295016619766903259)
XLA Ops:
  3.2 2.6 %collective-permute-start.1 = (bf16[64,1280]{1,0:T(8,128)(2,1)}, bf16[64,1280]{1,0:T(8,128)(2,1)S(1)}, u32[]{:S(2)}, u32[]{:S(2)}) collective-permute-start(bf16[64,1280]{1,0:T(8,128)(2,1)} %get-tuple-element.68), channel_id=1, source_target_pairs={{0,16},{8,24},{16,0},{24,8},{1,17},{9,25},{17,1},{25,9},{2,18},{10... | collective-permute-start | bytes 491528 | tf_op jit(solution)/shard_map/ppermute | solution.py:32
  6.4 2.3 %pack_heads.3 = (bf16[512,256]{1,0:T(8,128)(2,1)}, bf16[512,256]{1,0:T(8,128)(2,1)}, bf16[512,256]{1,0:T(8,128)(2,1)}, bf16[512,256]{1,0:T(8,128)(2,1)}) custom-call(s32[1]{0:T(128)} %bitcast.1.me_ref, bf16[512,512]{1,0:T(8,128)(2,1)} %bitcast.21, bf16[512,512]{1,0:T(8,128)(2,1)} %bitcast.22), custom_call_target="tpu_custom_call" | custom-call | tf_op jit(solution)/shard_map/pack_heads/pallas_call | solution.py:64
  8.8 2.2 %collective-permute-done.1.refs_2_ = bf16[64,1280]{1,0:T(8,128)(2,1)S(1)} collective-permute-done((bf16[64,1280]{1,0:T(8,128)(2,1)}, bf16[64,1280]{1,0:T(8,128)(2,1)S(1)}, u32[]{:S(2)}, u32[]{:S(2)}) %collective-permute-start.1) | collective-permute-done | bytes 163872 | tf_op jit(solution)/shard_map/ppermute | solution.py:32
  16.1 2.2 %copy-done = bf16[1024,2048]{1,0:T(8,128)(2,1)S(1)} copy-done((bf16[1024,2048]{1,0:T(8,128)(2,1)S(1)}, bf16[1024,2048]{1,0:T(8,128)(2,1)}, u32[]{:S(2)}) %copy-start) | copy-done | bytes 4194328
  20.2 4.7 %attend_near.1 = (f32[256,128]{1,0:T(8,128)S(1)}, f32[256,128]{1,0:T(8,128)S(1)}, f32[256,1024]{1,0:T(8,128)S(1)}) custom-call(s32[1]{0:T(128)} %bitcast.1.me_ref, s32[1]{0:T(128)S(6)} %copy.15.len_ref, bf16[64,1280]{1,0:T(8,128)(2,1)S(1)} %copy-done.2, bf16[64,1280]{1,0:T(8,128)(2,1)S(1)} %collective-permute-done.refs_1_, ...), custom_call_target="tpu_custom_call" | custom-call | tf_op jit(solution)/shard_map/attend_near/pallas_call | solution.py:171
  25.5 6.5 %attend_far.1 = (f32[128,2048]{1,0:T(8,128)S(1)}, bf16[128,2048]{1,0:T(8,128)(2,1)S(1)}) custom-call(s32[1]{0:T(128)} %bitcast.1.me_ref, s32[1]{0:T(128)S(6)} %copy.15.len_ref, bf16[64,1280]{1,0:T(8,128)(2,1)S(1)} %copy-done.2, bf16[64,1280]{1,0:T(8,128)(2,1)S(1)} %collective-permute-done.refs_1_, bf16[64,1280]{1,0:T(8,128)(2,1)S(1)} %collective-permute-done.1.refs_2_, ...), custom_call_target="tpu_custom_call" | custom-call | tf_op jit(solution)/shard_map/attend_far/pallas_call | solution.py:186
  36.1 6.9 %collective-permute-done.9.refs_2_ = bf16[64,2048]{1,0:T(8,128)(2,1)S(1)} collective-permute-done((bf16[64,2048]{1,0:T(8,128)(2,1)S(1)}, bf16[64,2048]{1,0:T(8,128)(2,1)S(1)}, u32[]{:S(2)}, u32[]{:S(2)}) %collective-permute-start.9) | collective-permute-done | bytes 262176 | tf_op jit(solution)/shard_map/ppermute | solution.py:32
  46.9 2.6 %collective-permute-start.12 = (bf16[64,2176]{1,0:T(8,128)(2,1)S(1)}, bf16[64,2176]{1,0:T(8,128)(2,1)S(1)}, u32[]{:S(2)}, u32[]{:S(2)}) collective-permute-start(bf16[64,2176]{1,0:T(8,128)(2,1)S(1)} %get-tuple-element.91.refs_11_), channel_id=1, source_target_pairs={{0,4},{1,5},{2,6},{3,7},{4,0},{5,1},{6,2},{7,3},{8,12},{9,13},{10,... | collective-permute-start | bytes 835592 | tf_op jit(solution)/shard_map/ppermute | solution.py:32
  51.5 5.0 %collective-permute-done.15.refs_2_ = bf16[64,2176]{1,0:T(8,128)(2,1)S(1)} collective-permute-done((bf16[64,2176]{1,0:T(8,128)(2,1)S(1)}, bf16[64,2176]{1,0:T(8,128)(2,1)S(1)}, u32[]{:S(2)}, u32[]{:S(2)}) %collective-permute-start.15) | collective-permute-done | bytes 278560 | tf_op jit(solution)/shard_map/ppermute | solution.py:32
  56.5 2.4 %collective-permute-start.24 = (bf16[64,2176]{1,0:T(8,128)(2,1)S(1)}, bf16[64,2176]{1,0:T(8,128)(2,1)S(1)}, u32[]{:S(2)}, u32[]{:S(2)}) collective-permute-start(bf16[64,2176]{1,0:T(8,128)(2,1)S(1)} %collective-permute-done.15.refs_2_), channel_id=1, source_target_pairs={{0,16},{8,24},{16,0},{24,8},{1,17},{9,25},{17,1},{25,9},{2,18},{10... | collective-permute-start | bytes 835592 | tf_op jit(solution)/shard_map/ppermute | solution.py:32
  61.3 3.6 %collective-permute-done.20.refs_7_ = bf16[64,2176]{1,0:T(8,128)(2,1)S(1)} collective-permute-done((bf16[64,2176]{1,0:T(8,128)(2,1)S(1)}, bf16[64,2176]{1,0:T(8,128)(2,1)S(1)}, u32[]{:S(2)}, u32[]{:S(2)}) %collective-permute-start.20) | collective-permute-done | bytes 278560 | tf_op jit(solution)/shard_map/ppermute | solution.py:32
  66.8 4.1 %collective-permute-done.23.refs_13_ = bf16[64,2176]{1,0:T(8,128)(2,1)S(1)} collective-permute-done((bf16[64,2176]{1,0:T(8,128)(2,1)S(1)}, bf16[64,2176]{1,0:T(8,128)(2,1)S(1)}, u32[]{:S(2)}, u32[]{:S(2)}) %collective-permute-start.23) | collective-permute-done | bytes 278560 | tf_op jit(solution)/shard_map/ppermute | solution.py:32
  71.7 2.9 %collective-permute-done.25.refs_15_ = bf16[64,2176]{1,0:T(8,128)(2,1)S(1)} collective-permute-done((bf16[64,2176]{1,0:T(8,128)(2,1)S(1)}, bf16[64,2176]{1,0:T(8,128)(2,1)S(1)}, u32[]{:S(2)}, u32[]{:S(2)}) %collective-permute-start.25) | collective-permute-done | bytes 278560 | tf_op jit(solution)/shard_map/ppermute | solution.py:32
  78.0 4.2 %collective-permute-done.19.refs_6_ = bf16[64,2176]{1,0:T(8,128)(2,1)} collective-permute-done((bf16[64,2176]{1,0:T(8,128)(2,1)S(1)}, bf16[64,2176]{1,0:T(8,128)(2,1)}, u32[]{:S(2)}, u32[]{:S(2)}) %collective-permute-start.19) | collective-permute-done | bytes 278560 | tf_op jit(solution)/shard_map/ppermute | solution.py:32
  82.2 3.6 %collective-permute-done.22.refs_12_ = bf16[64,2176]{1,0:T(8,128)(2,1)} collective-permute-done((bf16[64,2176]{1,0:T(8,128)(2,1)S(1)}, bf16[64,2176]{1,0:T(8,128)(2,1)}, u32[]{:S(2)}, u32[]{:S(2)}) %collective-permute-start.22) | collective-permute-done | bytes 278560 | tf_op jit(solution)/shard_map/ppermute | solution.py:32
  85.9 13.6 %experts.1 = (bf16[64,2048]{1,0:T(8,128)(2,1)S(1)}, bf16[64,2048]{1,0:T(8,128)(2,1)S(1)}, bf16[64,2048]{1,0:T(8,128)(2,1)S(1)}, bf16[64,2048]{1,0:T(8,128)(2,1)S...) custom-call(s32[2]{0:T(128)S(1)} %pad_add_fusion.mine_ref, ...), custom_call_target="tpu_custom_call" | custom-call | flops 7247757312 | bytes 6291456 | tf_op jit(solution)/shard_map/experts/pallas_call | solution.py:395
  103.6 2.2 %collective-permute-done.28 = bf16[64,2048]{1,0:T(8,128)(2,1)S(1)} collective-permute-done((bf16[64,2048]{1,0:T(8,128)(2,1)S(1)}, bf16[64,2048]{1,0:T(8,128)(2,1)S(1)}, u32[]{:S(2)}, u32[]{:S(2)}) %collective-permute-start.28) | collective-permute-done | bytes 262176 | tf_op jit(solution)/shard_map/ppermute | solution.py:32
  105.9 2.7 %collective-permute-done.29 = bf16[64,2048]{1,0:T(8,128)(2,1)S(1)} collective-permute-done((bf16[64,2048]{1,0:T(8,128)(2,1)S(1)}, bf16[64,2048]{1,0:T(8,128)(2,1)S(1)}, u32[]{:S(2)}, u32[]{:S(2)}) %collective-permute-start.29) | collective-permute-done | bytes 262176 | tf_op jit(solution)/shard_map/ppermute | solution.py:32
  111.5 2.4 %collective-permute-start.31 = (bf16[64,2048]{1,0:T(8,128)(2,1)S(1)}, bf16[64,2048]{1,0:T(8,128)(2,1)S(1)}, u32[]{:S(2)}, u32[]{:S(2)}) collective-permute-start(bf16[64,2048]{1,0:T(8,128)(2,1)S(1)} %add_convert_fusion.5), channel_id=1, source_target_pairs={{0,17},{1,16},{2,19},{3,18},{4,21},{5,20},{6,23},{7,22},{8,25},{9,... | collective-permute-start | bytes 786440 | tf_op jit(solution)/shard_map/ppermute | solution.py:38
  115.9 2.1 %collective-permute-done.27 = bf16[64,2048]{1,0:T(8,128)(2,1)S(1)} collective-permute-done((bf16[64,2048]{1,0:T(8,128)(2,1)S(1)}, bf16[64,2048]{1,0:T(8,128)(2,1)S(1)}, u32[]{:S(2)}, u32[]{:S(2)}) %collective-permute-start.27) | collective-permute-done | bytes 262176 | tf_op jit(solution)/shard_map/ppermute | solution.py:32
  118.0 2.7 %collective-permute-start.36 = (bf16[64,2048]{1,0:T(8,128)(2,1)S(1)}, bf16[64,2048]{1,0:T(8,128)(2,1)S(1)}, u32[]{:S(2)}, u32[]{:S(2)}) collective-permute-start(bf16[64,2048]{1,0:T(8,128)(2,1)S(1)} %get-tuple-element.121), channel_id=1, source_target_pairs={{0,2},{1,3},{2,0},{3,1},{4,6},{5,7},{6,4},{7,5},{8,10},{9,11},{10,... | collective-permute-start | bytes 786440 | tf_op jit(solution)/shard_map/ppermute | solution.py:32
  123.9 4.0 %collective-permute-done.36 = bf16[64,2048]{1,0:T(8,128)(2,1)S(1)} collective-permute-done((bf16[64,2048]{1,0:T(8,128)(2,1)S(1)}, bf16[64,2048]{1,0:T(8,128)(2,1)S(1)}, u32[]{:S(2)}, u32[]{:S(2)}) %collective-permute-start.36) | collective-permute-done | bytes 262176 | tf_op jit(solution)/shard_map/ppermute | solution.py:32
  128.4 3.0 %collective-permute-start.37 = (bf16[64,2048]{1,0:T(8,128)(2,1)S(1)}, bf16[64,2048]{1,0:T(8,128)(2,1)S(1)}, u32[]{:S(2)}, u32[]{:S(2)}) collective-permute-start(bf16[64,2048]{1,0:T(8,128)(2,1)S(1)} %add_convert_fusion.2), channel_id=1, source_target_pairs={{0,17},{1,16},{2,19},{3,18},{4,21},{5,20},{6,23},{7,22},{8,25},{9,... | collective-permute-start | bytes 786440 | tf_op jit(solution)/shard_map/ppermute | solution.py:38
  133.4 4.7 %collective-permute-done.33 = bf16[64,2048]{1,0:T(8,128)(2,1)S(1)} collective-permute-done((bf16[64,2048]{1,0:T(8,128)(2,1)S(1)}, bf16[64,2048]{1,0:T(8,128)(2,1)S(1)}, u32[]{:S(2)}, u32[]{:S(2)}) %collective-permute-start.33) | collective-permute-done | bytes 262176 | tf_op jit(solution)/shard_map/ppermute | solution.py:32
  (97 shorter events, 45.7 us)
Async XLA Ops:
  0.0 14.0 %collective-permute-start.3 = (bf16[1,2048,768]{2,1,0:T(8,128)(2,1)}, bf16[1,2048,768]{2,1,0:T(8,128)(2,1)}, u32[]{:S(2)}, u32[]{:S(2)}) collective-permute-start(bf16[1,2048,768]{2,1,0:T(8,128)(2,1)} %refs_16_), channel_id=1, source_target_pairs={{0,8},{8,0},{16,24},{24,16},{1,9},{9,1},{17,25},{25,17},{2,10},{10... | collective-permute-start | bytes 9437192 | tf_op jit(solution)/shard_map/ppermute | solution.py:32
  0.5 13.5 %collective-permute-start.4 = (bf16[1,2048,768]{2,1,0:T(8,128)(2,1)}, bf16[1,2048,768]{2,1,0:T(8,128)(2,1)}, u32[]{:S(2)}, u32[]{:S(2)}) collective-permute-start(bf16[1,2048,768]{2,1,0:T(8,128)(2,1)} %refs_17_), channel_id=1, source_target_pairs={{0,8},{8,0},{16,24},{24,16},{1,9},{9,1},{17,25},{25,17},{2,10},{10... | collective-permute-start | bytes 9437192 | tf_op jit(solution)/shard_map/ppermute | solution.py:32
  11.0 13.9 %collective-permute-start.5 = (bf16[512,256]{1,0:T(8,128)(2,1)}, bf16[512,256]{1,0:T(8,128)(2,1)S(1)}, u32[]{:S(2)}, u32[]{:S(2)}) collective-permute-start(bf16[512,256]{1,0:T(8,128)(2,1)} %get-tuple-element.76), channel_id=1, source_target_pairs={{0,16},{8,24},{16,0},{24,8},{1,17},{9,25},{17,1},{25,9},{2,18},{10... | collective-permute-start | bytes 786440 | tf_op jit(solution)/shard_map/ppermute | solution.py:32
  14.0 11.5 %collective-permute-start.6 = (bf16[512,256]{1,0:T(8,128)(2,1)}, bf16[512,256]{1,0:T(8,128)(2,1)S(1)}, u32[]{:S(2)}, u32[]{:S(2)}) collective-permute-start(bf16[512,256]{1,0:T(8,128)(2,1)} %get-tuple-element.77), channel_id=1, source_target_pairs={{0,24},{8,16},{16,8},{24,0},{1,25},{9,17},{17,9},{25,1},{2,26},{10... | collective-permute-start | bytes 786440 | tf_op jit(solution)/shard_map/ppermute | solution.py:32
  43.6 12.9 %collective-permute-start.15 = (bf16[64,2176]{1,0:T(8,128)(2,1)S(1)}, bf16[64,2176]{1,0:T(8,128)(2,1)S(1)}, u32[]{:S(2)}, u32[]{:S(2)}) collective-permute-start(bf16[64,2176]{1,0:T(8,128)(2,1)S(1)} %get-tuple-element.91.refs_11_), channel_id=1, source_target_pairs={{0,2},{1,3},{2,0},{3,1},{4,6},{5,7},{6,4},{7,5},{8,10},{9,11},{10,... | collective-permute-start | bytes 835592 | tf_op jit(solution)/shard_map/ppermute | solution.py:32
  45.4 13.5 %collective-permute-start.21 = (bf16[64,2176]{1,0:T(8,128)(2,1)S(1)}, bf16[64,2176]{1,0:T(8,128)(2,1)S(1)}, u32[]{:S(2)}, u32[]{:S(2)}) collective-permute-start(bf16[64,2176]{1,0:T(8,128)(2,1)S(1)} %get-tuple-element.91.refs_11_), channel_id=1, source_target_pairs={{0,16},{8,24},{16,0},{24,8},{1,17},{9,25},{17,1},{25,9},{2,18},{10... | collective-permute-start | bytes 835592 | tf_op jit(solution)/shard_map/ppermute | solution.py:32
  46.9 14.4 %collective-permute-start.12 = (bf16[64,2176]{1,0:T(8,128)(2,1)S(1)}, bf16[64,2176]{1,0:T(8,128)(2,1)S(1)}, u32[]{:S(2)}, u32[]{:S(2)}) collective-permute-start(bf16[64,2176]{1,0:T(8,128)(2,1)S(1)} %get-tuple-element.91.refs_11_), channel_id=1, source_target_pairs={{0,4},{1,5},{2,6},{3,7},{4,0},{5,1},{6,2},{7,3},{8,12},{9,13},{10,... | collective-permute-start | bytes 835592 | tf_op jit(solution)/shard_map/ppermute | solution.py:32
  49.5 15.4 %collective-permute-start.20 = (bf16[64,2176]{1,0:T(8,128)(2,1)S(1)}, bf16[64,2176]{1,0:T(8,128)(2,1)S(1)}, u32[]{:S(2)}, u32[]{:S(2)}) collective-permute-start(bf16[64,2176]{1,0:T(8,128)(2,1)S(1)} %get-tuple-element.91.refs_11_), channel_id=1, source_target_pairs={{0,1},{1,0},{2,3},{3,2},{4,5},{5,4},{6,7},{7,6},{8,9},{9,8},{10,11... | collective-permute-start | bytes 835592 | tf_op jit(solution)/shard_map/ppermute | solution.py:32
  51.0 15.0 %collective-permute-start.11 = (bf16[64,2176]{1,0:T(8,128)(2,1)S(1)}, bf16[64,2176]{1,0:T(8,128)(2,1)S(1)}, u32[]{:S(2)}, u32[]{:S(2)}) collective-permute-start(bf16[64,2176]{1,0:T(8,128)(2,1)S(1)} %get-tuple-element.91.refs_11_), channel_id=1, source_target_pairs={{0,17},{1,16},{2,19},{3,18},{4,21},{5,20},{6,23},{7,22},{8,25},{9,... | collective-permute-start | bytes 835592 | tf_op jit(solution)/shard_map/ppermute | solution.py:38
  58.9 11.9 %collective-permute-start.23 = (bf16[64,2176]{1,0:T(8,128)(2,1)S(1)}, bf16[64,2176]{1,0:T(8,128)(2,1)S(1)}, u32[]{:S(2)}, u32[]{:S(2)}) collective-permute-start(bf16[64,2176]{1,0:T(8,128)(2,1)S(1)} %collective-permute-done.15.refs_2_), channel_id=1, source_target_pairs={{0,1},{1,0},{2,3},{3,2},{4,5},{5,4},{6,7},{7,6},{8,9},{9,8},{10,11... | collective-permute-start | bytes 835592 | tf_op jit(solution)/shard_map/ppermute | solution.py:32
  61.3 10.2 %collective-permute-start.13 = (bf16[64,2176]{1,0:T(8,128)(2,1)S(1)}, bf16[64,2176]{1,0:T(8,128)(2,1)S(1)}, u32[]{:S(2)}, u32[]{:S(2)}) collective-permute-start(bf16[64,2176]{1,0:T(8,128)(2,1)S(1)} %collective-permute-done.12.refs_9_), channel_id=1, source_target_pairs={{0,2},{1,3},{2,0},{3,1},{4,6},{5,7},{6,4},{7,5},{8,10},{9,11},{10,... | collective-permute-start | bytes 835592 | tf_op jit(solution)/shard_map/ppermute | solution.py:32
  64.9 9.7 %collective-permute-start.25 = (bf16[64,2176]{1,0:T(8,128)(2,1)S(1)}, bf16[64,2176]{1,0:T(8,128)(2,1)S(1)}, u32[]{:S(2)}, u32[]{:S(2)}) collective-permute-start(bf16[64,2176]{1,0:T(8,128)(2,1)S(1)} %collective-permute-done.12.refs_9_), channel_id=1, source_target_pairs={{0,1},{1,0},{2,3},{3,2},{4,5},{5,4},{6,7},{7,6},{8,9},{9,8},{10,11... | collective-permute-start | bytes 835592 | tf_op jit(solution)/shard_map/ppermute | solution.py:32
  66.0 11.7 %collective-permute-start.18 = (bf16[64,2176]{1,0:T(8,128)(2,1)S(1)}, bf16[64,2176]{1,0:T(8,128)(2,1)S(1)}, u32[]{:S(2)}, u32[]{:S(2)}) collective-permute-start(bf16[64,2176]{1,0:T(8,128)(2,1)S(1)} %collective-permute-done.11.refs_0_), channel_id=1, source_target_pairs={{0,4},{1,5},{2,6},{3,7},{4,0},{5,1},{6,2},{7,3},{8,12},{9,13},{10,... | collective-permute-start | bytes 835592 | tf_op jit(solution)/shard_map/ppermute | solution.py:32
  66.0 12.0 %collective-permute-start.16 = (bf16[64,2176]{1,0:T(8,128)(2,1)S(1)}, bf16[64,2176]{1,0:T(8,128)(2,1)S(1)}, u32[]{:S(2)}, u32[]{:S(2)}) collective-permute-start(bf16[64,2176]{1,0:T(8,128)(2,1)S(1)} %collective-permute-done.12.refs_9_), channel_id=1, source_target_pairs={{0,16},{8,24},{16,0},{24,8},{1,17},{9,25},{17,1},{25,9},{2,18},{10... | collective-permute-start | bytes 835592 | tf_op jit(solution)/shard_map/ppermute | solution.py:32
  70.9 11.3 %collective-permute-start.19 = (bf16[64,2176]{1,0:T(8,128)(2,1)S(1)}, bf16[64,2176]{1,0:T(8,128)(2,1)}, u32[]{:S(2)}, u32[]{:S(2)}) collective-permute-start(bf16[64,2176]{1,0:T(8,128)(2,1)S(1)} %collective-permute-done.11.refs_0_), channel_id=1, source_target_pairs={{0,2},{1,3},{2,0},{3,1},{4,6},{5,7},{6,4},{7,5},{8,10},{9,11},{10,... | collective-permute-start | bytes 835592 | tf_op jit(solution)/shard_map/ppermute | solution.py:32
  71.5 10.7 %collective-permute-start.17 = (bf16[64,2176]{1,0:T(8,128)(2,1)S(1)}, bf16[64,2176]{1,0:T(8,128)(2,1)}, u32[]{:S(2)}, u32[]{:S(2)}) collective-permute-start(bf16[64,2176]{1,0:T(8,128)(2,1)S(1)} %collective-permute-done.13.refs_8_), channel_id=1, source_target_pairs={{0,16},{8,24},{16,0},{24,8},{1,17},{9,25},{17,1},{25,9},{2,18},{10... | collective-permute-start | bytes 835592 | tf_op jit(solution)/shard_map/ppermute | solution.py:32
  102.2 12.8 %collective-permute-start.26 = (bf16[64,2048]{1,0:T(8,128)(2,1)S(1)}, bf16[64,2048]{1,0:T(8,128)(2,1)S(1)}, u32[]{:S(2)}, u32[]{:S(2)}) collective-permute-start(bf16[64,2048]{1,0:T(8,128)(2,1)S(1)} %get-tuple-element.99), channel_id=1, source_target_pairs={{0,16},{8,24},{16,0},{24,8},{1,17},{9,25},{17,1},{25,9},{2,18},{10... | collective-permute-start | bytes 786440 | tf_op jit(solution)/shard_map/ppermute | solution.py:32
  103.1 14.9 %collective-permute-start.27 = (bf16[64,2048]{1,0:T(8,128)(2,1)S(1)}, bf16[64,2048]{1,0:T(8,128)(2,1)S(1)}, u32[]{:S(2)}, u32[]{:S(2)}) collective-permute-start(bf16[64,2048]{1,0:T(8,128)(2,1)S(1)} %get-tuple-element.100), channel_id=1, source_target_pairs={{0,1},{1,0},{2,3},{3,2},{4,5},{5,4},{6,7},{7,6},{8,9},{9,8},{10,11... | collective-permute-start | bytes 786440 | tf_op jit(solution)/shard_map/ppermute | solution.py:32
  109.7 11.0 %collective-permute-start.32 = (bf16[64,2048]{1,0:T(8,128)(2,1)S(1)}, bf16[64,2048]{1,0:T(8,128)(2,1)S(1)}, u32[]{:S(2)}, u32[]{:S(2)}) collective-permute-start(bf16[64,2048]{1,0:T(8,128)(2,1)S(1)} %add_convert_fusion.4), channel_id=1, source_target_pairs={{0,2},{1,3},{2,0},{3,1},{4,6},{5,7},{6,4},{7,5},{8,10},{9,11},{10,... | collective-permute-start | bytes 786440 | tf_op jit(solution)/shard_map/ppermute | solution.py:32
  111.5 10.2 %collective-permute-start.31 = (bf16[64,2048]{1,0:T(8,128)(2,1)S(1)}, bf16[64,2048]{1,0:T(8,128)(2,1)S(1)}, u32[]{:S(2)}, u32[]{:S(2)}) collective-permute-start(bf16[64,2048]{1,0:T(8,128)(2,1)S(1)} %add_convert_fusion.5), channel_id=1, source_target_pairs={{0,17},{1,16},{2,19},{3,18},{4,21},{5,20},{6,23},{7,22},{8,25},{9,... | collective-permute-start | bytes 786440 | tf_op jit(solution)/shard_map/ppermute | solution.py:38
  113.9 19.6 %collective-permute-start.34 = (bf16[64,2048]{1,0:T(8,128)(2,1)S(1)}, bf16[64,2048]{1,0:T(8,128)(2,1)S(1)}, u32[]{:S(2)}, u32[]{:S(2)}) collective-permute-start(bf16[64,2048]{1,0:T(8,128)(2,1)S(1)} %get-tuple-element.118), channel_id=1, source_target_pairs={{0,16},{8,24},{16,0},{24,8},{1,17},{9,25},{17,1},{25,9},{2,18},{10... | collective-permute-start | bytes 786440 | tf_op jit(solution)/shard_map/ppermute | solution.py:32
  115.1 18.4 %collective-permute-start.35 = (bf16[64,2048]{1,0:T(8,128)(2,1)S(1)}, bf16[64,2048]{1,0:T(8,128)(2,1)S(1)}, u32[]{:S(2)}, u32[]{:S(2)}) collective-permute-start(bf16[64,2048]{1,0:T(8,128)(2,1)S(1)} %get-tuple-element.119), channel_id=1, source_target_pairs={{0,1},{1,0},{2,3},{3,2},{4,5},{5,4},{6,7},{7,6},{8,9},{9,8},{10,11... | collective-permute-start | bytes 786440 | tf_op jit(solution)/shard_map/ppermute | solution.py:32
  118.0 9.9 %collective-permute-start.36 = (bf16[64,2048]{1,0:T(8,128)(2,1)S(1)}, bf16[64,2048]{1,0:T(8,128)(2,1)S(1)}, u32[]{:S(2)}, u32[]{:S(2)}) collective-permute-start(bf16[64,2048]{1,0:T(8,128)(2,1)S(1)} %get-tuple-element.121), channel_id=1, source_target_pairs={{0,2},{1,3},{2,0},{3,1},{4,6},{5,7},{6,4},{7,5},{8,10},{9,11},{10,... | collective-permute-start | bytes 786440 | tf_op jit(solution)/shard_map/ppermute | solution.py:32
  127.9 10.2 %collective-permute-start.33 = (bf16[64,2048]{1,0:T(8,128)(2,1)S(1)}, bf16[64,2048]{1,0:T(8,128)(2,1)S(1)}, u32[]{:S(2)}, u32[]{:S(2)}) collective-permute-start(bf16[64,2048]{1,0:T(8,128)(2,1)S(1)} %add_convert_fusion.3), channel_id=1, source_target_pairs={{0,4},{1,5},{2,6},{3,7},{4,0},{5,1},{6,2},{7,3},{8,12},{9,13},{10,... | collective-permute-start | bytes 786440 | tf_op jit(solution)/shard_map/ppermute | solution.py:32
  (29 other events, 265.6 us)

commit v7 on v6

--- a/solution.py
+++ b/solution.py
@@ -16,8 +16,8 @@
 EXPERT_MIB = 46
 GATHER = ("c2", "c1", "d0", "y0", "x0", "c3", "d2", "x2", "y2", "y1", "x1", "d1", "y3", "x3", "d3")
 TAKE = (3, 14, 4, 9, 13, 11, 7, 2, 12, 8, 1, 0, 15, 6, 5, 10)
-NEAR_MIB = 14
-FAR_MIB = 14
+NEAR_MIB = 24
+FAR_MIB = 24
 EXP2_SCALE = math.log2(math.e) / math.sqrt(HD)
 NT = (((1,), (1,)), ((), ()))
 TN = (((0,), (0,)), ((), ()))

time: 140 us -> 140 us (level)
  transfers between devices with their start and end apart: 41 -> 41, of which waited for: 24 -> 23; matrix products, arithmetic and copies ran while one was open for 0% -> 0% of each run, Pallas kernels for 7% -> 7%
where the time goes in v7:
time: 140 us
  waiting for transfers between devices  57.7 us (41%)
  starting transfers between devices  45.5 us (32%)
  Pallas kernels  29.9 us (21%)
  local copies, waits for them, and re-layouts  4.11 us (3%)
  other arithmetic  1.63 us (1%)
    ppermute x38, waiting for transfers between devices, swap(): lax.ppermute(rows, axis, [(i, i ^ bits) for i in range(lax.axis_size(axis...  56.9 us
    ppermute x38, starting transfers between devices, swap(): lax.ppermute(rows, axis, [(i, i ^ bits) for i in range(lax.axis_size(axis...  39.6 us
    pallas_call x1, Pallas kernels, expert_terms(): pl.pallas_call(functools.partial(expert_kernel, layouts, take, per_group,...  13.6 us
    pallas_call x1, Pallas kernels, project(): pl.pallas_call(functools.partial(far_kernel, nseq, ks), out_shape=[jax.Sh...  6.55 us
    ppermute x3, starting transfers between devices, swap_both(): lax.ppermute(rows, ('seq', 'exp'), [(i, i ^ bits) for i in range(nseq * n...  5.95 us
    pallas_call x1, Pallas kernels, project_attention(): pl.pallas_call(functools.partial(near_kernel, nseq), out_shape=[jax.Shape...  4.72 us
    pallas_call x2, Pallas kernels, pack(): pl.pallas_call(functools.partial(pack_kernel, nseq, widths), out_shape=[s...  4.45 us
    unnamed x24, local copies, waits for them, and re-layouts  4.09 us
  transfers between devices with their start and end apart: 41, of which 23 were waited for; matrix products, arithmetic and copies ran while one was open for 0% of the time, Pallas kernels for 7%

profile of v7, /device:TPU:0, one launch (start us, length us, event | category | flops | bytes accessed | tf_op | source)
XLA Modules:
  0.0 139.8 jit_solution(9103654479701980981)
XLA Ops:
  3.2 2.6 %collective-permute-start.1 = (bf16[64,1280]{1,0:T(8,128)(2,1)}, bf16[64,1280]{1,0:T(8,128)(2,1)S(1)}, u32[]{:S(2)}, u32[]{:S(2)}) collective-permute-start(bf16[64,1280]{1,0:T(8,128)(2,1)} %get-tuple-element.68), channel_id=1, source_target_pairs={{0,16},{8,24},{16,0},{24,8},{1,17},{9,25},{17,1},{25,9},{2,18},{10... | collective-permute-start | bytes 491528 | tf_op jit(solution)/shard_map/ppermute | solution.py:32
  6.4 2.3 %pack_heads.3 = (bf16[512,256]{1,0:T(8,128)(2,1)}, bf16[512,256]{1,0:T(8,128)(2,1)}, bf16[512,256]{1,0:T(8,128)(2,1)}, bf16[512,256]{1,0:T(8,128)(2,1)}) custom-call(s32[1]{0:T(128)} %bitcast.1.me_ref, bf16[512,512]{1,0:T(8,128)(2,1)} %bitcast.21, bf16[512,512]{1,0:T(8,128)(2,1)} %bitcast.22), custom_call_target="tpu_custom_call" | custom-call | tf_op jit(solution)/shard_map/pack_heads/pallas_call | solution.py:64
  8.8 2.2 %collective-permute-done.1.refs_2_ = bf16[64,1280]{1,0:T(8,128)(2,1)S(1)} collective-permute-done((bf16[64,1280]{1,0:T(8,128)(2,1)}, bf16[64,1280]{1,0:T(8,128)(2,1)S(1)}, u32[]{:S(2)}, u32[]{:S(2)}) %collective-permute-start.1) | collective-permute-done | bytes 163872 | tf_op jit(solution)/shard_map/ppermute | solution.py:32
  16.1 2.2 %copy-done = bf16[1024,2048]{1,0:T(8,128)(2,1)S(1)} copy-done((bf16[1024,2048]{1,0:T(8,128)(2,1)S(1)}, bf16[1024,2048]{1,0:T(8,128)(2,1)}, u32[]{:S(2)}) %copy-start) | copy-done | bytes 4194328
  20.2 4.7 %attend_near.1 = (f32[256,128]{1,0:T(8,128)S(1)}, f32[256,128]{1,0:T(8,128)S(1)}, f32[256,1024]{1,0:T(8,128)S(1)}) custom-call(s32[1]{0:T(128)} %bitcast.1.me_ref, s32[1]{0:T(128)S(6)} %copy.15.len_ref, bf16[64,1280]{1,0:T(8,128)(2,1)S(1)} %copy-done.2, bf16[64,1280]{1,0:T(8,128)(2,1)S(1)} %collective-permute-done.refs_1_, ...), custom_call_target="tpu_custom_call" | custom-call | tf_op jit(solution)/shard_map/attend_near/pallas_call | solution.py:171
  25.5 6.5 %attend_far.1 = (f32[128,2048]{1,0:T(8,128)S(1)}, bf16[128,2048]{1,0:T(8,128)(2,1)S(1)}) custom-call(s32[1]{0:T(128)} %bitcast.1.me_ref, s32[1]{0:T(128)S(6)} %copy.15.len_ref, bf16[64,1280]{1,0:T(8,128)(2,1)S(1)} %copy-done.2, bf16[64,1280]{1,0:T(8,128)(2,1)S(1)} %collective-permute-done.refs_1_, bf16[64,1280]{1,0:T(8,128)(2,1)S(1)} %collective-permute-done.1.refs_2_, ...), custom_call_target="tpu_custom_call" | custom-call | tf_op jit(solution)/shard_map/attend_far/pallas_call | solution.py:186
  36.1 6.9 %collective-permute-done.9.refs_2_ = bf16[64,2048]{1,0:T(8,128)(2,1)S(1)} collective-permute-done((bf16[64,2048]{1,0:T(8,128)(2,1)S(1)}, bf16[64,2048]{1,0:T(8,128)(2,1)S(1)}, u32[]{:S(2)}, u32[]{:S(2)}) %collective-permute-start.9) | collective-permute-done | bytes 262176 | tf_op jit(solution)/shard_map/ppermute | solution.py:32
  46.9 2.6 %collective-permute-start.12 = (bf16[64,2176]{1,0:T(8,128)(2,1)S(1)}, bf16[64,2176]{1,0:T(8,128)(2,1)S(1)}, u32[]{:S(2)}, u32[]{:S(2)}) collective-permute-start(bf16[64,2176]{1,0:T(8,128)(2,1)S(1)} %get-tuple-element.91.refs_11_), channel_id=1, source_target_pairs={{0,4},{1,5},{2,6},{3,7},{4,0},{5,1},{6,2},{7,3},{8,12},{9,13},{10,... | collective-permute-start | bytes 835592 | tf_op jit(solution)/shard_map/ppermute | solution.py:32
  51.5 5.0 %collective-permute-done.15.refs_2_ = bf16[64,2176]{1,0:T(8,128)(2,1)S(1)} collective-permute-done((bf16[64,2176]{1,0:T(8,128)(2,1)S(1)}, bf16[64,2176]{1,0:T(8,128)(2,1)S(1)}, u32[]{:S(2)}, u32[]{:S(2)}) %collective-permute-start.15) | collective-permute-done | bytes 278560 | tf_op jit(solution)/shard_map/ppermute | solution.py:32
  56.5 2.4 %collective-permute-start.24 = (bf16[64,2176]{1,0:T(8,128)(2,1)S(1)}, bf16[64,2176]{1,0:T(8,128)(2,1)S(1)}, u32[]{:S(2)}, u32[]{:S(2)}) collective-permute-start(bf16[64,2176]{1,0:T(8,128)(2,1)S(1)} %collective-permute-done.15.refs_2_), channel_id=1, source_target_pairs={{0,16},{8,24},{16,0},{24,8},{1,17},{9,25},{17,1},{25,9},{2,18},{10... | collective-permute-start | bytes 835592 | tf_op jit(solution)/shard_map/ppermute | solution.py:32
  61.3 3.6 %collective-permute-done.20.refs_7_ = bf16[64,2176]{1,0:T(8,128)(2,1)S(1)} collective-permute-done((bf16[64,2176]{1,0:T(8,128)(2,1)S(1)}, bf16[64,2176]{1,0:T(8,128)(2,1)S(1)}, u32[]{:S(2)}, u32[]{:S(2)}) %collective-permute-start.20) | collective-permute-done | bytes 278560 | tf_op jit(solution)/shard_map/ppermute | solution.py:32
  66.8 4.1 %collective-permute-done.23.refs_13_ = bf16[64,2176]{1,0:T(8,128)(2,1)S(1)} collective-permute-done((bf16[64,2176]{1,0:T(8,128)(2,1)S(1)}, bf16[64,2176]{1,0:T(8,128)(2,1)S(1)}, u32[]{:S(2)}, u32[]{:S(2)}) %collective-permute-start.23) | collective-permute-done | bytes 278560 | tf_op jit(solution)/shard_map/ppermute | solution.py:32
  71.7 2.9 %collective-permute-done.25.refs_15_ = bf16[64,2176]{1,0:T(8,128)(2,1)S(1)} collective-permute-done((bf16[64,2176]{1,0:T(8,128)(2,1)S(1)}, bf16[64,2176]{1,0:T(8,128)(2,1)S(1)}, u32[]{:S(2)}, u32[]{:S(2)}) %collective-permute-start.25) | collective-permute-done | bytes 278560 | tf_op jit(solution)/shard_map/ppermute | solution.py:32
  78.1 4.2 %collective-permute-done.19.refs_6_ = bf16[64,2176]{1,0:T(8,128)(2,1)} collective-permute-done((bf16[64,2176]{1,0:T(8,128)(2,1)S(1)}, bf16[64,2176]{1,0:T(8,128)(2,1)}, u32[]{:S(2)}, u32[]{:S(2)}) %collective-permute-start.19) | collective-permute-done | bytes 278560 | tf_op jit(solution)/shard_map/ppermute | solution.py:32
  82.2 3.7 %collective-permute-done.22.refs_12_ = bf16[64,2176]{1,0:T(8,128)(2,1)} collective-permute-done((bf16[64,2176]{1,0:T(8,128)(2,1)S(1)}, bf16[64,2176]{1,0:T(8,128)(2,1)}, u32[]{:S(2)}, u32[]{:S(2)}) %collective-permute-start.22) | collective-permute-done | bytes 278560 | tf_op jit(solution)/shard_map/ppermute | solution.py:32
  85.9 13.6 %experts.1 = (bf16[64,2048]{1,0:T(8,128)(2,1)S(1)}, bf16[64,2048]{1,0:T(8,128)(2,1)S(1)}, bf16[64,2048]{1,0:T(8,128)(2,1)S(1)}, bf16[64,2048]{1,0:T(8,128)(2,1)S...) custom-call(s32[2]{0:T(128)S(1)} %pad_add_fusion.mine_ref, ...), custom_call_target="tpu_custom_call" | custom-call | flops 7247757312 | bytes 6291456 | tf_op jit(solution)/shard_map/experts/pallas_call | solution.py:395
  103.6 2.2 %collective-permute-done.28 = bf16[64,2048]{1,0:T(8,128)(2,1)S(1)} collective-permute-done((bf16[64,2048]{1,0:T(8,128)(2,1)S(1)}, bf16[64,2048]{1,0:T(8,128)(2,1)S(1)}, u32[]{:S(2)}, u32[]{:S(2)}) %collective-permute-start.28) | collective-permute-done | bytes 262176 | tf_op jit(solution)/shard_map/ppermute | solution.py:32
  105.9 2.6 %collective-permute-done.29 = bf16[64,2048]{1,0:T(8,128)(2,1)S(1)} collective-permute-done((bf16[64,2048]{1,0:T(8,128)(2,1)S(1)}, bf16[64,2048]{1,0:T(8,128)(2,1)S(1)}, u32[]{:S(2)}, u32[]{:S(2)}) %collective-permute-start.29) | collective-permute-done | bytes 262176 | tf_op jit(solution)/shard_map/ppermute | solution.py:32
  111.5 2.4 %collective-permute-start.31 = (bf16[64,2048]{1,0:T(8,128)(2,1)S(1)}, bf16[64,2048]{1,0:T(8,128)(2,1)S(1)}, u32[]{:S(2)}, u32[]{:S(2)}) collective-permute-start(bf16[64,2048]{1,0:T(8,128)(2,1)S(1)} %add_convert_fusion.5), channel_id=1, source_target_pairs={{0,17},{1,16},{2,19},{3,18},{4,21},{5,20},{6,23},{7,22},{8,25},{9,... | collective-permute-start | bytes 786440 | tf_op jit(solution)/shard_map/ppermute | solution.py:38
  116.0 2.2 %collective-permute-done.27 = bf16[64,2048]{1,0:T(8,128)(2,1)S(1)} collective-permute-done((bf16[64,2048]{1,0:T(8,128)(2,1)S(1)}, bf16[64,2048]{1,0:T(8,128)(2,1)S(1)}, u32[]{:S(2)}, u32[]{:S(2)}) %collective-permute-start.27) | collective-permute-done | bytes 262176 | tf_op jit(solution)/shard_map/ppermute | solution.py:32
  118.2 2.5 %collective-permute-start.36 = (bf16[64,2048]{1,0:T(8,128)(2,1)S(1)}, bf16[64,2048]{1,0:T(8,128)(2,1)S(1)}, u32[]{:S(2)}, u32[]{:S(2)}) collective-permute-start(bf16[64,2048]{1,0:T(8,128)(2,1)S(1)} %get-tuple-element.121), channel_id=1, source_target_pairs={{0,2},{1,3},{2,0},{3,1},{4,6},{5,7},{6,4},{7,5},{8,10},{9,11},{10,... | collective-permute-start | bytes 786440 | tf_op jit(solution)/shard_map/ppermute | solution.py:32
  123.9 3.9 %collective-permute-done.36 = bf16[64,2048]{1,0:T(8,128)(2,1)S(1)} collective-permute-done((bf16[64,2048]{1,0:T(8,128)(2,1)S(1)}, bf16[64,2048]{1,0:T(8,128)(2,1)S(1)}, u32[]{:S(2)}, u32[]{:S(2)}) %collective-permute-start.36) | collective-permute-done | bytes 262176 | tf_op jit(solution)/shard_map/ppermute | solution.py:32
  128.3 3.1 %collective-permute-start.37 = (bf16[64,2048]{1,0:T(8,128)(2,1)S(1)}, bf16[64,2048]{1,0:T(8,128)(2,1)S(1)}, u32[]{:S(2)}, u32[]{:S(2)}) collective-permute-start(bf16[64,2048]{1,0:T(8,128)(2,1)S(1)} %add_convert_fusion.2), channel_id=1, source_target_pairs={{0,17},{1,16},{2,19},{3,18},{4,21},{5,20},{6,23},{7,22},{8,25},{9,... | collective-permute-start | bytes 786440 | tf_op jit(solution)/shard_map/ppermute | solution.py:38
  133.4 4.7 %collective-permute-done.33 = bf16[64,2048]{1,0:T(8,128)(2,1)S(1)} collective-permute-done((bf16[64,2048]{1,0:T(8,128)(2,1)S(1)}, bf16[64,2048]{1,0:T(8,128)(2,1)S(1)}, u32[]{:S(2)}, u32[]{:S(2)}) %collective-permute-start.33) | collective-permute-done | bytes 262176 | tf_op jit(solution)/shard_map/ppermute | solution.py:32
  (97 shorter events, 45.7 us)
Async XLA Ops:
  0.0 14.0 %collective-permute-start.3 = (bf16[1,2048,768]{2,1,0:T(8,128)(2,1)}, bf16[1,2048,768]{2,1,0:T(8,128)(2,1)}, u32[]{:S(2)}, u32[]{:S(2)}) collective-permute-start(bf16[1,2048,768]{2,1,0:T(8,128)(2,1)} %refs_16_), channel_id=1, source_target_pairs={{0,8},{8,0},{16,24},{24,16},{1,9},{9,1},{17,25},{25,17},{2,10},{10... | collective-permute-start | bytes 9437192 | tf_op jit(solution)/shard_map/ppermute | solution.py:32
  0.5 13.5 %collective-permute-start.4 = (bf16[1,2048,768]{2,1,0:T(8,128)(2,1)}, bf16[1,2048,768]{2,1,0:T(8,128)(2,1)}, u32[]{:S(2)}, u32[]{:S(2)}) collective-permute-start(bf16[1,2048,768]{2,1,0:T(8,128)(2,1)} %refs_17_), channel_id=1, source_target_pairs={{0,8},{8,0},{16,24},{24,16},{1,9},{9,1},{17,25},{25,17},{2,10},{10... | collective-permute-start | bytes 9437192 | tf_op jit(solution)/shard_map/ppermute | solution.py:32
  11.0 13.9 %collective-permute-start.5 = (bf16[512,256]{1,0:T(8,128)(2,1)}, bf16[512,256]{1,0:T(8,128)(2,1)S(1)}, u32[]{:S(2)}, u32[]{:S(2)}) collective-permute-start(bf16[512,256]{1,0:T(8,128)(2,1)} %get-tuple-element.76), channel_id=1, source_target_pairs={{0,16},{8,24},{16,0},{24,8},{1,17},{9,25},{17,1},{25,9},{2,18},{10... | collective-permute-start | bytes 786440 | tf_op jit(solution)/shard_map/ppermute | solution.py:32
  14.0 11.5 %collective-permute-start.6 = (bf16[512,256]{1,0:T(8,128)(2,1)}, bf16[512,256]{1,0:T(8,128)(2,1)S(1)}, u32[]{:S(2)}, u32[]{:S(2)}) collective-permute-start(bf16[512,256]{1,0:T(8,128)(2,1)} %get-tuple-element.77), channel_id=1, source_target_pairs={{0,24},{8,16},{16,8},{24,0},{1,25},{9,17},{17,9},{25,1},{2,26},{10... | collective-permute-start | bytes 786440 | tf_op jit(solution)/shard_map/ppermute | solution.py:32
  43.6 12.9 %collective-permute-start.15 = (bf16[64,2176]{1,0:T(8,128)(2,1)S(1)}, bf16[64,2176]{1,0:T(8,128)(2,1)S(1)}, u32[]{:S(2)}, u32[]{:S(2)}) collective-permute-start(bf16[64,2176]{1,0:T(8,128)(2,1)S(1)} %get-tuple-element.91.refs_11_), channel_id=1, source_target_pairs={{0,2},{1,3},{2,0},{3,1},{4,6},{5,7},{6,4},{7,5},{8,10},{9,11},{10,... | collective-permute-start | bytes 835592 | tf_op jit(solution)/shard_map/ppermute | solution.py:32
  45.4 13.5 %collective-permute-start.21 = (bf16[64,2176]{1,0:T(8,128)(2,1)S(1)}, bf16[64,2176]{1,0:T(8,128)(2,1)S(1)}, u32[]{:S(2)}, u32[]{:S(2)}) collective-permute-start(bf16[64,2176]{1,0:T(8,128)(2,1)S(1)} %get-tuple-element.91.refs_11_), channel_id=1, source_target_pairs={{0,16},{8,24},{16,0},{24,8},{1,17},{9,25},{17,1},{25,9},{2,18},{10... | collective-permute-start | bytes 835592 | tf_op jit(solution)/shard_map/ppermute | solution.py:32
  46.9 14.4 %collective-permute-start.12 = (bf16[64,2176]{1,0:T(8,128)(2,1)S(1)}, bf16[64,2176]{1,0:T(8,128)(2,1)S(1)}, u32[]{:S(2)}, u32[]{:S(2)}) collective-permute-start(bf16[64,2176]{1,0:T(8,128)(2,1)S(1)} %get-tuple-element.91.refs_11_), channel_id=1, source_target_pairs={{0,4},{1,5},{2,6},{3,7},{4,0},{5,1},{6,2},{7,3},{8,12},{9,13},{10,... | collective-permute-start | bytes 835592 | tf_op jit(solution)/shard_map/ppermute | solution.py:32
  49.5 15.4 %collective-permute-start.20 = (bf16[64,2176]{1,0:T(8,128)(2,1)S(1)}, bf16[64,2176]{1,0:T(8,128)(2,1)S(1)}, u32[]{:S(2)}, u32[]{:S(2)}) collective-permute-start(bf16[64,2176]{1,0:T(8,128)(2,1)S(1)} %get-tuple-element.91.refs_11_), channel_id=1, source_target_pairs={{0,1},{1,0},{2,3},{3,2},{4,5},{5,4},{6,7},{7,6},{8,9},{9,8},{10,11... | collective-permute-start | bytes 835592 | tf_op jit(solution)/shard_map/ppermute | solution.py:32
  51.0 15.0 %collective-permute-start.11 = (bf16[64,2176]{1,0:T(8,128)(2,1)S(1)}, bf16[64,2176]{1,0:T(8,128)(2,1)S(1)}, u32[]{:S(2)}, u32[]{:S(2)}) collective-permute-start(bf16[64,2176]{1,0:T(8,128)(2,1)S(1)} %get-tuple-element.91.refs_11_), channel_id=1, source_target_pairs={{0,17},{1,16},{2,19},{3,18},{4,21},{5,20},{6,23},{7,22},{8,25},{9,... | collective-permute-start | bytes 835592 | tf_op jit(solution)/shard_map/ppermute | solution.py:38
  58.9 11.9 %collective-permute-start.23 = (bf16[64,2176]{1,0:T(8,128)(2,1)S(1)}, bf16[64,2176]{1,0:T(8,128)(2,1)S(1)}, u32[]{:S(2)}, u32[]{:S(2)}) collective-permute-start(bf16[64,2176]{1,0:T(8,128)(2,1)S(1)} %collective-permute-done.15.refs_2_), channel_id=1, source_target_pairs={{0,1},{1,0},{2,3},{3,2},{4,5},{5,4},{6,7},{7,6},{8,9},{9,8},{10,11... | collective-permute-start | bytes 835592 | tf_op jit(solution)/shard_map/ppermute | solution.py:32
  61.3 10.1 %collective-permute-start.13 = (bf16[64,2176]{1,0:T(8,128)(2,1)S(1)}, bf16[64,2176]{1,0:T(8,128)(2,1)S(1)}, u32[]{:S(2)}, u32[]{:S(2)}) collective-permute-start(bf16[64,2176]{1,0:T(8,128)(2,1)S(1)} %collective-permute-done.12.refs_9_), channel_id=1, source_target_pairs={{0,2},{1,3},{2,0},{3,1},{4,6},{5,7},{6,4},{7,5},{8,10},{9,11},{10,... | collective-permute-start | bytes 835592 | tf_op jit(solution)/shard_map/ppermute | solution.py:32
  64.9 9.7 %collective-permute-start.25 = (bf16[64,2176]{1,0:T(8,128)(2,1)S(1)}, bf16[64,2176]{1,0:T(8,128)(2,1)S(1)}, u32[]{:S(2)}, u32[]{:S(2)}) collective-permute-start(bf16[64,2176]{1,0:T(8,128)(2,1)S(1)} %collective-permute-done.12.refs_9_), channel_id=1, source_target_pairs={{0,1},{1,0},{2,3},{3,2},{4,5},{5,4},{6,7},{7,6},{8,9},{9,8},{10,11... | collective-permute-start | bytes 835592 | tf_op jit(solution)/shard_map/ppermute | solution.py:32
  66.0 11.7 %collective-permute-start.18 = (bf16[64,2176]{1,0:T(8,128)(2,1)S(1)}, bf16[64,2176]{1,0:T(8,128)(2,1)S(1)}, u32[]{:S(2)}, u32[]{:S(2)}) collective-permute-start(bf16[64,2176]{1,0:T(8,128)(2,1)S(1)} %collective-permute-done.11.refs_0_), channel_id=1, source_target_pairs={{0,4},{1,5},{2,6},{3,7},{4,0},{5,1},{6,2},{7,3},{8,12},{9,13},{10,... | collective-permute-start | bytes 835592 | tf_op jit(solution)/shard_map/ppermute | solution.py:32
  66.0 12.0 %collective-permute-start.16 = (bf16[64,2176]{1,0:T(8,128)(2,1)S(1)}, bf16[64,2176]{1,0:T(8,128)(2,1)S(1)}, u32[]{:S(2)}, u32[]{:S(2)}) collective-permute-start(bf16[64,2176]{1,0:T(8,128)(2,1)S(1)} %collective-permute-done.12.refs_9_), channel_id=1, source_target_pairs={{0,16},{8,24},{16,0},{24,8},{1,17},{9,25},{17,1},{25,9},{2,18},{10... | collective-permute-start | bytes 835592 | tf_op jit(solution)/shard_map/ppermute | solution.py:32
  70.9 11.3 %collective-permute-start.19 = (bf16[64,2176]{1,0:T(8,128)(2,1)S(1)}, bf16[64,2176]{1,0:T(8,128)(2,1)}, u32[]{:S(2)}, u32[]{:S(2)}) collective-permute-start(bf16[64,2176]{1,0:T(8,128)(2,1)S(1)} %collective-permute-done.11.refs_0_), channel_id=1, source_target_pairs={{0,2},{1,3},{2,0},{3,1},{4,6},{5,7},{6,4},{7,5},{8,10},{9,11},{10,... | collective-permute-start | bytes 835592 | tf_op jit(solution)/shard_map/ppermute | solution.py:32
  71.4 10.8 %collective-permute-start.17 = (bf16[64,2176]{1,0:T(8,128)(2,1)S(1)}, bf16[64,2176]{1,0:T(8,128)(2,1)}, u32[]{:S(2)}, u32[]{:S(2)}) collective-permute-start(bf16[64,2176]{1,0:T(8,128)(2,1)S(1)} %collective-permute-done.13.refs_8_), channel_id=1, source_target_pairs={{0,16},{8,24},{16,0},{24,8},{1,17},{9,25},{17,1},{25,9},{2,18},{10... | collective-permute-start | bytes 835592 | tf_op jit(solution)/shard_map/ppermute | solution.py:32
  102.2 12.9 %collective-permute-start.26 = (bf16[64,2048]{1,0:T(8,128)(2,1)S(1)}, bf16[64,2048]{1,0:T(8,128)(2,1)S(1)}, u32[]{:S(2)}, u32[]{:S(2)}) collective-permute-start(bf16[64,2048]{1,0:T(8,128)(2,1)S(1)} %get-tuple-element.99), channel_id=1, source_target_pairs={{0,16},{8,24},{16,0},{24,8},{1,17},{9,25},{17,1},{25,9},{2,18},{10... | collective-permute-start | bytes 786440 | tf_op jit(solution)/shard_map/ppermute | solution.py:32
  103.1 15.1 %collective-permute-start.27 = (bf16[64,2048]{1,0:T(8,128)(2,1)S(1)}, bf16[64,2048]{1,0:T(8,128)(2,1)S(1)}, u32[]{:S(2)}, u32[]{:S(2)}) collective-permute-start(bf16[64,2048]{1,0:T(8,128)(2,1)S(1)} %get-tuple-element.100), channel_id=1, source_target_pairs={{0,1},{1,0},{2,3},{3,2},{4,5},{5,4},{6,7},{7,6},{8,9},{9,8},{10,11... | collective-permute-start | bytes 786440 | tf_op jit(solution)/shard_map/ppermute | solution.py:32
  109.8 10.9 %collective-permute-start.32 = (bf16[64,2048]{1,0:T(8,128)(2,1)S(1)}, bf16[64,2048]{1,0:T(8,128)(2,1)S(1)}, u32[]{:S(2)}, u32[]{:S(2)}) collective-permute-start(bf16[64,2048]{1,0:T(8,128)(2,1)S(1)} %add_convert_fusion.4), channel_id=1, source_target_pairs={{0,2},{1,3},{2,0},{3,1},{4,6},{5,7},{6,4},{7,5},{8,10},{9,11},{10,... | collective-permute-start | bytes 786440 | tf_op jit(solution)/shard_map/ppermute | solution.py:32
  111.5 10.2 %collective-permute-start.31 = (bf16[64,2048]{1,0:T(8,128)(2,1)S(1)}, bf16[64,2048]{1,0:T(8,128)(2,1)S(1)}, u32[]{:S(2)}, u32[]{:S(2)}) collective-permute-start(bf16[64,2048]{1,0:T(8,128)(2,1)S(1)} %add_convert_fusion.5), channel_id=1, source_target_pairs={{0,17},{1,16},{2,19},{3,18},{4,21},{5,20},{6,23},{7,22},{8,25},{9,... | collective-permute-start | bytes 786440 | tf_op jit(solution)/shard_map/ppermute | solution.py:38
  113.9 19.6 %collective-permute-start.34 = (bf16[64,2048]{1,0:T(8,128)(2,1)S(1)}, bf16[64,2048]{1,0:T(8,128)(2,1)S(1)}, u32[]{:S(2)}, u32[]{:S(2)}) collective-permute-start(bf16[64,2048]{1,0:T(8,128)(2,1)S(1)} %get-tuple-element.118), channel_id=1, source_target_pairs={{0,16},{8,24},{16,0},{24,8},{1,17},{9,25},{17,1},{25,9},{2,18},{10... | collective-permute-start | bytes 786440 | tf_op jit(solution)/shard_map/ppermute | solution.py:32
  115.1 18.3 %collective-permute-start.35 = (bf16[64,2048]{1,0:T(8,128)(2,1)S(1)}, bf16[64,2048]{1,0:T(8,128)(2,1)S(1)}, u32[]{:S(2)}, u32[]{:S(2)}) collective-permute-start(bf16[64,2048]{1,0:T(8,128)(2,1)S(1)} %get-tuple-element.119), channel_id=1, source_target_pairs={{0,1},{1,0},{2,3},{3,2},{4,5},{5,4},{6,7},{7,6},{8,9},{9,8},{10,11... | collective-permute-start | bytes 786440 | tf_op jit(solution)/shard_map/ppermute | solution.py:32
  127.9 10.2 %collective-permute-start.33 = (bf16[64,2048]{1,0:T(8,128)(2,1)S(1)}, bf16[64,2048]{1,0:T(8,128)(2,1)S(1)}, u32[]{:S(2)}, u32[]{:S(2)}) collective-permute-start(bf16[64,2048]{1,0:T(8,128)(2,1)S(1)} %add_convert_fusion.3), channel_id=1, source_target_pairs={{0,4},{1,5},{2,6},{3,7},{4,0},{5,1},{6,2},{7,3},{8,12},{9,13},{10,... | collective-permute-start | bytes 786440 | tf_op jit(solution)/shard_map/ppermute | solution.py:32
  128.3 9.8 %collective-permute-start.37 = (bf16[64,2048]{1,0:T(8,128)(2,1)S(1)}, bf16[64,2048]{1,0:T(8,128)(2,1)S(1)}, u32[]{:S(2)}, u32[]{:S(2)}) collective-permute-start(bf16[64,2048]{1,0:T(8,128)(2,1)S(1)} %add_convert_fusion.2), channel_id=1, source_target_pairs={{0,17},{1,16},{2,19},{3,18},{4,21},{5,20},{6,23},{7,22},{8,25},{9,... | collective-permute-start | bytes 786440 | tf_op jit(solution)/shard_map/ppermute | solution.py:38
  (29 other events, 265.6 us)

commit v8 on v6

--- a/solution.py
+++ b/solution.py
@@ -15,7 +15,7 @@
 MASKED = -1e30
 EXPERT_MIB = 46
 GATHER = ("c2", "c1", "d0", "y0", "x0", "c3", "d2", "x2", "y2", "y1", "x1", "d1", "y3", "x3", "d3")
-TAKE = (3, 14, 4, 9, 13, 11, 7, 2, 12, 8, 1, 0, 15, 6, 5, 10)
+TAKE = (3, 14, 4, 9, 13, 11, 7, 2, 0, 8, 1, 15, 12, 6, 5, 10)
 NEAR_MIB = 14
 FAR_MIB = 14
 EXP2_SCALE = math.log2(math.e) / math.sqrt(HD)

time: 140 us -> 140 us (level)
  no operation moved by 1% of the time
where the time goes in v8:
time: 140 us
  waiting for transfers between devices  57.9 us (41%)
  starting transfers between devices  45.4 us (32%)
  Pallas kernels  29.9 us (21%)
  local copies, waits for them, and re-layouts  4.11 us (3%)
  other arithmetic  1.63 us (1%)
    ppermute x38, waiting for transfers between devices, swap(): lax.ppermute(rows, axis, [(i, i ^ bits) for i in range(lax.axis_size(axis...  56.9 us
    ppermute x38, starting transfers between devices, swap(): lax.ppermute(rows, axis, [(i, i ^ bits) for i in range(lax.axis_size(axis...  39.5 us
    pallas_call x1, Pallas kernels, expert_terms(): pl.pallas_call(functools.partial(expert_kernel, layouts, take, per_group,...  13.6 us
    pallas_call x1, Pallas kernels, project(): pl.pallas_call(functools.partial(far_kernel, nseq, ks), out_shape=[jax.Sh...  6.55 us
    ppermute x3, starting transfers between devices, swap_both(): lax.ppermute(rows, ('seq', 'exp'), [(i, i ^ bits) for i in range(nseq * n...  5.83 us
    pallas_call x1, Pallas kernels, project_attention(): pl.pallas_call(functools.partial(near_kernel, nseq), out_shape=[jax.Shape...  4.72 us
    pallas_call x2, Pallas kernels, pack(): pl.pallas_call(functools.partial(pack_kernel, nseq, widths), out_shape=[s...  4.45 us
    unnamed x24, local copies, waits for them, and re-layouts  4.09 us
  transfers between devices with their start and end apart: 41, of which 24 were waited for; matrix products, arithmetic and copies ran while one was open for 0% of the time, Pallas kernels for 7%

profile of v8, /device:TPU:0, one launch (start us, length us, event | category | flops | bytes accessed | tf_op | source)
XLA Modules:
  0.0 139.7 jit_solution(2629290208096519098)
XLA Ops:
  3.2 2.6 %collective-permute-start.1 = (bf16[64,1280]{1,0:T(8,128)(2,1)}, bf16[64,1280]{1,0:T(8,128)(2,1)S(1)}, u32[]{:S(2)}, u32[]{:S(2)}) collective-permute-start(bf16[64,1280]{1,0:T(8,128)(2,1)} %get-tuple-element.68), channel_id=1, source_target_pairs={{0,16},{8,24},{16,0},{24,8},{1,17},{9,25},{17,1},{25,9},{2,18},{10... | collective-permute-start | bytes 491528 | tf_op jit(solution)/shard_map/ppermute | solution.py:32
  6.4 2.3 %pack_heads.3 = (bf16[512,256]{1,0:T(8,128)(2,1)}, bf16[512,256]{1,0:T(8,128)(2,1)}, bf16[512,256]{1,0:T(8,128)(2,1)}, bf16[512,256]{1,0:T(8,128)(2,1)}) custom-call(s32[1]{0:T(128)} %bitcast.1.me_ref, bf16[512,512]{1,0:T(8,128)(2,1)} %bitcast.21, bf16[512,512]{1,0:T(8,128)(2,1)} %bitcast.22), custom_call_target="tpu_custom_call" | custom-call | tf_op jit(solution)/shard_map/pack_heads/pallas_call | solution.py:64
  8.8 2.2 %collective-permute-done.1.refs_2_ = bf16[64,1280]{1,0:T(8,128)(2,1)S(1)} collective-permute-done((bf16[64,1280]{1,0:T(8,128)(2,1)}, bf16[64,1280]{1,0:T(8,128)(2,1)S(1)}, u32[]{:S(2)}, u32[]{:S(2)}) %collective-permute-start.1) | collective-permute-done | bytes 163872 | tf_op jit(solution)/shard_map/ppermute | solution.py:32
  16.1 2.2 %copy-done = bf16[1024,2048]{1,0:T(8,128)(2,1)S(1)} copy-done((bf16[1024,2048]{1,0:T(8,128)(2,1)S(1)}, bf16[1024,2048]{1,0:T(8,128)(2,1)}, u32[]{:S(2)}) %copy-start) | copy-done | bytes 4194328
  20.2 4.7 %attend_near.1 = (f32[256,128]{1,0:T(8,128)S(1)}, f32[256,128]{1,0:T(8,128)S(1)}, f32[256,1024]{1,0:T(8,128)S(1)}) custom-call(s32[1]{0:T(128)} %bitcast.1.me_ref, s32[1]{0:T(128)S(6)} %copy.15.len_ref, bf16[64,1280]{1,0:T(8,128)(2,1)S(1)} %copy-done.2, bf16[64,1280]{1,0:T(8,128)(2,1)S(1)} %collective-permute-done.refs_1_, ...), custom_call_target="tpu_custom_call" | custom-call | tf_op jit(solution)/shard_map/attend_near/pallas_call | solution.py:171
  25.5 6.5 %attend_far.1 = (f32[128,2048]{1,0:T(8,128)S(1)}, bf16[128,2048]{1,0:T(8,128)(2,1)S(1)}) custom-call(s32[1]{0:T(128)} %bitcast.1.me_ref, s32[1]{0:T(128)S(6)} %copy.15.len_ref, bf16[64,1280]{1,0:T(8,128)(2,1)S(1)} %copy-done.2, bf16[64,1280]{1,0:T(8,128)(2,1)S(1)} %collective-permute-done.refs_1_, bf16[64,1280]{1,0:T(8,128)(2,1)S(1)} %collective-permute-done.1.refs_2_, ...), custom_call_target="tpu_custom_call" | custom-call | tf_op jit(solution)/shard_map/attend_far/pallas_call | solution.py:186
  36.1 6.9 %collective-permute-done.9.refs_2_ = bf16[64,2048]{1,0:T(8,128)(2,1)S(1)} collective-permute-done((bf16[64,2048]{1,0:T(8,128)(2,1)S(1)}, bf16[64,2048]{1,0:T(8,128)(2,1)S(1)}, u32[]{:S(2)}, u32[]{:S(2)}) %collective-permute-start.9) | collective-permute-done | bytes 262176 | tf_op jit(solution)/shard_map/ppermute | solution.py:32
  46.9 2.6 %collective-permute-start.12 = (bf16[64,2176]{1,0:T(8,128)(2,1)S(1)}, bf16[64,2176]{1,0:T(8,128)(2,1)S(1)}, u32[]{:S(2)}, u32[]{:S(2)}) collective-permute-start(bf16[64,2176]{1,0:T(8,128)(2,1)S(1)} %get-tuple-element.91.refs_8_), channel_id=1, source_target_pairs={{0,4},{1,5},{2,6},{3,7},{4,0},{5,1},{6,2},{7,3},{8,12},{9,13},{10,... | collective-permute-start | bytes 835592 | tf_op jit(solution)/shard_map/ppermute | solution.py:32
  51.5 5.0 %collective-permute-done.15.refs_2_ = bf16[64,2176]{1,0:T(8,128)(2,1)S(1)} collective-permute-done((bf16[64,2176]{1,0:T(8,128)(2,1)S(1)}, bf16[64,2176]{1,0:T(8,128)(2,1)S(1)}, u32[]{:S(2)}, u32[]{:S(2)}) %collective-permute-start.15) | collective-permute-done | bytes 278560 | tf_op jit(solution)/shard_map/ppermute | solution.py:32
  56.5 2.4 %collective-permute-start.24 = (bf16[64,2176]{1,0:T(8,128)(2,1)S(1)}, bf16[64,2176]{1,0:T(8,128)(2,1)S(1)}, u32[]{:S(2)}, u32[]{:S(2)}) collective-permute-start(bf16[64,2176]{1,0:T(8,128)(2,1)S(1)} %collective-permute-done.15.refs_2_), channel_id=1, source_target_pairs={{0,16},{8,24},{16,0},{24,8},{1,17},{9,25},{17,1},{25,9},{2,18},{10... | collective-permute-start | bytes 835592 | tf_op jit(solution)/shard_map/ppermute | solution.py:32
  61.3 3.6 %collective-permute-done.20.refs_7_ = bf16[64,2176]{1,0:T(8,128)(2,1)S(1)} collective-permute-done((bf16[64,2176]{1,0:T(8,128)(2,1)S(1)}, bf16[64,2176]{1,0:T(8,128)(2,1)S(1)}, u32[]{:S(2)}, u32[]{:S(2)}) %collective-permute-start.20) | collective-permute-done | bytes 278560 | tf_op jit(solution)/shard_map/ppermute | solution.py:32
  66.8 4.1 %collective-permute-done.23.refs_13_ = bf16[64,2176]{1,0:T(8,128)(2,1)S(1)} collective-permute-done((bf16[64,2176]{1,0:T(8,128)(2,1)S(1)}, bf16[64,2176]{1,0:T(8,128)(2,1)S(1)}, u32[]{:S(2)}, u32[]{:S(2)}) %collective-permute-start.23) | collective-permute-done | bytes 278560 | tf_op jit(solution)/shard_map/ppermute | solution.py:32
  71.7 2.9 %collective-permute-done.25.refs_15_ = bf16[64,2176]{1,0:T(8,128)(2,1)S(1)} collective-permute-done((bf16[64,2176]{1,0:T(8,128)(2,1)S(1)}, bf16[64,2176]{1,0:T(8,128)(2,1)S(1)}, u32[]{:S(2)}, u32[]{:S(2)}) %collective-permute-start.25) | collective-permute-done | bytes 278560 | tf_op jit(solution)/shard_map/ppermute | solution.py:32
  78.0 4.2 %collective-permute-done.19.refs_6_ = bf16[64,2176]{1,0:T(8,128)(2,1)} collective-permute-done((bf16[64,2176]{1,0:T(8,128)(2,1)S(1)}, bf16[64,2176]{1,0:T(8,128)(2,1)}, u32[]{:S(2)}, u32[]{:S(2)}) %collective-permute-start.19) | collective-permute-done | bytes 278560 | tf_op jit(solution)/shard_map/ppermute | solution.py:32
  82.2 3.6 %collective-permute-done.22.refs_11_ = bf16[64,2176]{1,0:T(8,128)(2,1)} collective-permute-done((bf16[64,2176]{1,0:T(8,128)(2,1)S(1)}, bf16[64,2176]{1,0:T(8,128)(2,1)}, u32[]{:S(2)}, u32[]{:S(2)}) %collective-permute-start.22) | collective-permute-done | bytes 278560 | tf_op jit(solution)/shard_map/ppermute | solution.py:32
  85.9 13.6 %experts.1 = (bf16[64,2048]{1,0:T(8,128)(2,1)S(1)}, bf16[64,2048]{1,0:T(8,128)(2,1)S(1)}, bf16[64,2048]{1,0:T(8,128)(2,1)S(1)}, bf16[64,2048]{1,0:T(8,128)(2,1)S...) custom-call(s32[2]{0:T(128)S(1)} %pad_add_fusion.mine_ref, ...), custom_call_target="tpu_custom_call" | custom-call | flops 7247757312 | bytes 6291456 | tf_op jit(solution)/shard_map/experts/pallas_call | solution.py:395
  103.6 2.2 %collective-permute-done.28 = bf16[64,2048]{1,0:T(8,128)(2,1)S(1)} collective-permute-done((bf16[64,2048]{1,0:T(8,128)(2,1)S(1)}, bf16[64,2048]{1,0:T(8,128)(2,1)S(1)}, u32[]{:S(2)}, u32[]{:S(2)}) %collective-permute-start.28) | collective-permute-done | bytes 262176 | tf_op jit(solution)/shard_map/ppermute | solution.py:32
  105.9 2.7 %collective-permute-done.29 = bf16[64,2048]{1,0:T(8,128)(2,1)S(1)} collective-permute-done((bf16[64,2048]{1,0:T(8,128)(2,1)S(1)}, bf16[64,2048]{1,0:T(8,128)(2,1)S(1)}, u32[]{:S(2)}, u32[]{:S(2)}) %collective-permute-start.29) | collective-permute-done | bytes 262176 | tf_op jit(solution)/shard_map/ppermute | solution.py:32
  111.5 2.4 %collective-permute-start.31 = (bf16[64,2048]{1,0:T(8,128)(2,1)S(1)}, bf16[64,2048]{1,0:T(8,128)(2,1)S(1)}, u32[]{:S(2)}, u32[]{:S(2)}) collective-permute-start(bf16[64,2048]{1,0:T(8,128)(2,1)S(1)} %add_convert_fusion.5), channel_id=1, source_target_pairs={{0,17},{1,16},{2,19},{3,18},{4,21},{5,20},{6,23},{7,22},{8,25},{9,... | collective-permute-start | bytes 786440 | tf_op jit(solution)/shard_map/ppermute | solution.py:38
  115.9 2.1 %collective-permute-done.27 = bf16[64,2048]{1,0:T(8,128)(2,1)S(1)} collective-permute-done((bf16[64,2048]{1,0:T(8,128)(2,1)S(1)}, bf16[64,2048]{1,0:T(8,128)(2,1)S(1)}, u32[]{:S(2)}, u32[]{:S(2)}) %collective-permute-start.27) | collective-permute-done | bytes 262176 | tf_op jit(solution)/shard_map/ppermute | solution.py:32
  118.0 2.7 %collective-permute-start.36 = (bf16[64,2048]{1,0:T(8,128)(2,1)S(1)}, bf16[64,2048]{1,0:T(8,128)(2,1)S(1)}, u32[]{:S(2)}, u32[]{:S(2)}) collective-permute-start(bf16[64,2048]{1,0:T(8,128)(2,1)S(1)} %get-tuple-element.121), channel_id=1, source_target_pairs={{0,2},{1,3},{2,0},{3,1},{4,6},{5,7},{6,4},{7,5},{8,10},{9,11},{10,... | collective-permute-start | bytes 786440 | tf_op jit(solution)/shard_map/ppermute | solution.py:32
  123.9 4.0 %collective-permute-done.36 = bf16[64,2048]{1,0:T(8,128)(2,1)S(1)} collective-permute-done((bf16[64,2048]{1,0:T(8,128)(2,1)S(1)}, bf16[64,2048]{1,0:T(8,128)(2,1)S(1)}, u32[]{:S(2)}, u32[]{:S(2)}) %collective-permute-start.36) | collective-permute-done | bytes 262176 | tf_op jit(solution)/shard_map/ppermute | solution.py:32
  128.4 3.0 %collective-permute-start.37 = (bf16[64,2048]{1,0:T(8,128)(2,1)S(1)}, bf16[64,2048]{1,0:T(8,128)(2,1)S(1)}, u32[]{:S(2)}, u32[]{:S(2)}) collective-permute-start(bf16[64,2048]{1,0:T(8,128)(2,1)S(1)} %add_convert_fusion.2), channel_id=1, source_target_pairs={{0,17},{1,16},{2,19},{3,18},{4,21},{5,20},{6,23},{7,22},{8,25},{9,... | collective-permute-start | bytes 786440 | tf_op jit(solution)/shard_map/ppermute | solution.py:38
  133.4 4.7 %collective-permute-done.33 = bf16[64,2048]{1,0:T(8,128)(2,1)S(1)} collective-permute-done((bf16[64,2048]{1,0:T(8,128)(2,1)S(1)}, bf16[64,2048]{1,0:T(8,128)(2,1)S(1)}, u32[]{:S(2)}, u32[]{:S(2)}) %collective-permute-start.33) | collective-permute-done | bytes 262176 | tf_op jit(solution)/shard_map/ppermute | solution.py:32
  (97 shorter events, 45.7 us)
Async XLA Ops:
  0.0 14.0 %collective-permute-start.3 = (bf16[1,2048,768]{2,1,0:T(8,128)(2,1)}, bf16[1,2048,768]{2,1,0:T(8,128)(2,1)}, u32[]{:S(2)}, u32[]{:S(2)}) collective-permute-start(bf16[1,2048,768]{2,1,0:T(8,128)(2,1)} %refs_16_), channel_id=1, source_target_pairs={{0,8},{8,0},{16,24},{24,16},{1,9},{9,1},{17,25},{25,17},{2,10},{10... | collective-permute-start | bytes 9437192 | tf_op jit(solution)/shard_map/ppermute | solution.py:32
  0.5 13.5 %collective-permute-start.4 = (bf16[1,2048,768]{2,1,0:T(8,128)(2,1)}, bf16[1,2048,768]{2,1,0:T(8,128)(2,1)}, u32[]{:S(2)}, u32[]{:S(2)}) collective-permute-start(bf16[1,2048,768]{2,1,0:T(8,128)(2,1)} %refs_17_), channel_id=1, source_target_pairs={{0,8},{8,0},{16,24},{24,16},{1,9},{9,1},{17,25},{25,17},{2,10},{10... | collective-permute-start | bytes 9437192 | tf_op jit(solution)/shard_map/ppermute | solution.py:32
  11.0 13.9 %collective-permute-start.5 = (bf16[512,256]{1,0:T(8,128)(2,1)}, bf16[512,256]{1,0:T(8,128)(2,1)S(1)}, u32[]{:S(2)}, u32[]{:S(2)}) collective-permute-start(bf16[512,256]{1,0:T(8,128)(2,1)} %get-tuple-element.76), channel_id=1, source_target_pairs={{0,16},{8,24},{16,0},{24,8},{1,17},{9,25},{17,1},{25,9},{2,18},{10... | collective-permute-start | bytes 786440 | tf_op jit(solution)/shard_map/ppermute | solution.py:32
  14.0 11.5 %collective-permute-start.6 = (bf16[512,256]{1,0:T(8,128)(2,1)}, bf16[512,256]{1,0:T(8,128)(2,1)S(1)}, u32[]{:S(2)}, u32[]{:S(2)}) collective-permute-start(bf16[512,256]{1,0:T(8,128)(2,1)} %get-tuple-element.77), channel_id=1, source_target_pairs={{0,24},{8,16},{16,8},{24,0},{1,25},{9,17},{17,9},{25,1},{2,26},{10... | collective-permute-start | bytes 786440 | tf_op jit(solution)/shard_map/ppermute | solution.py:32
  43.6 12.9 %collective-permute-start.15 = (bf16[64,2176]{1,0:T(8,128)(2,1)S(1)}, bf16[64,2176]{1,0:T(8,128)(2,1)S(1)}, u32[]{:S(2)}, u32[]{:S(2)}) collective-permute-start(bf16[64,2176]{1,0:T(8,128)(2,1)S(1)} %get-tuple-element.91.refs_8_), channel_id=1, source_target_pairs={{0,2},{1,3},{2,0},{3,1},{4,6},{5,7},{6,4},{7,5},{8,10},{9,11},{10,... | collective-permute-start | bytes 835592 | tf_op jit(solution)/shard_map/ppermute | solution.py:32
  45.4 13.5 %collective-permute-start.21 = (bf16[64,2176]{1,0:T(8,128)(2,1)S(1)}, bf16[64,2176]{1,0:T(8,128)(2,1)S(1)}, u32[]{:S(2)}, u32[]{:S(2)}) collective-permute-start(bf16[64,2176]{1,0:T(8,128)(2,1)S(1)} %get-tuple-element.91.refs_8_), channel_id=1, source_target_pairs={{0,16},{8,24},{16,0},{24,8},{1,17},{9,25},{17,1},{25,9},{2,18},{10... | collective-permute-start | bytes 835592 | tf_op jit(solution)/shard_map/ppermute | solution.py:32
  46.9 14.4 %collective-permute-start.12 = (bf16[64,2176]{1,0:T(8,128)(2,1)S(1)}, bf16[64,2176]{1,0:T(8,128)(2,1)S(1)}, u32[]{:S(2)}, u32[]{:S(2)}) collective-permute-start(bf16[64,2176]{1,0:T(8,128)(2,1)S(1)} %get-tuple-element.91.refs_8_), channel_id=1, source_target_pairs={{0,4},{1,5},{2,6},{3,7},{4,0},{5,1},{6,2},{7,3},{8,12},{9,13},{10,... | collective-permute-start | bytes 835592 | tf_op jit(solution)/shard_map/ppermute | solution.py:32
  49.5 15.4 %collective-permute-start.20 = (bf16[64,2176]{1,0:T(8,128)(2,1)S(1)}, bf16[64,2176]{1,0:T(8,128)(2,1)S(1)}, u32[]{:S(2)}, u32[]{:S(2)}) collective-permute-start(bf16[64,2176]{1,0:T(8,128)(2,1)S(1)} %get-tuple-element.91.refs_8_), channel_id=1, source_target_pairs={{0,1},{1,0},{2,3},{3,2},{4,5},{5,4},{6,7},{7,6},{8,9},{9,8},{10,11... | collective-permute-start | bytes 835592 | tf_op jit(solution)/shard_map/ppermute | solution.py:32
  51.0 15.0 %collective-permute-start.11 = (bf16[64,2176]{1,0:T(8,128)(2,1)S(1)}, bf16[64,2176]{1,0:T(8,128)(2,1)S(1)}, u32[]{:S(2)}, u32[]{:S(2)}) collective-permute-start(bf16[64,2176]{1,0:T(8,128)(2,1)S(1)} %get-tuple-element.91.refs_8_), channel_id=1, source_target_pairs={{0,17},{1,16},{2,19},{3,18},{4,21},{5,20},{6,23},{7,22},{8,25},{9,... | collective-permute-start | bytes 835592 | tf_op jit(solution)/shard_map/ppermute | solution.py:38
  58.9 11.9 %collective-permute-start.23 = (bf16[64,2176]{1,0:T(8,128)(2,1)S(1)}, bf16[64,2176]{1,0:T(8,128)(2,1)S(1)}, u32[]{:S(2)}, u32[]{:S(2)}) collective-permute-start(bf16[64,2176]{1,0:T(8,128)(2,1)S(1)} %collective-permute-done.15.refs_2_), channel_id=1, source_target_pairs={{0,1},{1,0},{2,3},{3,2},{4,5},{5,4},{6,7},{7,6},{8,9},{9,8},{10,11... | collective-permute-start | bytes 835592 | tf_op jit(solution)/shard_map/ppermute | solution.py:32
  61.3 10.2 %collective-permute-start.13 = (bf16[64,2176]{1,0:T(8,128)(2,1)S(1)}, bf16[64,2176]{1,0:T(8,128)(2,1)S(1)}, u32[]{:S(2)}, u32[]{:S(2)}) collective-permute-start(bf16[64,2176]{1,0:T(8,128)(2,1)S(1)} %collective-permute-done.12.refs_9_), channel_id=1, source_target_pairs={{0,2},{1,3},{2,0},{3,1},{4,6},{5,7},{6,4},{7,5},{8,10},{9,11},{10,... | collective-permute-start | bytes 835592 | tf_op jit(solution)/shard_map/ppermute | solution.py:32
  64.9 9.7 %collective-permute-start.25 = (bf16[64,2176]{1,0:T(8,128)(2,1)S(1)}, bf16[64,2176]{1,0:T(8,128)(2,1)S(1)}, u32[]{:S(2)}, u32[]{:S(2)}) collective-permute-start(bf16[64,2176]{1,0:T(8,128)(2,1)S(1)} %collective-permute-done.12.refs_9_), channel_id=1, source_target_pairs={{0,1},{1,0},{2,3},{3,2},{4,5},{5,4},{6,7},{7,6},{8,9},{9,8},{10,11... | collective-permute-start | bytes 835592 | tf_op jit(solution)/shard_map/ppermute | solution.py:32
  66.0 11.7 %collective-permute-start.18 = (bf16[64,2176]{1,0:T(8,128)(2,1)S(1)}, bf16[64,2176]{1,0:T(8,128)(2,1)S(1)}, u32[]{:S(2)}, u32[]{:S(2)}) collective-permute-start(bf16[64,2176]{1,0:T(8,128)(2,1)S(1)} %collective-permute-done.11.refs_0_), channel_id=1, source_target_pairs={{0,4},{1,5},{2,6},{3,7},{4,0},{5,1},{6,2},{7,3},{8,12},{9,13},{10,... | collective-permute-start | bytes 835592 | tf_op jit(solution)/shard_map/ppermute | solution.py:32
  66.0 12.0 %collective-permute-start.16 = (bf16[64,2176]{1,0:T(8,128)(2,1)S(1)}, bf16[64,2176]{1,0:T(8,128)(2,1)S(1)}, u32[]{:S(2)}, u32[]{:S(2)}) collective-permute-start(bf16[64,2176]{1,0:T(8,128)(2,1)S(1)} %collective-permute-done.12.refs_9_), channel_id=1, source_target_pairs={{0,16},{8,24},{16,0},{24,8},{1,17},{9,25},{17,1},{25,9},{2,18},{10... | collective-permute-start | bytes 835592 | tf_op jit(solution)/shard_map/ppermute | solution.py:32
  70.9 11.3 %collective-permute-start.19 = (bf16[64,2176]{1,0:T(8,128)(2,1)S(1)}, bf16[64,2176]{1,0:T(8,128)(2,1)}, u32[]{:S(2)}, u32[]{:S(2)}) collective-permute-start(bf16[64,2176]{1,0:T(8,128)(2,1)S(1)} %collective-permute-done.11.refs_0_), channel_id=1, source_target_pairs={{0,2},{1,3},{2,0},{3,1},{4,6},{5,7},{6,4},{7,5},{8,10},{9,11},{10,... | collective-permute-start | bytes 835592 | tf_op jit(solution)/shard_map/ppermute | solution.py:32
  71.5 10.7 %collective-permute-start.17 = (bf16[64,2176]{1,0:T(8,128)(2,1)S(1)}, bf16[64,2176]{1,0:T(8,128)(2,1)}, u32[]{:S(2)}, u32[]{:S(2)}) collective-permute-start(bf16[64,2176]{1,0:T(8,128)(2,1)S(1)} %collective-permute-done.13.refs_12_), channel_id=1, source_target_pairs={{0,16},{8,24},{16,0},{24,8},{1,17},{9,25},{17,1},{25,9},{2,18},{10... | collective-permute-start | bytes 835592 | tf_op jit(solution)/shard_map/ppermute | solution.py:32
  102.2 12.8 %collective-permute-start.26 = (bf16[64,2048]{1,0:T(8,128)(2,1)S(1)}, bf16[64,2048]{1,0:T(8,128)(2,1)S(1)}, u32[]{:S(2)}, u32[]{:S(2)}) collective-permute-start(bf16[64,2048]{1,0:T(8,128)(2,1)S(1)} %get-tuple-element.99), channel_id=1, source_target_pairs={{0,16},{8,24},{16,0},{24,8},{1,17},{9,25},{17,1},{25,9},{2,18},{10... | collective-permute-start | bytes 786440 | tf_op jit(solution)/shard_map/ppermute | solution.py:32
  103.1 14.9 %collective-permute-start.27 = (bf16[64,2048]{1,0:T(8,128)(2,1)S(1)}, bf16[64,2048]{1,0:T(8,128)(2,1)S(1)}, u32[]{:S(2)}, u32[]{:S(2)}) collective-permute-start(bf16[64,2048]{1,0:T(8,128)(2,1)S(1)} %get-tuple-element.100), channel_id=1, source_target_pairs={{0,1},{1,0},{2,3},{3,2},{4,5},{5,4},{6,7},{7,6},{8,9},{9,8},{10,11... | collective-permute-start | bytes 786440 | tf_op jit(solution)/shard_map/ppermute | solution.py:32
  109.7 11.0 %collective-permute-start.32 = (bf16[64,2048]{1,0:T(8,128)(2,1)S(1)}, bf16[64,2048]{1,0:T(8,128)(2,1)S(1)}, u32[]{:S(2)}, u32[]{:S(2)}) collective-permute-start(bf16[64,2048]{1,0:T(8,128)(2,1)S(1)} %add_convert_fusion.4), channel_id=1, source_target_pairs={{0,2},{1,3},{2,0},{3,1},{4,6},{5,7},{6,4},{7,5},{8,10},{9,11},{10,... | collective-permute-start | bytes 786440 | tf_op jit(solution)/shard_map/ppermute | solution.py:32
  111.5 10.2 %collective-permute-start.31 = (bf16[64,2048]{1,0:T(8,128)(2,1)S(1)}, bf16[64,2048]{1,0:T(8,128)(2,1)S(1)}, u32[]{:S(2)}, u32[]{:S(2)}) collective-permute-start(bf16[64,2048]{1,0:T(8,128)(2,1)S(1)} %add_convert_fusion.5), channel_id=1, source_target_pairs={{0,17},{1,16},{2,19},{3,18},{4,21},{5,20},{6,23},{7,22},{8,25},{9,... | collective-permute-start | bytes 786440 | tf_op jit(solution)/shard_map/ppermute | solution.py:38
  113.9 19.6 %collective-permute-start.34 = (bf16[64,2048]{1,0:T(8,128)(2,1)S(1)}, bf16[64,2048]{1,0:T(8,128)(2,1)S(1)}, u32[]{:S(2)}, u32[]{:S(2)}) collective-permute-start(bf16[64,2048]{1,0:T(8,128)(2,1)S(1)} %get-tuple-element.118), channel_id=1, source_target_pairs={{0,16},{8,24},{16,0},{24,8},{1,17},{9,25},{17,1},{25,9},{2,18},{10... | collective-permute-start | bytes 786440 | tf_op jit(solution)/shard_map/ppermute | solution.py:32
  115.1 18.4 %collective-permute-start.35 = (bf16[64,2048]{1,0:T(8,128)(2,1)S(1)}, bf16[64,2048]{1,0:T(8,128)(2,1)S(1)}, u32[]{:S(2)}, u32[]{:S(2)}) collective-permute-start(bf16[64,2048]{1,0:T(8,128)(2,1)S(1)} %get-tuple-element.119), channel_id=1, source_target_pairs={{0,1},{1,0},{2,3},{3,2},{4,5},{5,4},{6,7},{7,6},{8,9},{9,8},{10,11... | collective-permute-start | bytes 786440 | tf_op jit(solution)/shard_map/ppermute | solution.py:32
  118.0 9.9 %collective-permute-start.36 = (bf16[64,2048]{1,0:T(8,128)(2,1)S(1)}, bf16[64,2048]{1,0:T(8,128)(2,1)S(1)}, u32[]{:S(2)}, u32[]{:S(2)}) collective-permute-start(bf16[64,2048]{1,0:T(8,128)(2,1)S(1)} %get-tuple-element.121), channel_id=1, source_target_pairs={{0,2},{1,3},{2,0},{3,1},{4,6},{5,7},{6,4},{7,5},{8,10},{9,11},{10,... | collective-permute-start | bytes 786440 | tf_op jit(solution)/shard_map/ppermute | solution.py:32
  127.9 10.2 %collective-permute-start.33 = (bf16[64,2048]{1,0:T(8,128)(2,1)S(1)}, bf16[64,2048]{1,0:T(8,128)(2,1)S(1)}, u32[]{:S(2)}, u32[]{:S(2)}) collective-permute-start(bf16[64,2048]{1,0:T(8,128)(2,1)S(1)} %add_convert_fusion.3), channel_id=1, source_target_pairs={{0,4},{1,5},{2,6},{3,7},{4,0},{5,1},{6,2},{7,3},{8,12},{9,13},{10,... | collective-permute-start | bytes 786440 | tf_op jit(solution)/shard_map/ppermute | solution.py:32
  (29 other events, 265.6 us)
